TPU v7x, 32 devices: a whole 2x2x4 slice. The times are simulated.
32 devices in a mesh: dp: 8 (over z, y), tensor: 4 (over x, core).
Axes of the slice: x: 2, y: 2, z: 4, core: 2. Of those that a mesh axis runs over, the one named last changes fastest.
Arguments:
- inputs: bfloat16 [4096, 4096], P('dp'), may hold values from -6 to 6
- weight: bfloat16 [4096, 4096], P(None, 'tensor'), may hold values from -0.09375 to 0.09375
- targets: bfloat16 [4096, 4096], P('dp', 'tensor'), may hold values from -6 to 6
- momentum: float32 [4096, 4096], P('dp', 'tensor'), may hold values from -6 to 6
Outputs:
- input_grad: bfloat16 [4096, 4096], P('tensor', 'dp')
- new_momentum: float32 [4096, 4096], P('dp', 'tensor')
- tree_norms: float32 [2], replicated
All inputs are finite; a program needn't handle non-finite values.
Results may differ from a plain program's by a relative error of at most 0.013.
Values may be sent and summed in bfloat16 or wider, within the bound.
No kernel may reach another device: no remote copies, remote signals or barrier semaphores. Data moves between devices by JAX's collectives and lax.ppermute only.
A program may use at most 128 MiB of HBM per device.

v0:
```python
import math

import jax
import jax.numpy as jnp
from jax import lax
from jax.sharding import PartitionSpec as P

ROWS = 512


def partner(value, axis, stride):
    mask = 2**stride
    pairs = [(source, source ^ mask) for source in range(lax.axis_size(axis))]
    return lax.ppermute(value, axis, pairs)


def body(inputs, weight, targets, momentum):
    outputs = jnp.dot(inputs, weight, preferred_element_type=jnp.float32)
    error = (outputs - targets.astype(jnp.float32)).astype(jnp.bfloat16)
    summed = lax.psum_scatter(
        lax.dot_general(
            weight, error, (((1,), (1,)), ((), ())), preferred_element_type=jnp.float32
        ).astype(jnp.bfloat16),
        "tensor",
        scatter_dimension=0,
        tiled=True,
    )
    grad = lax.dot_general(
        inputs, error, (((0,), (0,)), ((), ())), preferred_element_type=jnp.float32
    )
    grad = grad * (1.0 / math.sqrt(ROWS))
    groups = lax.axis_size("dp")
    depth = groups.bit_length() - 1
    my_index = lax.axis_index("dp")
    block_rows = grad.shape[0] // groups
    columns = grad.shape[1]
    piece = grad.reshape(groups, block_rows, columns)
    last_sums = None
    for level in range(depth):
        my_bit = my_index >> level & 1
        paired = piece.reshape(piece.shape[0] // 2, 2, block_rows, columns)
        lower_half = paired[:, 0]
        upper_half = paired[:, 1]
        is_lower = my_bit == 0
        kept = jnp.where(is_lower, lower_half, upper_half)
        sent = jnp.where(is_lower, upper_half, lower_half)
        received = partner(sent, "dp", level)
        first = jnp.where(is_lower, kept, received)
        second = jnp.where(is_lower, received, kept)
        partials = jnp.stack(
            [jnp.sum(first * second), jnp.sum(first * first), jnp.sum(second * second)]
        )
        sums = lax.psum(partials, "tensor")
        for inner in range(level + 1):
            sums = sums + partner(sums, "dp", inner)
        cross = sums[0]
        piece = (1.0 - cross / (2.0 * sums[1])) * first + (1.0 - cross / (2.0 * sums[2])) * second
        last_sums = sums
    combined = piece.reshape(block_rows, columns)
    width_total = weight.shape[0]
    tree_norms = jnp.sqrt(last_sums[1:3]) / width_total
    return (summed, 0.9 * momentum + combined, tree_norms)


def solution(mesh):
    return jax.shard_map(
        body,
        mesh=mesh,
        in_specs=(P("dp", None), P(None, "tensor"), P("dp", "tensor"), P("dp", "tensor")),
        out_specs=(P("tensor", "dp"), P("dp", "tensor"), P()),
        check_vma=False,
    )
```

profile of v0, /device:TPU:0, one launch (start us, length us, event | category | flops | bytes accessed | tf_op | source)
XLA Modules:
  0.0 602.0 jit_solution(2928750965513920113)
XLA Ops:
  7.2 0.0 reduce-scatter.2.cloned.1.call-start
  7.2 0.0 copy-start
  7.2 0.0 copy-start.1
  7.2 8.3 %fusion.8 = f32[512,1024]{1,0:T(8,128)S(1)} fusion(bf16[512,4096]{1,0:T(8,128)(2,1)} %param.4, bf16[4096,1024]{1,0:T(8,128)(2,1)} %param.5), kind=kOutput, calls=%fused_computation.39 | convolution fusion | flops 4294967296 | bytes 14680064 | tf_op jit(solution)/shard_map/dot_general | solution.py:18
  15.5 0.0 copy-done
  15.5 0.0 copy-done.1
  15.5 8.2 %multiply_bitcast_fusion = f32[4096,1024]{0,1:T(8,128)} fusion(bf16[512,4096]{1,0:T(8,128)(2,1)S(1)} %copy-done, f32[512,1024]{1,0:T(8,128)S(1)} %fusion.8, bf16[512,1024]{1,0:T(8,128)(2,1)S(1)} %copy-done.1), kind=kOutput, calls=%fused_computation | convolution fusion | flops 4300734464 | bytes 24117248 | tf_op jit(solution)/shard_map/dot_general | solution.py:28
  23.7 22.0 %reshape_reshape.3 = f32[4,2,512,1024]{2,1,0,3:T(2,128)} reshape(f32[4096,1024]{0,1:T(8,128)} %multiply_bitcast_fusion) | data formatting | bytes 33554432 | tf_op jit(solution)/shard_map/reshape;reshape | solution.py:41
  45.8 22.0 %fusion.4 = (f32[4,1,512,1024]{2,1,0,3:T(1,128)}, f32[4,1,512,1024]{2,1,0,3:T(1,128)}) fusion(f32[4,2,512,1024]{2,1,0,3:T(2,128)} %reshape_reshape.3), kind=kLoop, calls=%fused_computation.35 | loop fusion | bytes 33554432 | tf_op jit(solution)/shard_map/slice | solution.py:42
  67.8 20.7 %copy.20 = f32[4,1,512,1024]{3,2,0,1:T(8,128)} copy(f32[4,1,512,1024]{2,1,0,3:T(1,128)} %get-tuple-element.25) | data formatting | bytes 16777216
  88.5 20.7 %copy.19 = f32[4,1,512,1024]{3,2,0,1:T(8,128)} copy(f32[4,1,512,1024]{2,1,0,3:T(1,128)} %get-tuple-element.24) | data formatting | bytes 16777216
  109.2 9.6 %select_bitcast_fusion = f32[4,512,1024]{2,1,0:T(8,128)} fusion(f32[4,1,512,1024]{3,2,0,1:T(8,128)} %copy.20, f32[4,1,512,1024]{3,2,0,1:T(8,128)} %copy.19, pred[]{:T(512)S(6)} %eq.11), kind=kLoop, calls=%fused_computation.7 | loop fusion | flops 2097152 | bytes 25165824 | tf_op jit(solution)/shard_map/jit(_where)/select_n | solution.py:46
  118.8 3.0 collective-permute-start
  121.7 180.8 %collective-permute-done = f32[4,512,1024]{2,1,0:T(8,128)} collective-permute-done((f32[4,512,1024]{2,1,0:T(8,128)}, f32[4,512,1024]{2,1,0:T(8,128)}, u32[]{:S(2)}, u32[]{:S(2)}) %collective-permute-start) | collective-permute-done | bytes 8388640 | tf_op jit(solution)/shard_map/ppermute | solution.py:14
  302.5 12.5 %multiply_reduce_fusion.2 = (f32[]{:T(128)}, f32[]{:T(128)}, f32[]{:T(128)}, f32[4,512,1024]{2,1,0:T(8,128)}, f32[4,512,1024]{2,1,0:T(8,128)}) fusion(f32[4,512,1024]{2,1,0:T(8,128)} %collective-permute-done, f32[4,1,512,1024]{3,2,0,1:T(8,128)} %copy.19, f32[4,1,512,1024]{3,2,0,1:T(8,128)} %copy.20, pred[]{:T(512)S(6)} %eq.11), kind=kLoop, calls=%fused_computation.6 | loop fusion | flops 18874364 | bytes 41943052 | tf_op jit(solution)/shard_map/reduce_sum | solution.py:51
  315.0 2.0 pad_maximum_fusion
  317.1 6.1 %psum.21 = f32[3]{0:T(128)S(1)} all-reduce(f32[3]{0:T(128)S(1)} %pad_maximum_fusion), channel_id=1, replica_groups=mesh['dp'=8,'tensor'=4] {'tensor'}, use_global_device_ids=true, to_apply=%region_4.5 | all-reduce | flops 3 | bytes 24 | tf_op jit(solution)/shard_map/psum | solution.py:53
  323.1 1.6 collective-permute-start.1
  324.7 2.0 collective-permute-done.1
  326.7 0.6 fusion.7
  329.9 12.1 %multiply_add_fusion = f32[4,512,1024]{2,1,0:T(8,128)} fusion(f32[4,512,1024]{2,1,0:T(8,128)} %get-tuple-element.23, f32[4,512,1024]{2,1,0:T(8,128)} %get-tuple-element.22, f32[]{:T(128)} %bitcast.8, f32[]{:T(128)} %bitcast.7), kind=kLoop, calls=%fused_computation.3 | loop fusion | flops 6291456 | bytes 25165832 | tf_op jit(solution)/shard_map/add | solution.py:57
  342.0 6.8 %select_bitcast_fusion.1 = f32[2,512,1024]{2,1,0:T(8,128)} fusion(f32[2,2,512,1024]{3,2,1,0:T(8,128)} %bitcast.76, pred[]{:T(512)S(6)} %eq.10), kind=kLoop, calls=%fused_computation.16 | loop fusion | flops 1048576 | bytes 12582913 | tf_op jit(solution)/shard_map/jit(_where)/select_n | solution.py:46
  348.8 1.6 collective-permute-start.2
  350.3 9.5 %fusion = bf16[4096,512]{0,1:T(8,128)(2,1)} fusion(bf16[4096,1024]{1,0:T(8,128)(2,1)} %param.5, f32[512,1024]{1,0:T(8,128)S(1)} %fusion.8, bf16[512,1024]{1,0:T(8,128)(2,1)S(1)} %copy-done.1), kind=kOutput, calls=%fused_computation.9 | convolution fusion | flops 4298637312 | bytes 15728640 | tf_op jit(solution)/shard_map/dot_general | solution.py:21
  359.9 0.0 reduce-scatter.2.cloned.1.call-update
  359.9 80.2 %collective-permute-done.2 = f32[2,512,1024]{2,1,0:T(8,128)} collective-permute-done((f32[2,512,1024]{2,1,0:T(8,128)}, f32[2,512,1024]{2,1,0:T(8,128)}, u32[]{:S(2)}, u32[]{:S(2)}) %collective-permute-start.2) | collective-permute-done | bytes 4194336 | tf_op jit(solution)/shard_map/ppermute | solution.py:14
  440.1 8.5 %multiply_reduce_fusion.5 = (f32[]{:T(128)}, f32[]{:T(128)}, f32[]{:T(128)}, f32[2,512,1024]{2,1,0:T(8,128)}, f32[2,512,1024]{2,1,0:T(8,128)}) fusion(f32[2,512,1024]{2,1,0:T(8,128)} %collective-permute-done.2, f32[2,2,512,1024]{3,2,1,0:T(8,128)} %bitcast.77, pred[]{:T(512)S(6)} %eq.10), kind=kLoop, calls=%fused_computation.15 | loop fusion | flops 9437181 | bytes 20972556 | tf_op jit(solution)/shard_map/reduce_sum | solution.py:51
  448.6 2.0 pad_maximum_fusion.1
  450.6 5.6 psum.22
  456.2 1.7 collective-permute-start.3
  457.9 1.9 collective-permute-done.3
  459.8 1.7 collective-permute-start.4
  461.5 1.8 collective-permute-done.4
  463.4 0.6 fusion.6
  466.6 4.5 add_bitcast_fusion
  471.0 0.4 select_bitcast_fusion.2
  471.4 2.8 collective-permute-start.5
  474.2 88.3 %collective-permute-done.5 = f32[1,512,1024]{2,1,0:T(8,128)S(1)} collective-permute-done((f32[1,512,1024]{2,1,0:T(8,128)S(1)}, f32[1,512,1024]{2,1,0:T(8,128)S(1)}, u32[]{:S(2)}, u32[]{:S(2)}) %collective-permute-start.5) | collective-permute-done | bytes 2097184 | tf_op jit(solution)/shard_map/ppermute | solution.py:14
  562.5 2.8 multiply_reduce_fusion.8
  565.3 2.1 pad_maximum_fusion.2
  567.3 0.0 reduce-scatter.2.cloned.1.call-done
  567.3 2.3 copy.18
  569.6 5.7 psum.23
  575.3 1.6 collective-permute-start.6
  576.9 2.0 collective-permute-done.6
  578.9 1.9 collective-permute-start.7
  580.8 1.7 collective-permute-done.7
  582.5 3.2 collective-permute-start.8
  585.7 1.5 collective-permute-done.8
  587.2 0.7 fusion.5
  587.9 0.6 sqrt_multiply_fusion
  590.9 4.3 bitcast_add_fusion
  (6 shorter events, 0.0 us)
Async XLA Ops:
  7.2 560.2 %reduce-scatter.2.cloned.1.call-start = ((), (), s32[]{:S(2)}) async-start(), calls=%async_computation.1 | async-start | bytes 5242880 | tf_op jit(solution)/shard_map/reduce_scatter | solution.py:20
  7.2 8.3 %copy-start = (bf16[512,4096]{1,0:T(8,128)(2,1)S(1)}, bf16[512,4096]{1,0:T(8,128)(2,1)}, u32[]{:S(2)}) copy-start(bf16[512,4096]{1,0:T(8,128)(2,1)} %param.4) | copy-start | bytes 12582916
  7.2 8.3 %copy-start.1 = (bf16[512,1024]{1,0:T(8,128)(2,1)S(1)}, bf16[512,1024]{1,0:T(8,128)(2,1)}, u32[]{:S(2)}) copy-start(bf16[512,1024]{1,0:T(8,128)(2,1)} %param.6) | copy-start | bytes 3145732
  118.8 183.7 %collective-permute-start = (f32[4,512,1024]{2,1,0:T(8,128)}, f32[4,512,1024]{2,1,0:T(8,128)}, u32[]{:S(2)}, u32[]{:S(2)}) collective-permute-start(f32[4,512,1024]{2,1,0:T(8,128)} %select_bitcast_fusion), channel_id=1, source_target_pairs={{0,4},{4,0},{8,12},{12,8},{16,20},{20,16},{24,28},{28,24},{1,5},{5... | collective-permute-start | bytes 25165832 | tf_op jit(solution)/shard_map/ppermute | solution.py:14
  323.1 3.6 collective-permute-start.1
  348.8 91.3 %collective-permute-start.2 = (f32[2,512,1024]{2,1,0:T(8,128)}, f32[2,512,1024]{2,1,0:T(8,128)}, u32[]{:S(2)}, u32[]{:S(2)}) collective-permute-start(f32[2,512,1024]{2,1,0:T(8,128)} %select_bitcast_fusion.1), channel_id=1, source_target_pairs={{0,8},{4,12},{8,0},{12,4},{16,24},{20,28},{24,16},{28,20},{1,9},{5... | collective-permute-start | bytes 12582920 | tf_op jit(solution)/shard_map/ppermute | solution.py:14
  456.2 3.6 collective-permute-start.3
  459.8 3.5 collective-permute-start.4
  471.4 91.1 %collective-permute-start.5 = (f32[1,512,1024]{2,1,0:T(8,128)S(1)}, f32[1,512,1024]{2,1,0:T(8,128)S(1)}, u32[]{:S(2)}, u32[]{:S(2)}) collective-permute-start(f32[1,512,1024]{2,1,0:T(8,128)S(1)} %select_bitcast_fusion.2), channel_id=1, source_target_pairs={{0,16},{4,20},{8,24},{12,28},{16,0},{20,4},{24,8},{28,12},{1,17},{... | collective-permute-start | bytes 6291464 | tf_op jit(solution)/shard_map/ppermute | solution.py:14
  575.3 3.6 collective-permute-start.6
  578.9 3.5 collective-permute-start.7
  582.5 4.7 collective-permute-start.8
Sparse Core Ops, SparseCore 0:
  360.0 44.9 reduce-scatter.1
where the time goes:
time: 604 us; the launch traced here: 602 us
  waiting for transfers between devices  360 us (60%)
  local copies, waits for them, and re-layouts  89.6 us (15%)
  other arithmetic  68 us (11%)
  matrix products  26 us (4%)
  between operations  21.8 us (4%)
  starting transfers between devices  19 us (3%)
  blocking collectives  17.4 us (3%)
    ppermute x9, waiting for transfers between devices, partner(): return lax.ppermute(value, axis, pairs)  360 us
    unnamed x7, local copies, waits for them, and re-layouts  43.7 us
    reduce_sum x3, other arithmetic, body(): jnp.sum(first * second)  23.8 us
    another operation x1, local copies, waits for them, and re-layouts, body(): paired = piece.reshape(piece.shape[0] // 2, 2, block_rows, columns)  22 us
    slice x1, local copies, waits for them, and re-layouts, body(): lower_half = paired[:, 0]  22 us
    ppermute x9, starting transfers between devices, partner(): return lax.ppermute(value, axis, pairs)  18.9 us
    psum x3, blocking collectives, body(): sums = lax.psum(partials, 'tensor')  17.4 us
    select_n x3, other arithmetic, body(): sent = jnp.where(is_lower, upper_half, lower_half)  16.7 us
  transfers between devices with their start and end apart: 10, of which 9 were waited for; matrix products, arithmetic and copies ran while one was open for 5% of the time, Pallas kernels for 0%

commit v1 on v0

v1 whole, which is shorter than its diff:
```python
import functools
import math

import jax
import jax.numpy as jnp
from jax import lax
from jax.experimental import pallas as pl
from jax.experimental.pallas import tpu as pltpu
from jax.sharding import PartitionSpec as P

QUAD = 4
PAIRS = [(a, b) for a in range(QUAD) for b in range(a, QUAD)]
LANES = 128
VMEM_LIMIT = 40 * 2**20


def exchange(value, axis, mask):
    pairs = [(source, source ^ mask) for source in range(lax.axis_size(axis))]
    return lax.ppermute(value, axis, pairs)


def total_over(value, dp_bits):
    mask = 1
    while mask < lax.axis_size("tensor"):
        value = value + exchange(value, "tensor", mask)
        mask *= 2
    for bit in range(dp_bits):
        value = value + exchange(value, "dp", 2**bit)
    return value


def dot(a, b):
    return jnp.dot(a, b, preferred_element_type=jnp.float32)


def group_products(xt, others, errors):
    e0, e1, e2, e3_top, e3_low = errors
    half = e3_top.shape[0]
    return [
        dot(xt[...], e0[...]),
        dot(others[0, 0], e1[...]),
        dot(others[0, 1], e2[...]),
        dot(others[0, 2, :, :half], e3_top[...]) + dot(others[0, 2, :, half:], e3_low[...]),
    ]


def gram_kernel(idx, xt, others, e0, e1, e2, e3_top, e3_low, out, tiles, acc):
    step = pl.program_id(0)

    @pl.when(step == 0)
    def _():
        acc[...] = jnp.zeros_like(acc)

    for k, tile in enumerate(group_products(xt, others, (e0, e1, e2, e3_top, e3_low))):
        tiles[k] = tile
    rows, columns = tiles.shape[1:]
    chunks = columns // LANES

    def strip(i, sums):
        at = pl.ds(pl.multiple_of(i * 8, 8), 8)
        sums = list(sums)
        for c in range(chunks):
            parts = [tiles[k, at, c * LANES:(c + 1) * LANES] for k in range(QUAD)]
            for n, (a, b) in enumerate(PAIRS):
                sums[n] = sums[n] + parts[a] * parts[b]
        return tuple(sums)

    sums = lax.fori_loop(0, rows // 8, strip, tuple(acc[n] for n in range(len(PAIRS))))
    for n in range(len(PAIRS)):
        acc[n] = sums[n]

    @pl.when(step == pl.num_programs(0) - 1)
    def _():
        lane = lax.broadcasted_iota(jnp.int32, (1, LANES), 1)
        turn = idx[0] * (QUAD + 1)
        result = jnp.zeros((1, LANES), jnp.float32)
        for n, (a, b) in enumerate(PAIRS):
            value = jnp.sum(jnp.sum(acc[n], axis=0, keepdims=True), axis=1, keepdims=True)
            place = jnp.bitwise_xor(QUAD * a + b, turn)
            mirror = jnp.bitwise_xor(QUAD * b + a, turn)
            result = jnp.where((lane == place) | (lane == mirror), value, result)
        out[...] = result


def gram(idx, xt, others, errors):
    steps, _, width, rows = others.shape
    columns = errors[0].shape[1]
    whole = lambda e: pl.BlockSpec(e.shape, lambda j, idx: (0, 0))
    return pl.pallas_call(
        gram_kernel,
        grid_spec=pltpu.PrefetchScalarGridSpec(
            num_scalar_prefetch=1,
            grid=(steps,),
            in_specs=[
                pl.BlockSpec((width, rows), lambda j, idx: (j, 0)),
                pl.BlockSpec((1, QUAD - 1, width, rows), lambda j, idx: (idx[1 + j], 0, 0, 0)),
                *[whole(e) for e in errors],
            ],
            out_specs=pl.BlockSpec((1, LANES), lambda j, idx: (0, 0)),
            scratch_shapes=[
                pltpu.VMEM((QUAD, width, columns), jnp.float32),
                pltpu.VMEM((len(PAIRS), 8, LANES), jnp.float32),
            ],
        ),
        out_shape=jax.ShapeDtypeStruct((1, LANES), jnp.float32),
        compiler_params=pltpu.CompilerParams(vmem_limit_bytes=VMEM_LIMIT),
        cost_estimate=pl.CostEstimate(
            flops=2 * QUAD * steps * width * rows * columns, bytes_accessed=6 * 2**20, transcendentals=0
        ),
        name="gram",
    )(idx, xt, others, *errors)


def merge_factors(gram_at):
    factors = [None] * QUAD
    for a, b in ((0, 1), (2, 3)):
        cross = gram_at(a, b)
        factors[a] = 1.0 - cross / (2.0 * gram_at(a, a))
        factors[b] = 1.0 - cross / (2.0 * gram_at(b, b))

    def product(left, right):
        return sum(factors[a] * factors[b] * gram_at(a, b) for a in left for b in right)

    cross = product((0, 1), (2, 3))
    first = 1.0 - cross / (2.0 * product((0, 1), (0, 1)))
    second = 1.0 - cross / (2.0 * product((2, 3), (2, 3)))
    return [factors[0] * first, factors[1] * first, factors[2] * second, factors[3] * second]


def merge_kernel(scale, idx, gram_ref, xt, others, e0, e1, e2, e3_top, e3_low, out):
    turn = idx[0] * (QUAD + 1)
    factors = merge_factors(lambda a, b: gram_ref[jnp.bitwise_xor(QUAD * a + b, turn)])
    tiles = group_products(xt, others, (e0, e1, e2, e3_top, e3_low))
    total = (factors[0] * scale) * tiles[0]
    for k in range(1, QUAD):
        total = total + (factors[k] * scale) * tiles[k]
    out[...] = total.astype(out.dtype)


def merge(idx, sums, xt, others, errors, dtype):
    _, _, width, rows = others.shape
    steps = (idx.shape[0] - 1) // 2
    columns = errors[0].shape[1]
    whole = lambda e: pl.BlockSpec(e.shape, lambda j, idx, sums: (0, 0))
    return pl.pallas_call(
        functools.partial(merge_kernel, 1.0 / math.sqrt(rows)),
        grid_spec=pltpu.PrefetchScalarGridSpec(
            num_scalar_prefetch=2,
            grid=(steps,),
            in_specs=[
                pl.BlockSpec((width, rows), lambda j, idx, sums: (idx[1 + j], 0)),
                pl.BlockSpec(
                    (1, QUAD - 1, width, rows), lambda j, idx, sums: (idx[1 + steps + j], 0, 0, 0)
                ),
                *[whole(e) for e in errors],
            ],
            out_specs=pl.BlockSpec((width, columns), lambda j, idx, sums: (j, 0)),
        ),
        out_shape=jax.ShapeDtypeStruct((steps * width, columns), dtype),
        compiler_params=pltpu.CompilerParams(vmem_limit_bytes=VMEM_LIMIT),
        cost_estimate=pl.CostEstimate(
            flops=2 * QUAD * steps * width * rows * columns, bytes_accessed=4 * 2**20, transcendentals=0
        ),
        name="merge",
    )(idx, sums.reshape(LANES), xt, others, *errors)


def body(inputs, weight, targets, momentum):
    groups = lax.axis_size("dp")
    parts = lax.axis_size("tensor")
    depth = groups.bit_length() - 1
    me = lax.axis_index("dp")
    part = lax.axis_index("tensor")
    rows, depth_width = inputs.shape
    columns = weight.shape[1]
    block = depth_width // groups
    blocks = groups // QUAD
    width = blocks * block // parts
    per_block = block // width
    place = me % QUAD

    def columns_of(at, start, size):
        first = (QUAD * (start // block) + at) * block + start % block
        return lax.dynamic_slice(inputs, (0, first), (rows, size)).T

    slabs = [exchange(columns_of(place ^ k, part * width, width), "dp", k) for k in range(1, QUAD)]
    others = jnp.stack(slabs)[None]
    mask = parts // 2
    while mask:
        others = jnp.concatenate([others, exchange(others, "tensor", mask)])
        mask //= 2
    own = jnp.concatenate([columns_of(place, b * block, block) for b in range(blocks)])

    def slot(j):
        mask, result, bit = parts // 2, 0, 0
        source = j ^ part
        while mask:
            result = result + ((source & mask) // mask << bit)
            mask, bit = mask // 2, bit + 1
        return result

    halves = []
    for h in range(2):
        at = slice(h * columns // 2, (h + 1) * columns // 2)
        outputs = dot(inputs, weight[:, at])
        halves.append((outputs - targets[:, at].astype(jnp.float32)).astype(jnp.bfloat16))
    errors = []
    for e0 in halves:
        e1 = exchange(e0, "dp", 1)
        e2 = exchange(e0, "dp", 2)
        top = exchange(e2[: rows // 2], "dp", 1)
        low = exchange(e1[rows // 2:], "dp", 2)
        errors.append((e0, e1, e2, top, low))

    idx = jnp.stack([place] + [slot(j) for j in range(parts)]).astype(jnp.int32)
    sums = gram(idx, own, others, errors[0]) + gram(idx, own, others, errors[1])
    sums = total_over(sums, 2)

    error = jnp.concatenate(halves, axis=1)
    summed = lax.psum_scatter(
        lax.dot_general(
            weight, error, (((1,), (1,)), ((), ())), preferred_element_type=jnp.float32
        ).astype(jnp.bfloat16),
        "tensor",
        scatter_dimension=0,
        tiled=True,
    )

    def tiles_of(bit):
        order = [(2 * i + bit) * per_block + s for i in range(blocks // 2) for s in range(per_block)]
        return jnp.stack([place] + order + [slot(j) for j in order]).astype(jnp.int32)

    bit = me >> 2 & 1
    sent = [merge(tiles_of(1 - bit), sums, own, others, e, jnp.bfloat16) for e in errors]
    received = [exchange(s, "dp", 4) for s in sent]
    kept = [merge(tiles_of(bit), sums, own, others, e, jnp.float32) for e in errors]
    for level in range(2, depth):
        if level > 2:
            bit = me >> level & 1
            paired = [v.reshape(v.shape[0] // (2 * block), 2, block, v.shape[1]) for v in merged]
            kept = [jnp.where(bit == 0, v[:, 0], v[:, 1]).reshape(-1, v.shape[-1]) for v in paired]
            sent = [jnp.where(bit == 0, v[:, 1], v[:, 0]).reshape(-1, v.shape[-1]) for v in paired]
            received = [exchange(s.astype(jnp.bfloat16), "dp", 2**level) for s in sent]
        lower = bit == 0
        cross = sum(jnp.sum(a * b.astype(jnp.float32)) for a, b in zip(kept, received))
        mine = sum(jnp.sum(a * a) for a in kept)
        theirs = sum(jnp.sum(jnp.square(b.astype(jnp.float32))) for b in received)
        sums = total_over(
            jnp.stack([cross, jnp.where(lower, mine, theirs), jnp.where(lower, theirs, mine)]), level + 1
        )
        lower_factor = 1.0 - sums[0] / (2.0 * sums[1])
        upper_factor = 1.0 - sums[0] / (2.0 * sums[2])
        factor = jnp.where(lower, lower_factor, upper_factor)
        other = jnp.where(lower, upper_factor, lower_factor)
        merged = [factor * a + other * b.astype(jnp.float32) for a, b in zip(kept, received)]
    combined = jnp.concatenate(merged, axis=1)
    return (summed, 0.9 * momentum + combined, jnp.sqrt(sums[1:3]) / depth_width)


def solution(mesh):
    return jax.shard_map(
        body,
        mesh=mesh,
        in_specs=(P("dp", None), P(None, "tensor"), P("dp", "tensor"), P("dp", "tensor")),
        out_specs=(P("tensor", "dp"), P("dp", "tensor"), P()),
        check_vma=False,
    )
```

time: 604 us -> 229 us (0.38)
  waiting for transfers between devices: 360 us -> 101 us
  local copies, waits for them, and re-layouts: 89.6 us -> 23.5 us
  other arithmetic: 68 us -> 14.8 us
  Pallas kernels: 0 us -> 23.6 us
  blocking collectives: 17.4 us -> 0 us
  matrix products: 26 us -> 14.8 us
  starting transfers between devices: 19 us -> 28.8 us
    ppermute x9 -> x24, waiting for transfers between devices: 360 us -> 101 us  [exchange(): return lax.ppermute(value, axis, pairs)]
    unnamed x7 -> x88, local copies, waits for them, and re-layouts: 43.7 us -> 17.1 us
    pallas_call x0 -> x6, Pallas kernels: none -> 23.6 us  [the longest x2 12.1 us: gram(): pl.pallas_call(gram_kernel, grid_spec=pltpu.PrefetchScalarGridSpec(num_sc...]
    another operation x1 -> x3, local copies, waits for them, and re-layouts: 22 us -> 0.25 us  [the longest x2 0.17 us: tiles_of(): jnp.stack([place] + order + [slot(j) for j in order]).astype(jnp.int32)]
    slice x4 -> x5, local copies, waits for them, and re-layouts: 23.8 us -> 2.25 us  [the longest x2 0.81 us: body(): low = exchange(e1[rows // 2:], 'dp', 2)]
    reduce_sum x3 -> x2, other arithmetic: 23.8 us -> 4.01 us  [body(): jnp.sum(a * b.astype(jnp.float32))]
    psum x3 -> x0, blocking collectives: 17.4 us -> none  [body(): sums = lax.psum(partials, 'tensor')]
    select_n x3 -> x0, other arithmetic: 16.7 us -> none  [body(): sent = jnp.where(is_lower, upper_half, lower_half)]
  transfers between devices with their start and end apart: 10 -> 25, of which waited for: 9 -> 19; matrix products, arithmetic and copies ran while one was open for 5% -> 11% of each run, Pallas kernels for 0% -> 10%
where the time goes in v1:
time: 229 us; the launch traced here: 228 us
  waiting for transfers between devices  101 us (44%)
  starting transfers between devices  28.8 us (13%)
  Pallas kernels  23.6 us (10%)
  local copies, waits for them, and re-layouts  23.5 us (10%)
  between operations  20.9 us (9%)
  matrix products  14.8 us (6%)
  other arithmetic  14.8 us (6%)
    ppermute x24, waiting for transfers between devices, exchange(): return lax.ppermute(value, axis, pairs)  101 us
    ppermute x24, starting transfers between devices, exchange(): return lax.ppermute(value, axis, pairs)  28.8 us
    unnamed x88, local copies, waits for them, and re-layouts  17.1 us
    pallas_call x2, Pallas kernels, gram(): pl.pallas_call(gram_kernel, grid_spec=pltpu.PrefetchScalarGridSpec(num_sc...  12.1 us
    pallas_call x4, Pallas kernels, merge(): pl.pallas_call(functools.partial(merge_kernel, 1.0 / math.sqrt(rows)), gr...  11.6 us
    dot_general x2, matrix products, dot(): return jnp.dot(a, b, preferred_element_type=jnp.float32)  8.31 us
    dot_general x1, matrix products, body(): lax.dot_general(weight, error, (((1,), (1,)), ((), ())), preferred_elemen...  6.46 us
  transfers between devices with their start and end apart: 25, of which 19 were waited for; matrix products, arithmetic and copies ran while one was open for 11% of the time, Pallas kernels for 10%

profile of v1, /device:TPU:0, one launch (start us, length us, event | category | flops | bytes accessed | tf_op | source)
XLA Modules:
  0.0 227.8 jit_solution(10731691322743316303)
XLA Ops:
  7.2 6.0 %fusion.11.e0 = bf16[512,512]{1,0:T(8,128)(2,1)S(1)} fusion(bf16[512,4096]{1,0:T(8,128)(2,1)} %param.4, bf16[4096,1024]{1,0:T(8,128)(2,1)} %param.5, bf16[512,1024]{1,0:T(8,128)(2,1)} %param.6), kind=kOutput, calls=%fused_computation.17 | convolution fusion | flops 2148270080 | bytes 9437184 | tf_op jit(solution)/shard_map/dot_general | solution.py:33
  13.2 1.5 copy-done.39
  14.7 2.3 %fusion.14.e0 = bf16[512,512]{1,0:T(8,128)(2,1)S(1)} fusion(bf16[512,4096]{1,0:T(8,128)(2,1)S(1)} %copy-done.38, bf16[4096,1024]{1,0:T(8,128)(2,1)S(1)} %copy-done.39, bf16[512,1024]{1,0:T(8,128)(2,1)S(1)} %copy-done.40), kind=kOutput, calls=%fused_computation.18 | convolution fusion | flops 2148270080 | bytes 9437184 | tf_op jit(solution)/shard_map/dot_general | solution.py:33
  17.1 6.5 %fusion = bf16[4096,512]{0,1:T(8,128)(2,1)} fusion(bf16[4096,1024]{1,0:T(8,128)(2,1)S(1)} %copy-done.39, bf16[512,512]{1,0:T(8,128)(2,1)S(1)} %fusion.11.e0, bf16[512,512]{1,0:T(8,128)(2,1)S(1)} %fusion.14.e0), kind=kOutput, calls=%fused_computation.1 | convolution fusion | flops 4299161600 | bytes 13631488 | tf_op jit(solution)/shard_map/dot_general | solution.py:221
  23.6 1.6 constant_dynamic-slice_fusion.2
  25.4 3.0 %collective-permute-start = (bf16[256,512]{1,0:T(8,128)(2,1)S(1)}, bf16[256,512]{1,0:T(8,128)(2,1)S(1)}, u32[]{:S(2)}, u32[]{:S(2)}) collective-permute-start(bf16[256,512]{1,0:T(8,128)(2,1)S(1)} %bitcast.37), channel_id=1, source_target_pairs={{0,4},{4,0},{8,12},{12,8},{16,20},{20,16},{24,28},{28,24},{1,5},{5... | collective-permute-start | bytes 786440 | tf_op jit(solution)/shard_map/ppermute | solution.py:19
  28.6 1.6 collective-permute-start.1
  30.4 4.3 %collective-permute-done = bf16[256,512]{1,0:T(8,128)(2,1)S(1)} collective-permute-done((bf16[256,512]{1,0:T(8,128)(2,1)S(1)}, bf16[256,512]{1,0:T(8,128)(2,1)S(1)}, u32[]{:S(2)}, u32[]{:S(2)}) %collective-permute-start) | collective-permute-done | bytes 262176 | tf_op jit(solution)/shard_map/ppermute | solution.py:19
  34.7 3.1 %collective-permute-done.1 = bf16[256,512]{1,0:T(8,128)(2,1)S(1)} collective-permute-done((bf16[256,512]{1,0:T(8,128)(2,1)S(1)}, bf16[256,512]{1,0:T(8,128)(2,1)S(1)}, u32[]{:S(2)}, u32[]{:S(2)}) %collective-permute-start.1) | collective-permute-done | bytes 262176 | tf_op jit(solution)/shard_map/ppermute | solution.py:19
  37.9 3.9 %collective-permute-done.2 = bf16[256,512]{1,0:T(8,128)(2,1)S(1)} collective-permute-done((bf16[256,512]{1,0:T(8,128)(2,1)S(1)}, bf16[256,512]{1,0:T(8,128)(2,1)S(1)}, u32[]{:S(2)}, u32[]{:S(2)}) %collective-permute-start.2) | collective-permute-done | bytes 262176 | tf_op jit(solution)/shard_map/ppermute | solution.py:19
  41.9 1.7 collective-permute-start.3
  43.6 32.2 %collective-permute-done.3 = bf16[1,3,256,512]{3,2,1,0:T(8,128)(2,1)S(1)} collective-permute-done((bf16[1,3,256,512]{3,2,1,0:T(8,128)(2,1)S(1)}, bf16[1,3,256,512]{3,2,1,0:T(8,128)(2,1)S(1)}, u32[]{:S(2)}, u32[]{:S(2)}) %collective-permute-start.3) | collective-permute-done | bytes 786464 | tf_op jit(solution)/shard_map/ppermute | solution.py:19
  75.8 1.4 pad_maximum_fusion.1
  77.2 1.6 collective-permute-start.10
  78.7 1.6 collective-permute-start.9
  81.2 2.3 %constant_dynamic-slice_fusion.4 = (bf16[512,512]{1,0:T(8,128)(2,1)}, bf16[512,512]{1,0:T(8,128)(2,1)}) fusion(bf16[512,4096]{1,0:T(8,128)(2,1)} %param.4, s32[]{:T(128)S(6)} %select_n.96, s32[]{:T(128)S(6)} %select_n.97), kind=kLoop, calls=%fused_computation.36 | loop fusion | bytes 2097160 | tf_op jit(solution)/shard_map/dynamic_slice | solution.py:184
  83.5 2.1 copy.17
  85.6 2.0 copy.18
  87.6 4.2 %collective-permute-done.10.e2 = bf16[512,512]{1,0:T(8,128)(2,1)S(1)} collective-permute-done((bf16[512,512]{1,0:T(8,128)(2,1)S(1)}, bf16[512,512]{1,0:T(8,128)(2,1)S(1)}, u32[]{:S(2)}, u32[]{:S(2)}) %collective-permute-start.10) | collective-permute-done | bytes 524320 | tf_op jit(solution)/shard_map/ppermute | solution.py:19
  92.6 1.4 collective-permute-start.11
  94.1 0.8 slice.52
  94.9 1.7 collective-permute-start.12
  96.6 2.2 pad_maximum_fusion.2.xt
  98.9 4.2 %collective-permute-done.6.e2 = bf16[512,512]{1,0:T(8,128)(2,1)S(1)} collective-permute-done((bf16[512,512]{1,0:T(8,128)(2,1)S(1)}, bf16[512,512]{1,0:T(8,128)(2,1)S(1)}, u32[]{:S(2)}, u32[]{:S(2)}) %collective-permute-start.6) | collective-permute-done | bytes 524320 | tf_op jit(solution)/shard_map/ppermute | solution.py:19
  103.1 1.5 collective-permute-start.7
  104.8 1.7 collective-permute-start.8
  106.5 2.2 pad_maximum_fusion.others
  108.8 1.6 collective-permute-done.11.e3_top
  110.4 6.5 %gram.3 = f32[1,128]{1,0:T(1,128)S(1)} custom-call(s32[5]{0:T(128)S(1)} %stack.96.idx, bf16[1024,512]{1,0:T(8,128)(2,1)S(1)} %copy-done, bf16[4,3,256,512]{3,2,1,0:T(8,128)(2,1)S(1)} %pad_maximum_fusion.others, bf16[512,512]{1,0:T(8,128)(2,1)S(1)} %copy-done.26, bf16[512,512]{1,0:T(8,128)(2,1)S(1)} %copy-done.14, bf16[512,512]{1,0:T(8,128)(2,1)S(1)} %copy-done.6, ...), custom_call_target="tpu_custom_call" | custom-call | flops 2147483648 | bytes 6291456 | tf_op jit(solution)/shard_map/gram/pallas_call | solution.py:89
  117.0 5.6 %gram.2 = f32[1,128]{1,0:T(1,128)S(1)} custom-call(s32[5]{0:T(128)S(1)} %stack.96.idx, bf16[1024,512]{1,0:T(8,128)(2,1)S(1)} %copy-done, bf16[4,3,256,512]{3,2,1,0:T(8,128)(2,1)S(1)} %pad_maximum_fusion.others, bf16[512,512]{1,0:T(8,128)(2,1)S(1)} %copy-done.22, bf16[512,512]{1,0:T(8,128)(2,1)S(1)} %copy-done.18, bf16[512,512]{1,0:T(8,128)(2,1)S(1)} %copy-done.10, ...), custom_call_target="tpu_custom_call" | custom-call | flops 2147483648 | bytes 6291456 | tf_op jit(solution)/shard_map/gram/pallas_call | solution.py:89
  122.7 1.1 collective-permute-done.13
  123.8 2.4 %collective-permute-start.14 = (f32[1,128]{1,0:T(1,128)S(1)}, f32[1,128]{1,0:T(1,128)S(1)}, u32[]{:S(2)}, u32[]{:S(2)}) collective-permute-start(f32[1,128]{1,0:T(1,128)S(1)} %add.170), channel_id=1, source_target_pairs={{0,2},{1,3},{2,0},{3,1},{4,6},{5,7},{6,4},{7,5},{8,10},{9,11},{10,... | collective-permute-start | bytes 1544 | tf_op jit(solution)/shard_map/ppermute | solution.py:19
  126.1 1.5 collective-permute-done.14
  127.6 1.7 collective-permute-start.15
  129.3 1.8 collective-permute-done.15
  131.9 2.9 %collective-permute-done.16 = f32[1,128]{1,0:T(1,128)S(1)} collective-permute-done((f32[1,128]{1,0:T(1,128)S(1)}, f32[1,128]{1,0:T(1,128)S(1)}, u32[]{:S(2)}, u32[]{:S(2)}) %collective-permute-start.16) | collective-permute-done | bytes 544 | tf_op jit(solution)/shard_map/ppermute | solution.py:19
  134.7 1.2 copy-done.1
  136.0 1.0 copy-done.7
  137.0 1.0 copy-done.15
  138.1 1.0 copy-done.27
  139.1 3.7 %merge.7 = bf16[512,512]{1,0:T(8,128)(2,1)} custom-call(s32[5]{0:T(128)S(1)} %stack.105.idx, f32[128]{0:T(128)S(1)} %add_bitcast_fusion.gram_ref, bf16[1024,512]{1,0:T(8,128)(2,1)S(1)} %copy-done.1, bf16[4,3,256,512]{3,2,1,0:T(8,128)(2,1)S(1)} %pad_maximum_fusion.others, bf16[512,512]{1,0:T(8,128)(2,1)S(1)} %copy-done.27, bf16[512,512]{1,0:T(8,128)(2,1)S(1)} %copy-done.15, ...), custom_call_target="tpu_custom_call" | custom-call | flops 1073741824 | bytes 4194304 | tf_op jit(solution)/shard_map/merge/pallas_call | solution.py:145
  142.9 2.8 %collective-permute-start.18 = (bf16[512,512]{1,0:T(8,128)(2,1)}, bf16[512,512]{1,0:T(8,128)(2,1)}, u32[]{:S(2)}, u32[]{:S(2)}) collective-permute-start(bf16[512,512]{1,0:T(8,128)(2,1)} %merge.7), channel_id=1, source_target_pairs={{0,16},{4,20},{8,24},{12,28},{16,0},{20,4},{24,8},{28,12},{1,17},{... | collective-permute-start | bytes 1572872 | tf_op jit(solution)/shard_map/ppermute | solution.py:19
  145.7 2.7 %merge.5 = bf16[512,512]{1,0:T(8,128)(2,1)} custom-call(s32[5]{0:T(128)S(1)} %stack.105.idx, f32[128]{0:T(128)S(1)} %add_bitcast_fusion.gram_ref, bf16[1024,512]{1,0:T(8,128)(2,1)S(1)} %copy-done.1, bf16[4,3,256,512]{3,2,1,0:T(8,128)(2,1)S(1)} %pad_maximum_fusion.others, bf16[512,512]{1,0:T(8,128)(2,1)S(1)} %copy-done.23, bf16[512,512]{1,0:T(8,128)(2,1)S(1)} %copy-done.19, ...), custom_call_target="tpu_custom_call" | custom-call | flops 1073741824 | bytes 4194304 | tf_op jit(solution)/shard_map/merge/pallas_call | solution.py:145
  148.6 1.2 copy-done.2
  149.9 1.0 copy-done.8
  150.9 1.0 copy-done.16
  151.9 1.0 copy-done.28
  153.0 3.0 %merge.6 = f32[512,512]{1,0:T(8,128)S(1)} custom-call(s32[5]{0:T(128)S(1)} %stack.91.idx, f32[128]{0:T(128)S(1)} %add_bitcast_fusion.gram_ref, bf16[1024,512]{1,0:T(8,128)(2,1)S(1)} %copy-done.2, bf16[4,3,256,512]{3,2,1,0:T(8,128)(2,1)S(1)} %pad_maximum_fusion.others, bf16[512,512]{1,0:T(8,128)(2,1)S(1)} %copy-done.28, bf16[512,512]{1,0:T(8,128)(2,1)S(1)} %copy-done.16, ...), custom_call_target="tpu_custom_call" | custom-call | flops 1073741824 | bytes 4194304 | tf_op jit(solution)/shard_map/merge/pallas_call | solution.py:145
  156.1 2.0 merge.4
  158.2 19.4 %collective-permute-done.18 = bf16[512,512]{1,0:T(8,128)(2,1)} collective-permute-done((bf16[512,512]{1,0:T(8,128)(2,1)}, bf16[512,512]{1,0:T(8,128)(2,1)}, u32[]{:S(2)}, u32[]{:S(2)}) %collective-permute-start.18) | collective-permute-done | bytes 524320 | tf_op jit(solution)/shard_map/ppermute | solution.py:19
  177.5 2.0 fusion.20
  179.5 9.1 %collective-permute-done.17 = bf16[512,512]{1,0:T(8,128)(2,1)} collective-permute-done((bf16[512,512]{1,0:T(8,128)(2,1)}, bf16[512,512]{1,0:T(8,128)(2,1)}, u32[]{:S(2)}, u32[]{:S(2)}) %collective-permute-start.17) | collective-permute-done | bytes 524320 | tf_op jit(solution)/shard_map/ppermute | solution.py:19
  188.7 2.0 fusion.17
  194.6 1.1 collective-permute-done.19
  195.8 1.7 collective-permute-start.20
  197.6 1.8 collective-permute-done.20
  199.4 1.5 collective-permute-start.21
  200.9 2.0 collective-permute-done.21
  203.0 3.5 %collective-permute-done.22 = f32[3]{0:T(128)S(1)} collective-permute-done((f32[3]{0:T(128)S(1)}, f32[3]{0:T(128)S(1)}, u32[]{:S(2)}, u32[]{:S(2)}) %collective-permute-start.22) | collective-permute-done | bytes 44 | tf_op jit(solution)/shard_map/ppermute | solution.py:19
  206.5 1.1 collective-permute-start.23
  207.6 3.4 %collective-permute-done.23 = f32[3]{0:T(128)S(1)} collective-permute-done((f32[3]{0:T(128)S(1)}, f32[3]{0:T(128)S(1)}, u32[]{:S(2)}, u32[]{:S(2)}) %collective-permute-start.23) | collective-permute-done | bytes 44 | tf_op jit(solution)/shard_map/ppermute | solution.py:19
  214.7 2.2 fusion.19
  217.0 1.8 maximum_add_fusion
  218.7 2.3 copy.14
  (114 shorter events, 5.2 us)
Async XLA Ops:
  7.2 6.1 %copy-start.40 = (bf16[512,1024]{1,0:T(8,128)(2,1)S(1)}, bf16[512,1024]{1,0:T(8,128)(2,1)}, u32[]{:S(2)}) copy-start(bf16[512,1024]{1,0:T(8,128)(2,1)} %param.6) | copy-start | bytes 3145732
  7.2 211.5 %reduce-scatter.2.cloned.1.call-start = ((), (), s32[]{:S(2)}) async-start(), calls=%async_computation.1 | async-start | bytes 5242880 | tf_op jit(solution)/shard_map/reduce_scatter | solution.py:220
  7.2 6.0 %copy-start.38 = (bf16[512,4096]{1,0:T(8,128)(2,1)S(1)}, bf16[512,4096]{1,0:T(8,128)(2,1)}, u32[]{:S(2)}) copy-start(bf16[512,4096]{1,0:T(8,128)(2,1)} %param.4) | copy-start | bytes 12582916
  7.2 7.5 %copy-start.39 = (bf16[4096,1024]{1,0:T(8,128)(2,1)S(1)}, bf16[4096,1024]{1,0:T(8,128)(2,1)}, u32[]{:S(2)}) copy-start(bf16[4096,1024]{1,0:T(8,128)(2,1)} %param.5) | copy-start | bytes 25165828
  14.7 64.0 %copy-start.25 = (bf16[512,512]{1,0:T(8,128)(2,1)}, bf16[512,512]{1,0:T(8,128)(2,1)S(1)}, u32[]{:S(2)}) copy-start(bf16[512,512]{1,0:T(8,128)(2,1)S(1)} %fusion.11.e0) | copy-start | bytes 1572868
  17.1 63.5 %copy-start.21 = (bf16[512,512]{1,0:T(8,128)(2,1)}, bf16[512,512]{1,0:T(8,128)(2,1)S(1)}, u32[]{:S(2)}) copy-start(bf16[512,512]{1,0:T(8,128)(2,1)S(1)} %fusion.14.e0) | copy-start | bytes 1572868
  25.4 9.3 %collective-permute-start = (bf16[256,512]{1,0:T(8,128)(2,1)S(1)}, bf16[256,512]{1,0:T(8,128)(2,1)S(1)}, u32[]{:S(2)}, u32[]{:S(2)}) collective-permute-start(bf16[256,512]{1,0:T(8,128)(2,1)S(1)} %bitcast.37), channel_id=1, source_target_pairs={{0,4},{4,0},{8,12},{12,8},{16,20},{20,16},{24,28},{28,24},{1,5},{5... | collective-permute-start | bytes 786440 | tf_op jit(solution)/shard_map/ppermute | solution.py:19
  28.6 9.3 %collective-permute-start.1 = (bf16[256,512]{1,0:T(8,128)(2,1)S(1)}, bf16[256,512]{1,0:T(8,128)(2,1)S(1)}, u32[]{:S(2)}, u32[]{:S(2)}) collective-permute-start(bf16[256,512]{1,0:T(8,128)(2,1)S(1)} %bitcast.38), channel_id=1, source_target_pairs={{0,8},{4,12},{8,0},{12,4},{16,24},{20,28},{24,16},{28,20},{1,9},{5... | collective-permute-start | bytes 786440 | tf_op jit(solution)/shard_map/ppermute | solution.py:19
  30.3 11.4 %collective-permute-start.2 = (bf16[256,512]{1,0:T(8,128)(2,1)S(1)}, bf16[256,512]{1,0:T(8,128)(2,1)S(1)}, u32[]{:S(2)}, u32[]{:S(2)}) collective-permute-start(bf16[256,512]{1,0:T(8,128)(2,1)S(1)} %bitcast.39), channel_id=1, source_target_pairs={{0,12},{4,8},{8,4},{12,0},{16,28},{20,24},{24,20},{28,16},{1,13},{... | collective-permute-start | bytes 786440 | tf_op jit(solution)/shard_map/ppermute | solution.py:19
  41.9 38.4 %copy-start.35 = (bf16[1,3,256,512]{3,2,1,0:T(8,128)(2,1)}, bf16[1,3,256,512]{3,2,1,0:T(8,128)(2,1)S(1)}, u32[]{:S(2)}) copy-start(bf16[1,3,256,512]{3,2,1,0:T(8,128)(2,1)S(1)} %maximum_bitcast_fusion) | copy-start | bytes 2359300
  41.9 33.9 %collective-permute-start.3 = (bf16[1,3,256,512]{3,2,1,0:T(8,128)(2,1)S(1)}, bf16[1,3,256,512]{3,2,1,0:T(8,128)(2,1)S(1)}, u32[]{:S(2)}, u32[]{:S(2)}) collective-permute-start(bf16[1,3,256,512]{3,2,1,0:T(8,128)(2,1)S(1)} %maximum_bitcast_fusion), channel_id=1, source_target_pairs={{0,2},{1,3},{2,0},{3,1},{4,6},{5,7},{6,4},{7,5},{8,10},{9,11},{10,... | collective-permute-start | bytes 2359304 | tf_op jit(solution)/shard_map/ppermute | solution.py:19
  75.8 4.9 %copy-start.36 = (bf16[1,3,256,512]{3,2,1,0:T(8,128)(2,1)}, bf16[1,3,256,512]{3,2,1,0:T(8,128)(2,1)S(1)}, u32[]{:S(2)}) copy-start(bf16[1,3,256,512]{3,2,1,0:T(8,128)(2,1)S(1)} %collective-permute-done.3) | copy-start | bytes 2359300
  77.2 29.3 %collective-permute-start.4 = (bf16[2,3,256,512]{3,2,1,0:T(8,128)(2,1)}, bf16[2,3,256,512]{3,2,1,0:T(8,128)(2,1)}, u32[]{:S(2)}, u32[]{:S(2)}) collective-permute-start(bf16[2,3,256,512]{3,2,1,0:T(8,128)(2,1)} %pad_maximum_fusion.1), channel_id=1, source_target_pairs={{0,1},{1,0},{2,3},{3,2},{4,5},{5,4},{6,7},{7,6},{8,9},{9,8},{10,11... | collective-permute-start | bytes 4718600 | tf_op jit(solution)/shard_map/ppermute | solution.py:19
  77.2 14.7 %collective-permute-start.10 = (bf16[512,512]{1,0:T(8,128)(2,1)S(1)}, bf16[512,512]{1,0:T(8,128)(2,1)S(1)}, u32[]{:S(2)}, u32[]{:S(2)}) collective-permute-start(bf16[512,512]{1,0:T(8,128)(2,1)S(1)} %fusion.11.e0), channel_id=1, source_target_pairs={{0,8},{4,12},{8,0},{12,4},{16,24},{20,28},{24,16},{28,20},{1,9},{5... | collective-permute-start | bytes 1572872 | tf_op jit(solution)/shard_map/ppermute | solution.py:19
  78.7 15.3 %collective-permute-start.9 = (bf16[512,512]{1,0:T(8,128)(2,1)S(1)}, bf16[512,512]{1,0:T(8,128)(2,1)S(1)}, u32[]{:S(2)}, u32[]{:S(2)}) collective-permute-start(bf16[512,512]{1,0:T(8,128)(2,1)S(1)} %fusion.11.e0), channel_id=1, source_target_pairs={{0,4},{4,0},{8,12},{12,8},{16,20},{20,16},{24,28},{28,24},{1,5},{5... | collective-permute-start | bytes 1572872 | tf_op jit(solution)/shard_map/ppermute | solution.py:19
  80.3 22.8 %collective-permute-start.6 = (bf16[512,512]{1,0:T(8,128)(2,1)S(1)}, bf16[512,512]{1,0:T(8,128)(2,1)S(1)}, u32[]{:S(2)}, u32[]{:S(2)}) collective-permute-start(bf16[512,512]{1,0:T(8,128)(2,1)S(1)} %fusion.14.e0), channel_id=1, source_target_pairs={{0,8},{4,12},{8,0},{12,4},{16,24},{20,28},{24,16},{28,20},{1,9},{5... | collective-permute-start | bytes 1572872 | tf_op jit(solution)/shard_map/ppermute | solution.py:19
  80.6 24.1 %collective-permute-start.5 = (bf16[512,512]{1,0:T(8,128)(2,1)S(1)}, bf16[512,512]{1,0:T(8,128)(2,1)S(1)}, u32[]{:S(2)}, u32[]{:S(2)}) collective-permute-start(bf16[512,512]{1,0:T(8,128)(2,1)S(1)} %fusion.14.e0), channel_id=1, source_target_pairs={{0,4},{4,0},{8,12},{12,8},{16,20},{20,16},{24,28},{28,24},{1,5},{5... | collective-permute-start | bytes 1572872 | tf_op jit(solution)/shard_map/ppermute | solution.py:19
  91.9 14.6 %copy-start.5 = (bf16[512,512]{1,0:T(8,128)(2,1)}, bf16[512,512]{1,0:T(8,128)(2,1)S(1)}, u32[]{:S(2)}) copy-start(bf16[512,512]{1,0:T(8,128)(2,1)S(1)} %collective-permute-done.10.e2) | copy-start | bytes 1572868
  92.6 17.7 %collective-permute-start.11 = (bf16[256,512]{1,0:T(8,128)(2,1)}, bf16[256,512]{1,0:T(8,128)(2,1)S(1)}, u32[]{:S(2)}, u32[]{:S(2)}) collective-permute-start(bf16[256,512]{1,0:T(8,128)(2,1)} %slice.51), channel_id=1, source_target_pairs={{0,4},{4,0},{8,12},{12,8},{16,20},{20,16},{24,28},{28,24},{1,5},{5... | collective-permute-start | bytes 786440 | tf_op jit(solution)/shard_map/ppermute | solution.py:19
  94.1 12.4 %copy-start.13 = (bf16[512,512]{1,0:T(8,128)(2,1)}, bf16[512,512]{1,0:T(8,128)(2,1)S(1)}, u32[]{:S(2)}) copy-start(bf16[512,512]{1,0:T(8,128)(2,1)S(1)} %collective-permute-done.9.e1) | copy-start | bytes 1572868
  94.9 15.5 %collective-permute-start.12 = (bf16[256,512]{1,0:T(8,128)(2,1)}, bf16[256,512]{1,0:T(8,128)(2,1)}, u32[]{:S(2)}, u32[]{:S(2)}) collective-permute-start(bf16[256,512]{1,0:T(8,128)(2,1)} %slice.52), channel_id=1, source_target_pairs={{0,8},{4,12},{8,0},{12,4},{16,24},{20,28},{24,16},{28,20},{1,9},{5... | collective-permute-start | bytes 786440 | tf_op jit(solution)/shard_map/ppermute | solution.py:19
  103.1 3.3 %copy-start.9 = (bf16[512,512]{1,0:T(8,128)(2,1)}, bf16[512,512]{1,0:T(8,128)(2,1)S(1)}, u32[]{:S(2)}) copy-start(bf16[512,512]{1,0:T(8,128)(2,1)S(1)} %collective-permute-done.6.e2) | copy-start | bytes 1572868
  103.1 13.8 %collective-permute-start.7 = (bf16[256,512]{1,0:T(8,128)(2,1)S(1)}, bf16[256,512]{1,0:T(8,128)(2,1)S(1)}, u32[]{:S(2)}, u32[]{:S(2)}) collective-permute-start(bf16[256,512]{1,0:T(8,128)(2,1)S(1)} %slice.49), channel_id=1, source_target_pairs={{0,4},{4,0},{8,12},{12,8},{16,20},{20,16},{24,28},{28,24},{1,5},{5... | collective-permute-start | bytes 786440 | tf_op jit(solution)/shard_map/ppermute | solution.py:19
  104.7 1.8 copy-start.17
  104.7 5.6 %copy-start = (bf16[1024,512]{1,0:T(8,128)(2,1)S(1)}, bf16[1024,512]{1,0:T(8,128)(2,1)}, u32[]{:S(2)}) copy-start(bf16[1024,512]{1,0:T(8,128)(2,1)} %pad_maximum_fusion.2.xt) | copy-start | bytes 3145732
  104.8 5.6 %copy-start.26 = (bf16[512,512]{1,0:T(8,128)(2,1)S(1)}, bf16[512,512]{1,0:T(8,128)(2,1)}, u32[]{:S(2)}) copy-start(bf16[512,512]{1,0:T(8,128)(2,1)} %copy-done.25) | copy-start | bytes 1572868
  104.8 12.2 %collective-permute-start.8 = (bf16[256,512]{1,0:T(8,128)(2,1)S(1)}, bf16[256,512]{1,0:T(8,128)(2,1)S(1)}, u32[]{:S(2)}, u32[]{:S(2)}) collective-permute-start(bf16[256,512]{1,0:T(8,128)(2,1)S(1)} %slice.50), channel_id=1, source_target_pairs={{0,8},{4,12},{8,0},{12,4},{16,24},{20,28},{24,16},{28,20},{1,9},{5... | collective-permute-start | bytes 786440 | tf_op jit(solution)/shard_map/ppermute | solution.py:19
  106.5 3.9 %copy-start.6 = (bf16[512,512]{1,0:T(8,128)(2,1)S(1)}, bf16[512,512]{1,0:T(8,128)(2,1)}, u32[]{:S(2)}) copy-start(bf16[512,512]{1,0:T(8,128)(2,1)} %copy-done.5) | copy-start | bytes 1572868
  106.5 3.9 %copy-start.14 = (bf16[512,512]{1,0:T(8,128)(2,1)S(1)}, bf16[512,512]{1,0:T(8,128)(2,1)}, u32[]{:S(2)}) copy-start(bf16[512,512]{1,0:T(8,128)(2,1)} %copy-done.13) | copy-start | bytes 1572868
  108.7 8.2 %copy-start.10 = (bf16[512,512]{1,0:T(8,128)(2,1)S(1)}, bf16[512,512]{1,0:T(8,128)(2,1)}, u32[]{:S(2)}) copy-start(bf16[512,512]{1,0:T(8,128)(2,1)} %copy-done.9) | copy-start | bytes 1572868
  108.8 8.2 %copy-start.18 = (bf16[512,512]{1,0:T(8,128)(2,1)S(1)}, bf16[512,512]{1,0:T(8,128)(2,1)}, u32[]{:S(2)}) copy-start(bf16[512,512]{1,0:T(8,128)(2,1)} %copy-done.17) | copy-start | bytes 1572868
  108.8 8.2 %copy-start.22 = (bf16[512,512]{1,0:T(8,128)(2,1)S(1)}, bf16[512,512]{1,0:T(8,128)(2,1)}, u32[]{:S(2)}) copy-start(bf16[512,512]{1,0:T(8,128)(2,1)} %copy-done.21) | copy-start | bytes 1572868
  116.9 5.6 %copy-start.29 = (bf16[256,512]{1,0:T(8,128)(2,1)}, bf16[256,512]{1,0:T(8,128)(2,1)S(1)}, u32[]{:S(2)}) copy-start(bf16[256,512]{1,0:T(8,128)(2,1)S(1)} %collective-permute-done.7.e3_top) | copy-start | bytes 786436
  117.0 5.6 %copy-start.32 = (bf16[256,512]{1,0:T(8,128)(2,1)}, bf16[256,512]{1,0:T(8,128)(2,1)S(1)}, u32[]{:S(2)}) copy-start(bf16[256,512]{1,0:T(8,128)(2,1)S(1)} %collective-permute-done.8.e3_low) | copy-start | bytes 786436
  122.6 1.2 collective-permute-start.13
  123.8 3.9 %collective-permute-start.14 = (f32[1,128]{1,0:T(1,128)S(1)}, f32[1,128]{1,0:T(1,128)S(1)}, u32[]{:S(2)}, u32[]{:S(2)}) collective-permute-start(f32[1,128]{1,0:T(1,128)S(1)} %add.170), channel_id=1, source_target_pairs={{0,2},{1,3},{2,0},{3,1},{4,6},{5,7},{6,4},{7,5},{8,10},{9,11},{10,... | collective-permute-start | bytes 1544 | tf_op jit(solution)/shard_map/ppermute | solution.py:19
  127.6 3.5 %collective-permute-start.15 = (f32[1,128]{1,0:T(1,128)S(1)}, f32[1,128]{1,0:T(1,128)S(1)}, u32[]{:S(2)}, u32[]{:S(2)}) collective-permute-start(f32[1,128]{1,0:T(1,128)S(1)} %add.171), channel_id=1, source_target_pairs={{0,4},{4,0},{8,12},{12,8},{16,20},{20,16},{24,28},{28,24},{1,5},{5... | collective-permute-start | bytes 1544 | tf_op jit(solution)/shard_map/ppermute | solution.py:19
  131.2 3.5 %collective-permute-start.16 = (f32[1,128]{1,0:T(1,128)S(1)}, f32[1,128]{1,0:T(1,128)S(1)}, u32[]{:S(2)}, u32[]{:S(2)}) collective-permute-start(f32[1,128]{1,0:T(1,128)S(1)} %add.172), channel_id=1, source_target_pairs={{0,8},{4,12},{8,0},{12,4},{16,24},{20,28},{24,16},{28,20},{1,9},{5... | collective-permute-start | bytes 1544 | tf_op jit(solution)/shard_map/ppermute | solution.py:19
  134.7 1.2 copy-start.1
  136.0 1.0 copy-start.7
  137.0 1.0 copy-start.15
  138.0 1.0 copy-start.27
  139.1 6.6 %copy-start.11 = (bf16[512,512]{1,0:T(8,128)(2,1)S(1)}, bf16[512,512]{1,0:T(8,128)(2,1)}, u32[]{:S(2)}) copy-start(bf16[512,512]{1,0:T(8,128)(2,1)} %copy-done.9) | copy-start | bytes 1572868
  139.1 6.6 %copy-start.19 = (bf16[512,512]{1,0:T(8,128)(2,1)S(1)}, bf16[512,512]{1,0:T(8,128)(2,1)}, u32[]{:S(2)}) copy-start(bf16[512,512]{1,0:T(8,128)(2,1)} %copy-done.17) | copy-start | bytes 1572868
  139.1 6.6 %copy-start.23 = (bf16[512,512]{1,0:T(8,128)(2,1)S(1)}, bf16[512,512]{1,0:T(8,128)(2,1)}, u32[]{:S(2)}) copy-start(bf16[512,512]{1,0:T(8,128)(2,1)} %copy-done.21) | copy-start | bytes 1572868
  139.1 6.6 %copy-start.30 = (bf16[256,512]{1,0:T(8,128)(2,1)S(1)}, bf16[256,512]{1,0:T(8,128)(2,1)}, u32[]{:S(2)}) copy-start(bf16[256,512]{1,0:T(8,128)(2,1)} %copy-done.29) | copy-start | bytes 786436
  139.1 6.6 %copy-start.33 = (bf16[256,512]{1,0:T(8,128)(2,1)S(1)}, bf16[256,512]{1,0:T(8,128)(2,1)}, u32[]{:S(2)}) copy-start(bf16[256,512]{1,0:T(8,128)(2,1)} %copy-done.32) | copy-start | bytes 786436
  142.9 34.7 %collective-permute-start.18 = (bf16[512,512]{1,0:T(8,128)(2,1)}, bf16[512,512]{1,0:T(8,128)(2,1)}, u32[]{:S(2)}, u32[]{:S(2)}) collective-permute-start(bf16[512,512]{1,0:T(8,128)(2,1)} %merge.7), channel_id=1, source_target_pairs={{0,16},{4,20},{8,24},{12,28},{16,0},{20,4},{24,8},{28,12},{1,17},{... | collective-permute-start | bytes 1572872 | tf_op jit(solution)/shard_map/ppermute | solution.py:19
  148.4 40.3 %collective-permute-start.17 = (bf16[512,512]{1,0:T(8,128)(2,1)}, bf16[512,512]{1,0:T(8,128)(2,1)}, u32[]{:S(2)}, u32[]{:S(2)}) collective-permute-start(bf16[512,512]{1,0:T(8,128)(2,1)} %merge.5), channel_id=1, source_target_pairs={{0,16},{4,20},{8,24},{12,28},{16,0},{20,4},{24,8},{28,12},{1,17},{... | collective-permute-start | bytes 1572872 | tf_op jit(solution)/shard_map/ppermute | solution.py:19
  148.6 1.2 copy-start.2
  149.9 1.0 copy-start.8
  153.0 3.1 %copy-start.12 = (bf16[512,512]{1,0:T(8,128)(2,1)S(1)}, bf16[512,512]{1,0:T(8,128)(2,1)}, u32[]{:S(2)}) copy-start(bf16[512,512]{1,0:T(8,128)(2,1)} %copy-done.9) | copy-start | bytes 1572868
  153.0 3.1 %copy-start.20 = (bf16[512,512]{1,0:T(8,128)(2,1)S(1)}, bf16[512,512]{1,0:T(8,128)(2,1)}, u32[]{:S(2)}) copy-start(bf16[512,512]{1,0:T(8,128)(2,1)} %copy-done.17) | copy-start | bytes 1572868
  153.0 3.1 %copy-start.24 = (bf16[512,512]{1,0:T(8,128)(2,1)S(1)}, bf16[512,512]{1,0:T(8,128)(2,1)}, u32[]{:S(2)}) copy-start(bf16[512,512]{1,0:T(8,128)(2,1)} %copy-done.21) | copy-start | bytes 1572868
  153.0 3.1 %copy-start.31 = (bf16[256,512]{1,0:T(8,128)(2,1)S(1)}, bf16[256,512]{1,0:T(8,128)(2,1)}, u32[]{:S(2)}) copy-start(bf16[256,512]{1,0:T(8,128)(2,1)} %copy-done.29) | copy-start | bytes 786436
  153.0 3.1 %copy-start.34 = (bf16[256,512]{1,0:T(8,128)(2,1)S(1)}, bf16[256,512]{1,0:T(8,128)(2,1)}, u32[]{:S(2)}) copy-start(bf16[256,512]{1,0:T(8,128)(2,1)} %copy-done.32) | copy-start | bytes 786436
  156.1 21.4 %copy-start.3 = (f32[512,512]{1,0:T(8,128)}, f32[512,512]{1,0:T(8,128)S(1)}, u32[]{:S(2)}) copy-start(f32[512,512]{1,0:T(8,128)S(1)} %merge.6) | copy-start | bytes 3145732
  158.1 30.5 %copy-start.4 = (f32[512,512]{1,0:T(8,128)}, f32[512,512]{1,0:T(8,128)S(1)}, u32[]{:S(2)}) copy-start(f32[512,512]{1,0:T(8,128)S(1)} %merge.4) | copy-start | bytes 3145732
  179.5 37.4 %copy-start.37 = (f32[512,1024]{1,0:T(8,128)S(1)}, f32[512,1024]{1,0:T(8,128)}, u32[]{:S(2)}) copy-start(f32[512,1024]{1,0:T(8,128)} %param.7) | copy-start | bytes 6291460
  194.6 1.1 collective-permute-start.19
  195.8 3.5 %collective-permute-start.20 = (f32[3]{0:T(128)S(1)}, f32[3]{0:T(128)S(1)}, u32[]{:S(2)}, u32[]{:S(2)}) collective-permute-start(f32[3]{0:T(128)S(1)} %fusion.31), channel_id=1, source_target_pairs={{0,2},{1,3},{2,0},{3,1},{4,6},{5,7},{6,4},{7,5},{8,10},{9,11},{10,... | collective-permute-start | bytes 44 | tf_op jit(solution)/shard_map/ppermute | solution.py:19
  199.4 3.5 %collective-permute-start.21 = (f32[3]{0:T(128)S(1)}, f32[3]{0:T(128)S(1)}, u32[]{:S(2)}, u32[]{:S(2)}) collective-permute-start(f32[3]{0:T(128)S(1)} %fusion.32), channel_id=1, source_target_pairs={{0,4},{4,0},{8,12},{12,8},{16,20},{20,16},{24,28},{28,24},{1,5},{5... | collective-permute-start | bytes 44 | tf_op jit(solution)/shard_map/ppermute | solution.py:19
  203.0 3.5 %collective-permute-start.22 = (f32[3]{0:T(128)S(1)}, f32[3]{0:T(128)S(1)}, u32[]{:S(2)}, u32[]{:S(2)}) collective-permute-start(f32[3]{0:T(128)S(1)} %add.182), channel_id=1, source_target_pairs={{0,8},{4,12},{8,0},{12,4},{16,24},{20,28},{24,16},{28,20},{1,9},{5... | collective-permute-start | bytes 44 | tf_op jit(solution)/shard_map/ppermute | solution.py:19
  206.5 4.4 %collective-permute-start.23 = (f32[3]{0:T(128)S(1)}, f32[3]{0:T(128)S(1)}, u32[]{:S(2)}, u32[]{:S(2)}) collective-permute-start(f32[3]{0:T(128)S(1)} %add.183), channel_id=1, source_target_pairs={{0,16},{4,20},{8,24},{12,28},{16,0},{20,4},{24,8},{28,12},{1,17},{... | collective-permute-start | bytes 44 | tf_op jit(solution)/shard_map/ppermute | solution.py:19
  (2 other events, 2.1 us)
Sparse Core Ops, SparseCore 0:
  23.7 60.4 reduce-scatter.1

commit v2 on v1

v2 whole, which is shorter than its diff:
```python
import functools
import math

import jax
import jax.numpy as jnp
from jax import lax
from jax.experimental import pallas as pl
from jax.experimental.pallas import tpu as pltpu
from jax.sharding import PartitionSpec as P

QUAD = 4
LANES = 128
VMEM_LIMIT = 18 * 2**20
FULL_VMEM = 60 * 2**20


def exchange(value, axis, mask):
    pairs = [(source, source ^ mask) for source in range(lax.axis_size(axis))]
    return lax.ppermute(value, axis, pairs)


def total_over(value, dp_bits):
    mask = 1
    while mask < lax.axis_size("tensor"):
        value = value + exchange(value, "tensor", mask)
        mask *= 2
    for bit in range(dp_bits):
        value = value + exchange(value, "dp", 2**bit)
    return value


def dot(a, b):
    return jnp.dot(a, b, preferred_element_type=jnp.float32)


def pair_sums(step, pairs, strips, rows, load, acc):
    @pl.when(step == 0)
    def _():
        acc[...] = jnp.zeros_like(acc)

    def strip(i, sums):
        at = pl.ds(pl.multiple_of(i * rows, rows), rows)
        sums = list(sums)
        for tile in load(at):
            for n, (a, b) in enumerate(pairs):
                sums[n] = sums[n] + tile[a] * tile[b]
        return tuple(sums)

    sums = lax.fori_loop(0, strips, strip, tuple(acc[n] for n in range(len(pairs))))
    for n in range(len(pairs)):
        acc[n] = sums[n]


def place_sums(place, pairs, acc, result):
    lane = lax.broadcasted_iota(jnp.int32, (1, LANES), 1)
    turn = place * (QUAD + 1)
    for n, (a, b) in enumerate(pairs):
        value = jnp.sum(jnp.sum(acc[n], axis=0, keepdims=True), axis=1, keepdims=True)
        first = jnp.bitwise_xor(QUAD * a + b, turn)
        second = jnp.bitwise_xor(QUAD * b + a, turn)
        result = jnp.where((lane == first) | (lane == second), value, result)
    return result


def lanes_of(columns):
    return [slice(c, c + LANES) for c in range(0, columns, LANES)]


NEAR_PAIRS = [(a, b) for a in range(QUAD - 1) for b in range(a, QUAD - 1)]
FAR_PAIRS = [(a, QUAD - 1) for a in range(QUAD)]


def forward_kernel(x, w, targets, top, low):
    error = (dot(x[...], w[...]) - targets[...].astype(jnp.float32)).astype(top.dtype)
    half = top.shape[0]
    top[...] = error[:half]
    low[...] = error[half:]


def forward(inputs, weight, targets):
    rows, inner = inputs.shape
    columns = weight.shape[1]
    tile = math.gcd(columns, 256)
    half = jax.ShapeDtypeStruct((rows // 2, columns), jnp.bfloat16)
    return pl.pallas_call(
        forward_kernel,
        grid=(columns // tile,),
        in_specs=[
            pl.BlockSpec((rows, inner), lambda j: (0, 0), pipeline_mode=pl.Buffered(1)),
            pl.BlockSpec((inner, tile), lambda j: (0, j)),
            pl.BlockSpec((rows, tile), lambda j: (0, j)),
        ],
        out_specs=[pl.BlockSpec((rows // 2, tile), lambda j: (0, j))] * 2,
        out_shape=[half, half],
        compiler_params=pltpu.CompilerParams(vmem_limit_bytes=FULL_VMEM),
        cost_estimate=pl.CostEstimate(
            flops=2 * rows * inner * columns, bytes_accessed=14 * 2**20, transcendentals=0
        ),
        name="forward",
    )(inputs, weight, targets)


def input_grad_kernel(w, top, low, out):
    half = top.shape[0]
    for at, error in ((0, top), (half, low)):
        out[:, at:at + half] = lax.dot_general(
            w[...], error[...], (((1,), (1,)), ((), ())), preferred_element_type=jnp.float32
        ).astype(out.dtype)


def input_grad_part(weight, top, low):
    inner, columns = weight.shape
    half = top.shape[0]
    tile = math.gcd(inner, 512)
    whole = pl.BlockSpec((half, columns), lambda j: (0, 0), pipeline_mode=pl.Buffered(1))
    return pl.pallas_call(
        input_grad_kernel,
        grid=(inner // tile,),
        in_specs=[pl.BlockSpec((tile, columns), lambda j: (j, 0)), whole, whole],
        out_specs=pl.BlockSpec((tile, 2 * half), lambda j: (j, 0)),
        out_shape=jax.ShapeDtypeStruct((inner, 2 * half), jnp.bfloat16),
        compiler_params=pltpu.CompilerParams(vmem_limit_bytes=VMEM_LIMIT),
        cost_estimate=pl.CostEstimate(
            flops=4 * inner * half * columns, bytes_accessed=14 * 2**20, transcendentals=0
        ),
        name="input_grad_part",
    )(weight, top, low)


def halves_dot(xt, top, low):
    half = top.shape[0]
    return dot(xt[:, :half], top[...]) + dot(xt[:, half:], low[...])


def near_kernel(pieces, idx, xt, own_top, own_low, y_top, y_low, z_top, z_low, *refs):
    others, (out, grads, tiles, acc) = refs[:pieces], refs[pieces:]
    step = pl.program_id(0)
    tiles[0] = halves_dot(xt, own_top, own_low)
    for q, other in enumerate(others):

        @pl.when(step == q)
        def _():
            tiles[1] = halves_dot(other.at[0], y_top, y_low)
            tiles[2] = halves_dot(other.at[1], z_top, z_low)

    def load(at):
        for lanes in lanes_of(tiles.shape[2]):
            tile = [tiles[k, at, lanes] for k in range(QUAD - 1)]
            for k in range(QUAD - 1):
                grads[k, at, lanes] = tile[k].astype(grads.dtype)
            yield tile

    pair_sums(step, NEAR_PAIRS, tiles.shape[1] // 16, 16, load, acc)

    @pl.when(step == pl.num_programs(0) - 1)
    def _():
        out[...] = place_sums(idx[0], NEAR_PAIRS, acc, jnp.zeros((1, LANES), jnp.float32))


def far_kernel(pieces, idx, before, top, low, grads, *refs):
    others, (out, last, tile, acc) = refs[:pieces], refs[pieces:]
    step = pl.program_id(0)
    for q, other in enumerate(others):

        @pl.when(step == q)
        def _():
            tile[...] = halves_dot(other.at[0], top, low)

    def load(at):
        for lanes in lanes_of(tile.shape[1]):
            mine = tile[at, lanes]
            last[at, lanes] = mine.astype(last.dtype)
            yield [grads[k, at, lanes].astype(jnp.float32) for k in range(QUAD - 1)] + [mine]

    pair_sums(step, FAR_PAIRS, tile.shape[0] // 16, 16, load, acc)

    @pl.when(step == pl.num_programs(0) - 1)
    def _():
        out[...] = place_sums(idx[0], FAR_PAIRS, acc, before[...])


def once(shape, at):
    return pl.BlockSpec(shape, lambda j, idx: at, pipeline_mode=pl.Buffered(1))


PLACE, BIT, TILE = 0, 1, 2


def near_gram(idx, xt, others, errors):
    _, width, rows = others[0].shape
    columns = errors[0].shape[1]
    steps = len(others)
    return pl.pallas_call(
        functools.partial(near_kernel, steps),
        grid_spec=pltpu.PrefetchScalarGridSpec(
            num_scalar_prefetch=1,
            grid=(steps,),
            in_specs=[pl.BlockSpec((width, rows), lambda j, idx: (idx[TILE + j], 0))]
            + [once(e.shape, (0, 0)) for e in errors]
            + [once((QUAD - 2, width, rows), (0, 0, 0))] * steps,
            out_specs=[
                pl.BlockSpec((1, LANES), lambda j, idx: (0, 0)),
                pl.BlockSpec((QUAD - 1, width, columns), lambda j, idx: (0, idx[TILE + j], 0)),
            ],
            scratch_shapes=[
                pltpu.VMEM((QUAD - 1, width, columns), jnp.float32),
                pltpu.VMEM((len(NEAR_PAIRS), 16, LANES), jnp.float32),
            ],
        ),
        out_shape=[
            jax.ShapeDtypeStruct((1, LANES), jnp.float32),
            jax.ShapeDtypeStruct((QUAD - 1, steps * width, columns), jnp.bfloat16),
        ],
        compiler_params=pltpu.CompilerParams(vmem_limit_bytes=VMEM_LIMIT),
        cost_estimate=pl.CostEstimate(
            flops=6 * steps * width * rows * columns, bytes_accessed=12 * 2**20, transcendentals=0
        ),
        name="near_gram",
    )(idx, xt, *errors, *others)


def far_gram(idx, before, others, top, low, grads):
    _, width, rows = others[0].shape
    columns = top.shape[1]
    steps = len(others)
    return pl.pallas_call(
        functools.partial(far_kernel, steps),
        grid_spec=pltpu.PrefetchScalarGridSpec(
            num_scalar_prefetch=1,
            grid=(steps,),
            in_specs=[pl.BlockSpec((1, LANES), lambda j, idx: (0, 0))]
            + [once(top.shape, (0, 0))] * 2
            + [pl.BlockSpec((QUAD - 1, width, columns), lambda j, idx: (0, idx[TILE + j], 0))]
            + [once((1, width, rows), (QUAD - 2, 0, 0))] * steps,
            out_specs=[
                pl.BlockSpec((1, LANES), lambda j, idx: (0, 0)),
                pl.BlockSpec((width, columns), lambda j, idx: (idx[TILE + j], 0)),
            ],
            scratch_shapes=[
                pltpu.VMEM((width, columns), jnp.float32),
                pltpu.VMEM((len(FAR_PAIRS), 16, LANES), jnp.float32),
            ],
        ),
        out_shape=[
            jax.ShapeDtypeStruct((1, LANES), jnp.float32),
            jax.ShapeDtypeStruct((steps * width, columns), jnp.bfloat16),
        ],
        compiler_params=pltpu.CompilerParams(vmem_limit_bytes=VMEM_LIMIT),
        cost_estimate=pl.CostEstimate(
            flops=2 * steps * width * rows * columns, bytes_accessed=8 * 2**20, transcendentals=0
        ),
        name="far_gram",
    )(idx, before, top, low, grads, *others)


def merge_factors(gram_at):
    factors = [None] * QUAD
    for a, b in ((0, 1), (2, 3)):
        cross = gram_at(a, b)
        factors[a] = 1.0 - cross / (2.0 * gram_at(a, a))
        factors[b] = 1.0 - cross / (2.0 * gram_at(b, b))

    def product(left, right):
        return sum(factors[a] * factors[b] * gram_at(a, b) for a in left for b in right)

    cross = product((0, 1), (2, 3))
    first = 1.0 - cross / (2.0 * product((0, 1), (0, 1)))
    second = 1.0 - cross / (2.0 * product((2, 3), (2, 3)))
    return [factors[0] * first, factors[1] * first, factors[2] * second, factors[3] * second]


def merge_kernel(scale, idx, sums, grads, last, out):
    turn = idx[PLACE] * (QUAD + 1)
    factors = merge_factors(lambda a, b: sums[0, jnp.bitwise_xor(QUAD * a + b, turn)])
    total = (factors[QUAD - 1] * scale) * last[...].astype(jnp.float32)
    for k in range(QUAD - 1):
        total = total + (factors[k] * scale) * grads[k].astype(jnp.float32)
    out[...] = total.astype(out.dtype)


def merge(idx, flip, sums, grads, last, scale, per_block, width, at, columns):
    steps = grads.shape[1] // (2 * width)

    def tile(j, idx):
        bit = 1 - idx[BIT] if flip else idx[BIT]
        return (2 * (j // per_block) + bit) * per_block + j % per_block

    return pl.pallas_call(
        functools.partial(merge_kernel, scale),
        grid_spec=pltpu.PrefetchScalarGridSpec(
            num_scalar_prefetch=1,
            grid=(steps,),
            in_specs=[
                pl.BlockSpec(sums.shape, lambda j, idx: (0, 0), memory_space=pltpu.SMEM),
                pl.BlockSpec((QUAD - 1, width, columns), lambda j, idx: (0, tile(j, idx), at)),
                pl.BlockSpec((width, columns), lambda j, idx: (tile(j, idx), at)),
            ],
            out_specs=pl.BlockSpec((width, columns), lambda j, idx: (j, 0)),
        ),
        out_shape=jax.ShapeDtypeStruct((steps * width, columns), jnp.bfloat16),
        compiler_params=pltpu.CompilerParams(vmem_limit_bytes=VMEM_LIMIT),
        cost_estimate=pl.CostEstimate(
            flops=2 * QUAD * steps * width * columns,
            bytes_accessed=2 * (QUAD + 1) * steps * width * columns,
            transcendentals=0,
        ),
        name="merge",
    )(idx, sums, grads, last)


def partial_kernel(first_at, before, kept, received, out, acc):
    lane = lax.broadcasted_iota(jnp.int32, (1, LANES), 1)
    rows, columns = kept.shape

    def strip(i, sums):
        at = pl.ds(pl.multiple_of(i * 16, 16), 16)
        cross, mine, theirs = sums
        for c in range(columns // LANES):
            lanes = slice(c * LANES, (c + 1) * LANES)
            a = kept[at, lanes].astype(jnp.float32)
            b = received[at, lanes].astype(jnp.float32)
            cross, mine, theirs = cross + a * b, mine + a * a, theirs + b * b
        return cross, mine, theirs

    zero = jnp.zeros((16, LANES), jnp.float32)
    sums = lax.fori_loop(0, rows // 16, strip, (zero, zero, zero))
    result = before[...]
    for place, value in zip((0, 1 + first_at[0], 2 - first_at[0]), sums):
        total = jnp.sum(jnp.sum(value, axis=0, keepdims=True), axis=1, keepdims=True)
        result = result + jnp.where(lane == place, total, 0.0)
    out[...] = result


def partial_sums(bit, before, kept, received):
    return pl.pallas_call(
        partial_kernel,
        in_specs=[pl.BlockSpec(memory_space=pltpu.SMEM)] + [pl.BlockSpec(memory_space=pltpu.VMEM)] * 3,
        out_shape=jax.ShapeDtypeStruct((1, LANES), jnp.float32),
        scratch_shapes=[pltpu.VMEM((8, LANES), jnp.float32)],
        compiler_params=pltpu.CompilerParams(vmem_limit_bytes=VMEM_LIMIT),
        cost_estimate=pl.CostEstimate(flops=6 * kept.size, bytes_accessed=6 * kept.size, transcendentals=0),
        name="partial_sums",
    )(bit.reshape(1).astype(jnp.int32), before, kept, received)


def update_kernel(bit, sums, momentum, kept_0, kept_1, received_0, received_1, out):
    half = kept_0.shape[1]
    lower = bit[0] == 0
    lower_factor = 1.0 - sums[0, 0] / (2.0 * sums[0, 1])
    upper_factor = 1.0 - sums[0, 0] / (2.0 * sums[0, 2])
    factor = jnp.where(lower, lower_factor, upper_factor)
    other = jnp.where(lower, upper_factor, lower_factor)
    for at, a, b in ((slice(0, half), kept_0, received_0), (slice(half, 2 * half), kept_1, received_1)):
        out[:, at] = 0.9 * momentum[:, at] + (
            factor * a[...].astype(jnp.float32) + other * b[...].astype(jnp.float32)
        )


def update(bit, sums, momentum, kept, received):
    rows, columns = momentum.shape
    tile = math.gcd(rows, 128)
    spec = lambda width: pl.BlockSpec((tile, width), lambda i, *_: (i, 0))
    return pl.pallas_call(
        update_kernel,
        grid_spec=pltpu.PrefetchScalarGridSpec(
            num_scalar_prefetch=1,
            grid=(rows // tile,),
            in_specs=[pl.BlockSpec(sums.shape, lambda i, *_: (0, 0), memory_space=pltpu.SMEM), spec(columns)] + [spec(columns // 2)] * 4,
            out_specs=spec(columns),
        ),
        out_shape=jax.ShapeDtypeStruct(momentum.shape, jnp.float32),
        compiler_params=pltpu.CompilerParams(vmem_limit_bytes=VMEM_LIMIT),
        cost_estimate=pl.CostEstimate(
            flops=5 * momentum.size, bytes_accessed=14 * momentum.size, transcendentals=0
        ),
        name="update",
    )(bit.reshape(1).astype(jnp.int32), sums, momentum, *kept, *received)


def body(inputs, weight, targets, momentum):
    groups = lax.axis_size("dp")
    parts = lax.axis_size("tensor")
    depth = groups.bit_length() - 1
    me = lax.axis_index("dp")
    part = lax.axis_index("tensor")
    rows, depth_width = inputs.shape
    columns = weight.shape[1]
    block = depth_width // groups
    blocks = groups // QUAD
    width = blocks * block // parts
    per_block = block // width
    place = me % QUAD

    def columns_of(at, start, size):
        first = (QUAD * (start // block) + at) * block + start % block
        return lax.dynamic_slice(inputs, (0, first), (rows, size)).T

    slabs = [columns_of(place ^ k, part * width, width) for k in range(1, QUAD)]
    slabs, ready = lax.optimization_barrier((slabs, inputs))
    arrived = [exchange(s, "dp", k + 1) for k, s in enumerate(slabs)]

    top, low = forward(ready, weight, targets)
    arrived, top, low = lax.optimization_barrier((arrived, top, low))
    y_low, z_top = exchange(low, "dp", 1), exchange(top, "dp", 2)
    y_top, z_low = exchange(top, "dp", 1), exchange(low, "dp", 2)
    others, sources = [jnp.stack(arrived)], [part]
    own = jnp.concatenate([columns_of(place, b * block, block) for b in range(blocks)])
    part_grad = input_grad_part(weight, top, low)
    mask = parts // 2
    while mask:
        if mask == 1:
            others, own, part_grad, y_top, y_low, z_top, z_low = lax.optimization_barrier(
                (others, own, part_grad, y_top, y_low, z_top, z_low)
            )
        others = others + [exchange(o, "tensor", mask) for o in others]
        sources = sources + [s ^ mask for s in sources]
        mask //= 2
    far_top, far_low = exchange(z_top, "dp", 1), exchange(y_low, "dp", 2)

    bit = me >> 2 & 1
    idx = jnp.stack([place, bit] + sources).astype(jnp.int32)
    sums, grads = near_gram(idx, own, others, (top, low, y_top, y_low, z_top, z_low))
    sums, last = far_gram(idx, sums, others, far_top, far_low, grads)
    sums = total_over(sums, 2)
    half = columns // 2

    def merged_half(flip, h):
        return merge(idx, flip, sums, grads, last, rows**-0.5, per_block, width, h, half)

    sent = [merged_half(True, h) for h in range(2)]
    received = [exchange(s, "dp", 4) for s in sent]
    kept = [merged_half(False, h) for h in range(2)]
    summed = lax.psum_scatter(part_grad, "tensor", scatter_dimension=0, tiled=True)

    for level in range(2, depth):
        if level > 2:
            lower = bit == 0
            lower_factor = 1.0 - sums[0, 0] / (2.0 * sums[0, 1])
            upper_factor = 1.0 - sums[0, 0] / (2.0 * sums[0, 2])
            factor = jnp.where(lower, lower_factor, upper_factor)
            other = jnp.where(lower, upper_factor, lower_factor)
            merged = [
                factor * a.astype(jnp.float32) + other * b.astype(jnp.float32) for a, b in zip(kept, received)
            ]
            bit = me >> level & 1
            paired = [v.reshape(v.shape[0] // (2 * block), 2, block, v.shape[1]) for v in merged]
            kept = [jnp.where(bit == 0, v[:, 0], v[:, 1]).reshape(-1, v.shape[-1]) for v in paired]
            sent = [jnp.where(bit == 0, v[:, 1], v[:, 0]).reshape(-1, v.shape[-1]) for v in paired]
            received = [exchange(s.astype(jnp.bfloat16), "dp", 2**level) for s in sent]
        sums = jnp.zeros((1, LANES), jnp.float32)
        for a, b in zip(kept, received):
            sums = partial_sums(bit, sums, a, b)
        sums = total_over(sums, level + 1)
    new_momentum = update(bit, sums, momentum, kept, received)
    return (summed, new_momentum, jnp.sqrt(sums[0, 1:3]) / depth_width)


def solution(mesh):
    return jax.shard_map(
        body,
        mesh=mesh,
        in_specs=(P("dp", None), P(None, "tensor"), P("dp", "tensor"), P("dp", "tensor")),
        out_specs=(P("tensor", "dp"), P("dp", "tensor"), P()),
        check_vma=False,
    )
```

time: 229 us -> 164 us (0.72)
  waiting for transfers between devices: 101 us -> 66 us
  Pallas kernels: 23.6 us -> 44.7 us
  matrix products: 14.8 us -> 0 us
  other arithmetic: 14.8 us -> 1.97 us
  local copies, waits for them, and re-layouts: 23.5 us -> 11.7 us
  between operations: 20.9 us -> 14.3 us
  starting transfers between devices: 28.8 us -> 25.1 us
    ppermute x24 -> x23, waiting for transfers between devices: 101 us -> 66 us  [exchange(): return lax.ppermute(value, axis, pairs)]
    pallas_call x6 -> x11, Pallas kernels: 23.6 us -> 44.7 us  [the longest x1 9.98 us: near_gram(): pl.pallas_call(functools.partial(near_kernel, steps), grid_spec=pltpu.Pre...]
    dot_general x3 -> x0, matrix products: 14.8 us -> none  [the longest x2 8.31 us: dot(): return jnp.dot(a, b, preferred_element_type=jnp.float32)]
    unnamed x88 -> x15, local copies, waits for them, and re-layouts: 17.1 us -> 8.8 us
    reduce_sum x2 -> x0, other arithmetic: 4.01 us -> none  [body(): jnp.sum(a * b.astype(jnp.float32))]
    add x3 -> x0, other arithmetic: 3.98 us -> none  [the longest x1 2.22 us: body(): factor * a + other * b.astype(jnp.float32)]
    ppermute x24 -> x23, starting transfers between devices: 28.8 us -> 25.1 us  [exchange(): return lax.ppermute(value, axis, pairs)]
    concatenate x2 -> x0, other arithmetic: 3.63 us -> none  [body(): others = jnp.concatenate([others, exchange(others, 'tensor', mask)])]
  transfers between devices with their start and end apart: 25 -> 24, of which waited for: 19 -> 17; matrix products, arithmetic and copies ran while one was open for 11% -> 3% of each run, Pallas kernels for 10% -> 27%
where the time goes in v2:
time: 164 us
  waiting for transfers between devices  66 us (40%)
  Pallas kernels  44.7 us (27%)
  starting transfers between devices  25.1 us (15%)
  between operations  14.3 us (9%)
  local copies, waits for them, and re-layouts  11.7 us (7%)
  other arithmetic  1.97 us (1%)
    ppermute x23, waiting for transfers between devices, exchange(): return lax.ppermute(value, axis, pairs)  66 us
    ppermute x23, starting transfers between devices, exchange(): return lax.ppermute(value, axis, pairs)  25.1 us
    pallas_call x1, Pallas kernels, near_gram(): pl.pallas_call(functools.partial(near_kernel, steps), grid_spec=pltpu.Pre...  9.98 us
    pallas_call x1, Pallas kernels, forward(): pl.pallas_call(forward_kernel, grid=(columns // tile,), in_specs=[pl.Bloc...  9.17 us
    unnamed x15, local copies, waits for them, and re-layouts  8.8 us
    pallas_call x4, Pallas kernels, merge(): pl.pallas_call(functools.partial(merge_kernel, scale), grid_spec=pltpu.Pr...  8.65 us
    pallas_call x1, Pallas kernels, input_grad_part(): pl.pallas_call(input_grad_kernel, grid=(inner // tile,), in_specs=[pl.Blo...  7.04 us
    pallas_call x1, Pallas kernels, far_gram(): pl.pallas_call(functools.partial(far_kernel, steps), grid_spec=pltpu.Pref...  6.07 us
  transfers between devices with their start and end apart: 24, of which 17 were waited for; matrix products, arithmetic and copies ran while one was open for 3% of the time, Pallas kernels for 27%

profile of v2, /device:TPU:0, one launch (start us, length us, event | category | flops | bytes accessed | tf_op | source)
XLA Modules:
  0.0 163.8 jit_solution(9785933127224032835)
XLA Ops:
  7.2 0.0 reduce-scatter.2.cloned.1.call-start
  7.3 1.6 constant_dynamic-slice_fusion.2
  8.9 0.1 copy.12
  9.0 0.1 copy.13
  9.1 0.1 copy.14
  9.3 3.0 %collective-permute-start = (bf16[256,512]{1,0:T(8,128)(2,1)S(1)}, bf16[256,512]{1,0:T(8,128)(2,1)S(1)}, u32[]{:S(2)}, u32[]{:S(2)}) collective-permute-start(bf16[256,512]{1,0:T(8,128)(2,1)S(1)} %bitcast.20), channel_id=1, source_target_pairs={{0,4},{4,0},{8,12},{12,8},{16,20},{20,16},{24,28},{28,24},{1,5},{5... | collective-permute-start | bytes 786440 | tf_op jit(solution)/shard_map/ppermute | solution.py:19
  12.3 1.6 collective-permute-start.1
  13.9 9.2 %forward.1 = (bf16[256,1024]{1,0:T(8,128)(2,1)}, bf16[256,1024]{1,0:T(8,128)(2,1)}) custom-call(bf16[512,4096]{1,0:T(8,128)(2,1)} %x, bf16[4096,1024]{1,0:T(8,128)(2,1)} %w.3, bf16[512,1024]{1,0:T(8,128)(2,1)} %targets.1), custom_call_target="tpu_custom_call" | custom-call | flops 4294967296 | bytes 14680064 | tf_op jit(solution)/shard_map/forward/pallas_call | solution.py:85
  23.1 2.4 %collective-permute-done.2 = bf16[256,512]{1,0:T(8,128)(2,1)S(1)} collective-permute-done((bf16[256,512]{1,0:T(8,128)(2,1)S(1)}, bf16[256,512]{1,0:T(8,128)(2,1)S(1)}, u32[]{:S(2)}, u32[]{:S(2)}) %collective-permute-start.2) | collective-permute-done | bytes 262176 | tf_op jit(solution)/shard_map/ppermute | solution.py:19
  25.5 0.1 pad_maximum_fusion.1.refs_0_
  25.6 1.7 %collective-permute-start.3 = (bf16[3,256,512]{2,1,0:T(8,128)(2,1)S(1)}, bf16[3,256,512]{2,1,0:T(8,128)(2,1)S(1)}, u32[]{:S(2)}, u32[]{:S(2)}) collective-permute-start(bf16[3,256,512]{2,1,0:T(8,128)(2,1)S(1)} %pad_maximum_fusion.1.refs_0_), channel_id=1, source_target_pairs={{0,2},{1,3},{2,0},{3,1},{4,6},{5,7},{6,4},{7,5},{8,10},{9,11},{10,... | collective-permute-start | bytes 2359304 | tf_op jit(solution)/shard_map/ppermute | solution.py:19
  27.3 1.3 constant_dynamic-slice_fusion.1
  28.5 1.0 copy.16
  29.5 1.0 copy.15
  30.5 1.5 collective-permute-start.4
  32.1 1.6 collective-permute-start.6
  33.7 0.5 collective-permute-start.5
  34.1 0.5 collective-permute-start.7
  34.6 1.3 pad_maximum_fusion.xt
  35.9 3.4 %copy-done.2 = bf16[4096,1024]{1,0:T(8,128)(2,1)S(1)} copy-done((bf16[4096,1024]{1,0:T(8,128)(2,1)S(1)}, bf16[4096,1024]{1,0:T(8,128)(2,1)}, u32[]{:S(2)}) %copy-start.2) | copy-done | bytes 8388632
  39.3 7.0 %input_grad_part.1 = bf16[4096,512]{1,0:T(8,128)(2,1)S(1)} custom-call(bf16[4096,1024]{1,0:T(8,128)(2,1)S(1)} %copy-done.2, bf16[256,1024]{1,0:T(8,128)(2,1)S(1)} %copy-done.3, bf16[256,1024]{1,0:T(8,128)(2,1)} %get-tuple-element.36.low.own_low), custom_call_target="tpu_custom_call" | custom-call | flops 4294967296 | bytes 14680064 | tf_op jit(solution)/shard_map/input_grad_part/pallas_call | solution.py:116
  46.3 1.9 %copy-done = bf16[4096,512]{1,0:T(8,128)(2,1)} copy-done((bf16[4096,512]{1,0:T(8,128)(2,1)}, bf16[4096,512]{1,0:T(8,128)(2,1)S(1)}, u32[]{:S(2)}) %copy-start) | copy-done | bytes 4194328
  48.3 5.8 %collective-permute-done.5.y_low = bf16[256,1024]{1,0:T(8,128)(2,1)} collective-permute-done((bf16[256,1024]{1,0:T(8,128)(2,1)}, bf16[256,1024]{1,0:T(8,128)(2,1)}, u32[]{:S(2)}, u32[]{:S(2)}) %collective-permute-start.5) | collective-permute-done | bytes 524320 | tf_op jit(solution)/shard_map/ppermute | solution.py:19
  54.0 1.2 collective-permute-done.7.z_low
  55.3 0.1 collective-permute-start.8
  55.4 0.5 collective-permute-start.9
  55.9 0.5 collective-permute-start.10
  56.4 1.6 collective-permute-start.11
  57.9 0.1 stack.40.idx
  58.0 0.9 collective-permute-done.9.refs_3_
  58.9 1.0 copy-done.4
  59.9 10.0 %near_gram.1 = (f32[1,128]{1,0:T(1,128)S(1)}, bf16[3,1024,1024]{2,1,0:T(8,128)(2,1)S(1)}) custom-call(s32[6]{0:T(128)S(1)} %stack.40.idx, bf16[1024,512]{1,0:T(8,128)(2,1)S(1)} %pad_maximum_fusion.xt, bf16[256,1024]{1,0:T(8,128)(2,1)S(1)} %copy-done.4, bf16[256,1024]{1,0:T(8,128)(2,1)} %get-tuple-element.36.low.own_low, ...), custom_call_target="tpu_custom_call" | custom-call | flops 3221225472 | bytes 12582912 | tf_op jit(solution)/shard_map/near_gram/pallas_call | solution.py:193
  69.9 0.2 collective-permute-done.10.top
  70.1 0.2 collective-permute-done.11.low
  70.3 6.1 %far_gram.1 = (f32[1,128]{1,0:T(1,128)S(1)}, bf16[1024,1024]{1,0:T(8,128)(2,1)S(1)}) custom-call(s32[6]{0:T(128)S(1)} %stack.40.idx, f32[1,128]{1,0:T(1,128)S(1)} %get-tuple-element.45.before, bf16[256,1024]{1,0:T(8,128)(2,1)} %collective-permute-done.10.top, bf16[256,1024]{1,0:T(8,128)(2,1)} %collective-permute-done.11.low, ...), custom_call_target="tpu_custom_call" | custom-call | flops 1073741824 | bytes 8388608 | tf_op jit(solution)/shard_map/far_gram/pallas_call | solution.py:226
  76.4 0.0 collective-permute-start.12
  76.5 1.1 collective-permute-done.12
  77.6 0.9 collective-permute-start.13
  78.4 2.7 %collective-permute-done.13 = f32[1,128]{1,0:T(1,128)S(1)} collective-permute-done((f32[1,128]{1,0:T(1,128)S(1)}, f32[1,128]{1,0:T(1,128)S(1)}, u32[]{:S(2)}, u32[]{:S(2)}) %collective-permute-start.13) | collective-permute-done | bytes 544 | tf_op jit(solution)/shard_map/ppermute | solution.py:19
  81.1 1.5 collective-permute-start.14
  82.6 2.0 %collective-permute-done.14 = f32[1,128]{1,0:T(1,128)S(1)} collective-permute-done((f32[1,128]{1,0:T(1,128)S(1)}, f32[1,128]{1,0:T(1,128)S(1)}, u32[]{:S(2)}, u32[]{:S(2)}) %collective-permute-start.14) | collective-permute-done | bytes 544 | tf_op jit(solution)/shard_map/ppermute | solution.py:19
  84.7 1.6 collective-permute-start.15
  86.2 2.0 %collective-permute-done.15 = f32[1,128]{1,0:T(1,128)S(1)} collective-permute-done((f32[1,128]{1,0:T(1,128)S(1)}, f32[1,128]{1,0:T(1,128)S(1)}, u32[]{:S(2)}, u32[]{:S(2)}) %collective-permute-start.15) | collective-permute-done | bytes 544 | tf_op jit(solution)/shard_map/ppermute | solution.py:19
  88.2 2.2 %merge.5 = bf16[512,512]{1,0:T(8,128)(2,1)S(1)} custom-call(s32[6]{0:T(128)S(1)} %stack.40.idx, f32[1,128]{1,0:T(1,128)S(1)} %add.92.sums, bf16[3,1024,1024]{2,1,0:T(8,128)(2,1)S(1)} %get-tuple-element.46.grads, bf16[1024,1024]{1,0:T(8,128)(2,1)S(1)} %get-tuple-element.48.last), custom_call_target="tpu_custom_call" | custom-call | flops 2097152 | bytes 2621440 | tf_op jit(solution)/shard_map/merge/pallas_call | solution.py:288
  90.4 2.6 %collective-permute-start.16 = (bf16[512,512]{1,0:T(8,128)(2,1)S(1)}, bf16[512,512]{1,0:T(8,128)(2,1)S(1)}, u32[]{:S(2)}, u32[]{:S(2)}) collective-permute-start(bf16[512,512]{1,0:T(8,128)(2,1)S(1)} %merge.5), channel_id=1, source_target_pairs={{0,16},{4,20},{8,24},{12,28},{16,0},{20,4},{24,8},{28,12},{1,17},{... | collective-permute-start | bytes 1572872 | tf_op jit(solution)/shard_map/ppermute | solution.py:19
  93.0 2.2 %merge.7 = bf16[512,512]{1,0:T(8,128)(2,1)S(1)} custom-call(s32[6]{0:T(128)S(1)} %stack.40.idx, f32[1,128]{1,0:T(1,128)S(1)} %add.92.sums, bf16[3,1024,1024]{2,1,0:T(8,128)(2,1)S(1)} %get-tuple-element.46.grads, bf16[1024,1024]{1,0:T(8,128)(2,1)S(1)} %get-tuple-element.48.last), custom_call_target="tpu_custom_call" | custom-call | flops 2097152 | bytes 2621440 | tf_op jit(solution)/shard_map/merge/pallas_call | solution.py:288
  95.2 0.4 collective-permute-start.17
  95.6 2.2 %merge.4.kept.kept_0 = bf16[512,512]{1,0:T(8,128)(2,1)S(1)} custom-call(s32[6]{0:T(128)S(1)} %stack.40.idx, f32[1,128]{1,0:T(1,128)S(1)} %add.92.sums, bf16[3,1024,1024]{2,1,0:T(8,128)(2,1)S(1)} %get-tuple-element.46.grads, bf16[1024,1024]{1,0:T(8,128)(2,1)S(1)} %get-tuple-element.48.last), custom_call_target="tpu_custom_call" | custom-call | flops 2097152 | bytes 2621440 | tf_op jit(solution)/shard_map/merge/pallas_call | solution.py:288
  97.8 2.2 %merge.6.kept.kept_1 = bf16[512,512]{1,0:T(8,128)(2,1)S(1)} custom-call(s32[6]{0:T(128)S(1)} %stack.40.idx, f32[1,128]{1,0:T(1,128)S(1)} %add.92.sums, bf16[3,1024,1024]{2,1,0:T(8,128)(2,1)S(1)} %get-tuple-element.46.grads, bf16[1024,1024]{1,0:T(8,128)(2,1)S(1)} %get-tuple-element.48.last), custom_call_target="tpu_custom_call" | custom-call | flops 2097152 | bytes 2621440 | tf_op jit(solution)/shard_map/merge/pallas_call | solution.py:288
  100.0 26.8 %collective-permute-done.16.received.received_0 = bf16[512,512]{1,0:T(8,128)(2,1)S(1)} collective-permute-done((bf16[512,512]{1,0:T(8,128)(2,1)S(1)}, bf16[512,512]{1,0:T(8,128)(2,1)S(1)}, u32[]{:S(2)}, u32[]{:S(2)}) %collective-permute-start.16) | collective-permute-done | bytes 524320 | tf_op jit(solution)/shard_map/ppermute | solution.py:19
  126.7 0.5 partial_sums.2.before
  127.2 9.6 %collective-permute-done.17.received.received_1 = bf16[512,512]{1,0:T(8,128)(2,1)S(1)} collective-permute-done((bf16[512,512]{1,0:T(8,128)(2,1)S(1)}, bf16[512,512]{1,0:T(8,128)(2,1)S(1)}, u32[]{:S(2)}, u32[]{:S(2)}) %collective-permute-start.17) | collective-permute-done | bytes 524320 | tf_op jit(solution)/shard_map/ppermute | solution.py:19
  136.8 0.5 partial_sums.3
  137.3 1.1 collective-permute-done.18
  138.4 0.9 collective-permute-start.19
  139.3 2.7 %collective-permute-done.19 = f32[1,128]{1,0:T(1,128)S(1)} collective-permute-done((f32[1,128]{1,0:T(1,128)S(1)}, f32[1,128]{1,0:T(1,128)S(1)}, u32[]{:S(2)}, u32[]{:S(2)}) %collective-permute-start.19) | collective-permute-done | bytes 544 | tf_op jit(solution)/shard_map/ppermute | solution.py:19
  142.0 1.5 collective-permute-start.20
  143.5 2.0 %collective-permute-done.20 = f32[1,128]{1,0:T(1,128)S(1)} collective-permute-done((f32[1,128]{1,0:T(1,128)S(1)}, f32[1,128]{1,0:T(1,128)S(1)}, u32[]{:S(2)}, u32[]{:S(2)}) %collective-permute-start.20) | collective-permute-done | bytes 544 | tf_op jit(solution)/shard_map/ppermute | solution.py:19
  145.5 0.7 collective-permute-start.21
  146.2 2.9 %collective-permute-done.21 = f32[1,128]{1,0:T(1,128)S(1)} collective-permute-done((f32[1,128]{1,0:T(1,128)S(1)}, f32[1,128]{1,0:T(1,128)S(1)}, u32[]{:S(2)}, u32[]{:S(2)}) %collective-permute-start.21) | collective-permute-done | bytes 544 | tf_op jit(solution)/shard_map/ppermute | solution.py:19
  149.1 2.0 %collective-permute-start.22 = (f32[1,128]{1,0:T(1,128)S(1)}, f32[1,128]{1,0:T(1,128)S(1)}, u32[]{:S(2)}, u32[]{:S(2)}) collective-permute-start(f32[1,128]{1,0:T(1,128)S(1)} %add.96), channel_id=1, source_target_pairs={{0,16},{4,20},{8,24},{12,28},{16,0},{20,4},{24,8},{28,12},{1,17},{... | collective-permute-start | bytes 1544 | tf_op jit(solution)/shard_map/ppermute | solution.py:19
  151.1 2.4 %collective-permute-done.22 = f32[1,128]{1,0:T(1,128)S(1)} collective-permute-done((f32[1,128]{1,0:T(1,128)S(1)}, f32[1,128]{1,0:T(1,128)S(1)}, u32[]{:S(2)}, u32[]{:S(2)}) %collective-permute-start.22) | collective-permute-done | bytes 544 | tf_op jit(solution)/shard_map/ppermute | solution.py:19
  153.5 2.8 %update.1 = f32[512,1024]{1,0:T(8,128)} custom-call(s32[1]{0:T(128)} %bitcast.8.first_at.bit, f32[1,128]{1,0:T(1,128)S(1)} %add.97.sums, f32[512,1024]{1,0:T(8,128)S(1)} %copy-done.1, bf16[512,512]{1,0:T(8,128)(2,1)S(1)} %merge.4.kept.kept_0, bf16[512,512]{1,0:T(8,128)(2,1)S(1)} %merge.6.kept.kept_1, ...), custom_call_target="tpu_custom_call" | custom-call | flops 2621440 | bytes 7340032 | tf_op jit(solution)/shard_map/update/pallas_call | solution.py:363
  156.3 0.6 multiply_bitcast_fusion
  (27 shorter events, 0.1 us)
Async XLA Ops:
  7.2 149.8 %reduce-scatter.2.cloned.1.call-start = ((), (), s32[]{:S(2)}) async-start(), calls=%async_computation.1 | async-start | bytes 5242880 | tf_op jit(solution)/shard_map/reduce_scatter | solution.py:433
  9.3 13.8 %collective-permute-start = (bf16[256,512]{1,0:T(8,128)(2,1)S(1)}, bf16[256,512]{1,0:T(8,128)(2,1)S(1)}, u32[]{:S(2)}, u32[]{:S(2)}) collective-permute-start(bf16[256,512]{1,0:T(8,128)(2,1)S(1)} %bitcast.20), channel_id=1, source_target_pairs={{0,4},{4,0},{8,12},{12,8},{16,20},{20,16},{24,28},{28,24},{1,5},{5... | collective-permute-start | bytes 786440 | tf_op jit(solution)/shard_map/ppermute | solution.py:19
  12.3 10.8 %collective-permute-start.1 = (bf16[256,512]{1,0:T(8,128)(2,1)S(1)}, bf16[256,512]{1,0:T(8,128)(2,1)S(1)}, u32[]{:S(2)}, u32[]{:S(2)}) collective-permute-start(bf16[256,512]{1,0:T(8,128)(2,1)S(1)} %bitcast.19), channel_id=1, source_target_pairs={{0,8},{4,12},{8,0},{12,4},{16,24},{20,28},{24,16},{28,20},{1,9},{5... | collective-permute-start | bytes 786440 | tf_op jit(solution)/shard_map/ppermute | solution.py:19
  13.9 11.6 %collective-permute-start.2 = (bf16[256,512]{1,0:T(8,128)(2,1)S(1)}, bf16[256,512]{1,0:T(8,128)(2,1)S(1)}, u32[]{:S(2)}, u32[]{:S(2)}) collective-permute-start(bf16[256,512]{1,0:T(8,128)(2,1)S(1)} %bitcast.18), channel_id=1, source_target_pairs={{0,12},{4,8},{8,4},{12,0},{16,28},{20,24},{24,20},{28,16},{1,13},{... | collective-permute-start | bytes 786440 | tf_op jit(solution)/shard_map/ppermute | solution.py:19
  23.1 7.5 %copy-start.3 = (bf16[256,1024]{1,0:T(8,128)(2,1)S(1)}, bf16[256,1024]{1,0:T(8,128)(2,1)}, u32[]{:S(2)}) copy-start(bf16[256,1024]{1,0:T(8,128)(2,1)} %get-tuple-element.35.top.own_top) | copy-start | bytes 1572868
  25.6 29.7 %collective-permute-start.3 = (bf16[3,256,512]{2,1,0:T(8,128)(2,1)S(1)}, bf16[3,256,512]{2,1,0:T(8,128)(2,1)S(1)}, u32[]{:S(2)}, u32[]{:S(2)}) collective-permute-start(bf16[3,256,512]{2,1,0:T(8,128)(2,1)S(1)} %pad_maximum_fusion.1.refs_0_), channel_id=1, source_target_pairs={{0,2},{1,3},{2,0},{3,1},{4,6},{5,7},{6,4},{7,5},{8,10},{9,11},{10,... | collective-permute-start | bytes 2359304 | tf_op jit(solution)/shard_map/ppermute | solution.py:19
  30.5 17.7 %collective-permute-start.4 = (bf16[256,1024]{1,0:T(8,128)(2,1)S(1)}, bf16[256,1024]{1,0:T(8,128)(2,1)}, u32[]{:S(2)}, u32[]{:S(2)}) collective-permute-start(bf16[256,1024]{1,0:T(8,128)(2,1)S(1)} %copy-done.3), channel_id=1, source_target_pairs={{0,4},{4,0},{8,12},{12,8},{16,20},{20,16},{24,28},{28,24},{1,5},{5... | collective-permute-start | bytes 1572872 | tf_op jit(solution)/shard_map/ppermute | solution.py:19
  32.1 22.0 %collective-permute-start.6 = (bf16[256,1024]{1,0:T(8,128)(2,1)S(1)}, bf16[256,1024]{1,0:T(8,128)(2,1)}, u32[]{:S(2)}, u32[]{:S(2)}) collective-permute-start(bf16[256,1024]{1,0:T(8,128)(2,1)S(1)} %copy-done.3), channel_id=1, source_target_pairs={{0,8},{4,12},{8,0},{12,4},{16,24},{20,28},{24,16},{28,20},{1,9},{5... | collective-permute-start | bytes 1572872 | tf_op jit(solution)/shard_map/ppermute | solution.py:19
  33.7 20.4 %collective-permute-start.5 = (bf16[256,1024]{1,0:T(8,128)(2,1)}, bf16[256,1024]{1,0:T(8,128)(2,1)}, u32[]{:S(2)}, u32[]{:S(2)}) collective-permute-start(bf16[256,1024]{1,0:T(8,128)(2,1)} %get-tuple-element.36.low.own_low), channel_id=1, source_target_pairs={{0,4},{4,0},{8,12},{12,8},{16,20},{20,16},{24,28},{28,24},{1,5},{5... | collective-permute-start | bytes 1572872 | tf_op jit(solution)/shard_map/ppermute | solution.py:19
  34.1 21.1 %collective-permute-start.7 = (bf16[256,1024]{1,0:T(8,128)(2,1)}, bf16[256,1024]{1,0:T(8,128)(2,1)}, u32[]{:S(2)}, u32[]{:S(2)}) collective-permute-start(bf16[256,1024]{1,0:T(8,128)(2,1)} %get-tuple-element.36.low.own_low), channel_id=1, source_target_pairs={{0,8},{4,12},{8,0},{12,4},{16,24},{20,28},{24,16},{28,20},{1,9},{5... | collective-permute-start | bytes 1572872 | tf_op jit(solution)/shard_map/ppermute | solution.py:19
  35.9 3.4 %copy-start.2 = (bf16[4096,1024]{1,0:T(8,128)(2,1)S(1)}, bf16[4096,1024]{1,0:T(8,128)(2,1)}, u32[]{:S(2)}) copy-start(bf16[4096,1024]{1,0:T(8,128)(2,1)} %w.3) | copy-start | bytes 25165828
  46.3 2.0 %copy-start = (bf16[4096,512]{1,0:T(8,128)(2,1)}, bf16[4096,512]{1,0:T(8,128)(2,1)S(1)}, u32[]{:S(2)}) copy-start(bf16[4096,512]{1,0:T(8,128)(2,1)S(1)} %input_grad_part.1) | copy-start | bytes 12582916
  55.3 2.7 %collective-permute-start.8 = (bf16[3,256,512]{2,1,0:T(8,128)(2,1)S(1)}, bf16[3,256,512]{2,1,0:T(8,128)(2,1)S(1)}, u32[]{:S(2)}, u32[]{:S(2)}) collective-permute-start(bf16[3,256,512]{2,1,0:T(8,128)(2,1)S(1)} %pad_maximum_fusion.1.refs_0_), channel_id=1, source_target_pairs={{0,1},{1,0},{2,3},{3,2},{4,5},{5,4},{6,7},{7,6},{8,9},{9,8},{10,11... | collective-permute-start | bytes 2359304 | tf_op jit(solution)/shard_map/ppermute | solution.py:19
  55.4 3.5 %collective-permute-start.9 = (bf16[3,256,512]{2,1,0:T(8,128)(2,1)S(1)}, bf16[3,256,512]{2,1,0:T(8,128)(2,1)}, u32[]{:S(2)}, u32[]{:S(2)}) collective-permute-start(bf16[3,256,512]{2,1,0:T(8,128)(2,1)S(1)} %collective-permute-done.3.refs_1_), channel_id=1, source_target_pairs={{0,1},{1,0},{2,3},{3,2},{4,5},{5,4},{6,7},{7,6},{8,9},{9,8},{10,11... | collective-permute-start | bytes 2359304 | tf_op jit(solution)/shard_map/ppermute | solution.py:19
  55.9 14.2 %collective-permute-start.10 = (bf16[256,1024]{1,0:T(8,128)(2,1)}, bf16[256,1024]{1,0:T(8,128)(2,1)}, u32[]{:S(2)}, u32[]{:S(2)}) collective-permute-start(bf16[256,1024]{1,0:T(8,128)(2,1)} %collective-permute-done.6.z_top), channel_id=1, source_target_pairs={{0,4},{4,0},{8,12},{12,8},{16,20},{20,16},{24,28},{28,24},{1,5},{5... | collective-permute-start | bytes 1572872 | tf_op jit(solution)/shard_map/ppermute | solution.py:19
  56.4 13.9 %collective-permute-start.11 = (bf16[256,1024]{1,0:T(8,128)(2,1)}, bf16[256,1024]{1,0:T(8,128)(2,1)}, u32[]{:S(2)}, u32[]{:S(2)}) collective-permute-start(bf16[256,1024]{1,0:T(8,128)(2,1)} %collective-permute-done.5.y_low), channel_id=1, source_target_pairs={{0,8},{4,12},{8,0},{12,4},{16,24},{20,28},{24,16},{28,20},{1,9},{5... | collective-permute-start | bytes 1572872 | tf_op jit(solution)/shard_map/ppermute | solution.py:19
  58.9 1.0 copy-start.4
  76.4 1.2 collective-permute-start.12
  77.6 3.5 %collective-permute-start.13 = (f32[1,128]{1,0:T(1,128)S(1)}, f32[1,128]{1,0:T(1,128)S(1)}, u32[]{:S(2)}, u32[]{:S(2)}) collective-permute-start(f32[1,128]{1,0:T(1,128)S(1)} %add.89), channel_id=1, source_target_pairs={{0,2},{1,3},{2,0},{3,1},{4,6},{5,7},{6,4},{7,5},{8,10},{9,11},{10,... | collective-permute-start | bytes 1544 | tf_op jit(solution)/shard_map/ppermute | solution.py:19
  81.1 3.5 %collective-permute-start.14 = (f32[1,128]{1,0:T(1,128)S(1)}, f32[1,128]{1,0:T(1,128)S(1)}, u32[]{:S(2)}, u32[]{:S(2)}) collective-permute-start(f32[1,128]{1,0:T(1,128)S(1)} %add.90), channel_id=1, source_target_pairs={{0,4},{4,0},{8,12},{12,8},{16,20},{20,16},{24,28},{28,24},{1,5},{5... | collective-permute-start | bytes 1544 | tf_op jit(solution)/shard_map/ppermute | solution.py:19
  84.7 3.5 %collective-permute-start.15 = (f32[1,128]{1,0:T(1,128)S(1)}, f32[1,128]{1,0:T(1,128)S(1)}, u32[]{:S(2)}, u32[]{:S(2)}) collective-permute-start(f32[1,128]{1,0:T(1,128)S(1)} %add.91), channel_id=1, source_target_pairs={{0,8},{4,12},{8,0},{12,4},{16,24},{20,28},{24,16},{28,20},{1,9},{5... | collective-permute-start | bytes 1544 | tf_op jit(solution)/shard_map/ppermute | solution.py:19
  90.4 36.4 %collective-permute-start.16 = (bf16[512,512]{1,0:T(8,128)(2,1)S(1)}, bf16[512,512]{1,0:T(8,128)(2,1)S(1)}, u32[]{:S(2)}, u32[]{:S(2)}) collective-permute-start(bf16[512,512]{1,0:T(8,128)(2,1)S(1)} %merge.5), channel_id=1, source_target_pairs={{0,16},{4,20},{8,24},{12,28},{16,0},{20,4},{24,8},{28,12},{1,17},{... | collective-permute-start | bytes 1572872 | tf_op jit(solution)/shard_map/ppermute | solution.py:19
  95.2 41.6 %collective-permute-start.17 = (bf16[512,512]{1,0:T(8,128)(2,1)S(1)}, bf16[512,512]{1,0:T(8,128)(2,1)S(1)}, u32[]{:S(2)}, u32[]{:S(2)}) collective-permute-start(bf16[512,512]{1,0:T(8,128)(2,1)S(1)} %merge.7), channel_id=1, source_target_pairs={{0,16},{4,20},{8,24},{12,28},{16,0},{20,4},{24,8},{28,12},{1,17},{... | collective-permute-start | bytes 1572872 | tf_op jit(solution)/shard_map/ppermute | solution.py:19
  97.8 55.8 %copy-start.1 = (f32[512,1024]{1,0:T(8,128)S(1)}, f32[512,1024]{1,0:T(8,128)}, u32[]{:S(2)}) copy-start(f32[512,1024]{1,0:T(8,128)} %momentum.1) | copy-start | bytes 6291460
  137.3 1.1 collective-permute-start.18
  138.4 3.5 %collective-permute-start.19 = (f32[1,128]{1,0:T(1,128)S(1)}, f32[1,128]{1,0:T(1,128)S(1)}, u32[]{:S(2)}, u32[]{:S(2)}) collective-permute-start(f32[1,128]{1,0:T(1,128)S(1)} %add.93), channel_id=1, source_target_pairs={{0,2},{1,3},{2,0},{3,1},{4,6},{5,7},{6,4},{7,5},{8,10},{9,11},{10,... | collective-permute-start | bytes 1544 | tf_op jit(solution)/shard_map/ppermute | solution.py:19
  142.0 3.5 %collective-permute-start.20 = (f32[1,128]{1,0:T(1,128)S(1)}, f32[1,128]{1,0:T(1,128)S(1)}, u32[]{:S(2)}, u32[]{:S(2)}) collective-permute-start(f32[1,128]{1,0:T(1,128)S(1)} %add.94), channel_id=1, source_target_pairs={{0,4},{4,0},{8,12},{12,8},{16,20},{20,16},{24,28},{28,24},{1,5},{5... | collective-permute-start | bytes 1544 | tf_op jit(solution)/shard_map/ppermute | solution.py:19
  145.5 3.5 %collective-permute-start.21 = (f32[1,128]{1,0:T(1,128)S(1)}, f32[1,128]{1,0:T(1,128)S(1)}, u32[]{:S(2)}, u32[]{:S(2)}) collective-permute-start(f32[1,128]{1,0:T(1,128)S(1)} %add.95), channel_id=1, source_target_pairs={{0,8},{4,12},{8,0},{12,4},{16,24},{20,28},{24,16},{28,20},{1,9},{5... | collective-permute-start | bytes 1544 | tf_op jit(solution)/shard_map/ppermute | solution.py:19
  149.1 4.4 %collective-permute-start.22 = (f32[1,128]{1,0:T(1,128)S(1)}, f32[1,128]{1,0:T(1,128)S(1)}, u32[]{:S(2)}, u32[]{:S(2)}) collective-permute-start(f32[1,128]{1,0:T(1,128)S(1)} %add.96), channel_id=1, source_target_pairs={{0,16},{4,20},{8,24},{12,28},{16,0},{20,4},{24,8},{28,12},{1,17},{... | collective-permute-start | bytes 1544 | tf_op jit(solution)/shard_map/ppermute | solution.py:19
Sparse Core Ops, SparseCore 0:
  55.4 43.9 reduce-scatter.1

commit v3 on v2

v3 whole, which is shorter than its diff:
```python
import functools
import math

import jax
import jax.numpy as jnp
from jax import lax
from jax.experimental import pallas as pl
from jax.experimental.pallas import tpu as pltpu
from jax.sharding import PartitionSpec as P

QUAD = 4
LANES = 128
SMALL = pl.CostEstimate(flops=1, bytes_accessed=1, transcendentals=0)
VMEM_LIMIT = 18 * 2**20
FULL_VMEM = 44 * 2**20


def in_hbm(value):
    return pltpu.with_memory_space_constraint(value, pltpu.HBM)


def exchange(value, axis, mask):
    pairs = [(source, source ^ mask) for source in range(lax.axis_size(axis))]
    return lax.ppermute(value, axis, pairs)


def total_over(value, dp_bits):
    mask = 1
    while mask < lax.axis_size("tensor"):
        value = value + exchange(value, "tensor", mask)
        mask *= 2
    for bit in range(dp_bits):
        value = value + exchange(value, "dp", 2**bit)
    return value


def dot(a, b):
    return jnp.dot(a, b, preferred_element_type=jnp.float32)


def pair_sums(pairs, strips, rows, load, acc):
    def strip(i, sums):
        sums = list(sums)
        for tile in load(i * rows):
            for n, (a, b) in enumerate(pairs):
                sums[n] = sums[n] + tile[a] * tile[b]
        return tuple(sums)

    sums = lax.fori_loop(0, strips, strip, tuple(acc[n] for n in range(len(pairs))))
    for n in range(len(pairs)):
        acc[n] = sums[n]


def place_sums(place, pairs, acc, result):
    lane = lax.broadcasted_iota(jnp.int32, (1, LANES), 1)
    turn = place * (QUAD + 1)
    for n, (a, b) in enumerate(pairs):
        value = jnp.sum(jnp.sum(acc[n], axis=0, keepdims=True), axis=1, keepdims=True)
        first = jnp.bitwise_xor(QUAD * a + b, turn)
        second = jnp.bitwise_xor(QUAD * b + a, turn)
        result = jnp.where((lane == first) | (lane == second), value, result)
    return result


def lanes_of(columns):
    return [slice(c, c + LANES) for c in range(0, columns, LANES)]


NEAR_PAIRS = [(0, 1), (0, 2), (1, 1), (1, 2), (2, 2)]
FAR_PAIRS = [(a, QUAD - 1) for a in range(QUAD)]


def forward_kernel(x, w, targets, out):
    out[...] = (dot(x[...], w[...]) - targets[...].astype(jnp.float32)).astype(out.dtype)


def forward(inputs, weight, targets, part, parts):
    rows, inner = inputs.shape
    columns = weight.shape[1] // parts
    tile = math.gcd(columns, 256)
    first = part * columns // tile
    return pl.pallas_call(
        forward_kernel,
        grid=(columns // tile,),
        in_specs=[
            pl.BlockSpec((rows, inner), lambda j: (0, 0), pipeline_mode=pl.Buffered(1)),
            pl.BlockSpec((inner, tile), lambda j: (0, first + j)),
            pl.BlockSpec((rows, tile), lambda j: (0, first + j)),
        ],
        out_specs=pl.BlockSpec((rows, tile), lambda j: (0, j)),
        out_shape=jax.ShapeDtypeStruct((rows, columns), jnp.bfloat16),
        compiler_params=pltpu.CompilerParams(vmem_limit_bytes=FULL_VMEM),
        cost_estimate=SMALL,
        name="forward",
    )(inputs, weight, targets)


def input_grad_kernel(w, left, right, out):
    half = left.shape[1]
    total = 0.0
    for at, error in ((0, left), (half, right)):
        total = total + lax.dot_general(
            w[:, at:at + half], error[...], (((1,), (1,)), ((), ())), preferred_element_type=jnp.float32
        )
    out[...] = total.astype(out.dtype)


def input_grad_part(weight, left, right):
    inner, columns = weight.shape
    rows = left.shape[0]
    tile = math.gcd(inner, 1024)
    whole = pl.BlockSpec(left.shape, lambda j: (0, 0), pipeline_mode=pl.Buffered(1))
    return pl.pallas_call(
        input_grad_kernel,
        grid=(inner // tile,),
        in_specs=[pl.BlockSpec((tile, columns), lambda j: (j, 0)), whole, whole],
        out_specs=pl.BlockSpec((tile, rows), lambda j: (j, 0)),
        out_shape=pltpu.HBM((inner, rows), jnp.bfloat16),
        compiler_params=pltpu.CompilerParams(vmem_limit_bytes=FULL_VMEM),
        cost_estimate=SMALL,
        name="input_grad_part",
    )(weight, left, right)


def fill(tile, xt, left, right):
    half = left.shape[1]
    tile[:, :half] = dot(xt, left[...])
    tile[:, half:] = dot(xt, right[...])


STRIP = 16


def strip_at(first):
    return pl.ds(pl.multiple_of(first, STRIP), STRIP)


def own_kernel(idx, x, left, right, out, grads, tile, acc):
    step = pl.program_id(0)
    half = left.shape[1]

    @pl.when(step == 0)
    def _():
        acc[...] = jnp.zeros_like(acc)

    for at, error in ((0, left), (half, right)):
        tile[:, at:at + half] = lax.dot_general(
            x[...], error[...], (((0,), (0,)), ((), ())), preferred_element_type=jnp.float32
        )

    def load(first):
        at = strip_at(first)
        for lanes in lanes_of(tile.shape[1]):
            mine = tile[at, lanes]
            grads[at, lanes] = mine.astype(grads.dtype)
            yield [mine]

    pair_sums([(0, 0)], tile.shape[0] // STRIP, STRIP, load, acc)

    @pl.when(step == pl.num_programs(0) - 1)
    def _():
        out[...] = place_sums(idx[PLACE], [(0, 0)], acc, jnp.zeros((1, LANES), jnp.float32))


def own_gram(idx, inputs, left, right, width, block):
    rows, inner = inputs.shape
    columns = 2 * left.shape[1]
    steps = inner // (QUAD * width)
    per_block = block // width

    def tile(j, idx):
        return (QUAD * (j // per_block) + idx[PLACE]) * per_block + j % per_block

    return pl.pallas_call(
        own_kernel,
        grid_spec=pltpu.PrefetchScalarGridSpec(
            num_scalar_prefetch=1,
            grid=(steps,),
            in_specs=[pl.BlockSpec((rows, width), lambda j, idx: (0, tile(j, idx)))]
            + [once(left.shape, (0, 0))] * 2,
            out_specs=[
                pl.BlockSpec((1, LANES), lambda j, idx: (0, 0)),
                pl.BlockSpec((width, columns), lambda j, idx: (j, 0)),
            ],
            scratch_shapes=[
                pltpu.VMEM((width, columns), jnp.float32),
                pltpu.VMEM((1, 16, LANES), jnp.float32),
            ],
        ),
        out_shape=[
            jax.ShapeDtypeStruct((1, LANES), jnp.float32),
            jax.ShapeDtypeStruct((steps * width, columns), jnp.bfloat16),
        ],
        compiler_params=pltpu.CompilerParams(vmem_limit_bytes=FULL_VMEM),
        cost_estimate=SMALL,
        name="own_gram",
    )(idx, inputs, left, right)


def near_kernel(pieces, idx, before, own, y_left, y_right, z_left, z_right, *refs):
    others, (out, grads, tiles, acc) = refs[:pieces], refs[pieces:]
    width = tiles.shape[1]
    acc[...] = jnp.zeros_like(acc)
    for q, other in enumerate(others):
        fill(tiles.at[0], other[0], y_left, y_right)
        fill(tiles.at[1], other[1], z_left, z_right)

        def load(first):
            at, there = strip_at(first), strip_at(idx[TILE + q] * width + first)
            for lanes in lanes_of(tiles.shape[2]):
                tile = [tiles[k, at, lanes] for k in range(QUAD - 2)]
                for k in range(QUAD - 2):
                    grads[k, there, lanes] = tile[k].astype(grads.dtype)
                yield [own[there, lanes].astype(jnp.float32)] + tile

        pair_sums(NEAR_PAIRS, width // STRIP, STRIP, load, acc)
    out[...] = place_sums(idx[PLACE], NEAR_PAIRS, acc, before[...])


def far_kernel(pieces, idx, before, left, right, own, grads, *refs):
    others, (out, last, tile, acc) = refs[:pieces], refs[pieces:]
    width = tile.shape[0]
    acc[...] = jnp.zeros_like(acc)
    for q, other in enumerate(others):
        fill(tile, other[QUAD - 2], left, right)

        def load(first):
            at, there = strip_at(first), strip_at(idx[TILE + q] * width + first)
            for lanes in lanes_of(tile.shape[1]):
                mine = tile[at, lanes]
                last[there, lanes] = mine.astype(last.dtype)
                three = [own[there, lanes]] + [grads[k, there, lanes] for k in range(QUAD - 2)]
                yield [v.astype(jnp.float32) for v in three] + [mine]

        pair_sums(FAR_PAIRS, width // STRIP, STRIP, load, acc)
    out[...] = place_sums(idx[PLACE], FAR_PAIRS, acc, before[...])


def once(shape, at):
    return pl.BlockSpec(shape, lambda j, idx: at, pipeline_mode=pl.Buffered(1))


PLACE, BIT, TILE = 0, 1, 2


def in_place(kernel, inputs, out_shape, scratch_shapes, name):
    return pl.pallas_call(
        kernel,
        in_specs=[pl.BlockSpec(memory_space=m) for m, _ in inputs],
        out_specs=[pl.BlockSpec(memory_space=pltpu.VMEM)] * len(out_shape),
        out_shape=out_shape,
        scratch_shapes=scratch_shapes,
        compiler_params=pltpu.CompilerParams(vmem_limit_bytes=VMEM_LIMIT),
        cost_estimate=SMALL,
        name=name,
    )(*[v for _, v in inputs])


def near_gram(idx, before, own, others, errors):
    _, width, _ = others[0].shape
    rows, columns = own.shape
    return in_place(
        functools.partial(near_kernel, len(others)),
        [(pltpu.SMEM, idx)] + [(pltpu.VMEM, v) for v in (before, own, *errors, *others)],
        [
            jax.ShapeDtypeStruct((1, LANES), jnp.float32),
            jax.ShapeDtypeStruct((QUAD - 2, rows, columns), jnp.bfloat16),
        ],
        [
            pltpu.VMEM((QUAD - 2, width, columns), jnp.float32),
            pltpu.VMEM((len(NEAR_PAIRS), STRIP, LANES), jnp.float32),
        ],
        "near_gram",
    )


def far_gram(idx, before, own, others, left, right, grads):
    _, width, _ = others[0].shape
    rows, columns = own.shape
    return in_place(
        functools.partial(far_kernel, len(others)),
        [(pltpu.SMEM, idx)] + [(pltpu.VMEM, v) for v in (before, left, right, own, grads, *others)],
        [
            jax.ShapeDtypeStruct((1, LANES), jnp.float32),
            jax.ShapeDtypeStruct((rows, columns), jnp.bfloat16),
        ],
        [
            pltpu.VMEM((width, columns), jnp.float32),
            pltpu.VMEM((len(FAR_PAIRS), STRIP, LANES), jnp.float32),
        ],
        "far_gram",
    )


def merge_factors(gram_at):
    factors = [None] * QUAD
    for a, b in ((0, 1), (2, 3)):
        cross = gram_at(a, b)
        factors[a] = 1.0 - cross / (2.0 * gram_at(a, a))
        factors[b] = 1.0 - cross / (2.0 * gram_at(b, b))

    def product(left, right):
        return sum(factors[a] * factors[b] * gram_at(a, b) for a in left for b in right)

    cross = product((0, 1), (2, 3))
    first = 1.0 - cross / (2.0 * product((0, 1), (0, 1)))
    second = 1.0 - cross / (2.0 * product((2, 3), (2, 3)))
    return [factors[0] * first, factors[1] * first, factors[2] * second, factors[3] * second]


def merge_kernel(scale, flip, per_block, width, at, idx, sums, own, grads, last, out):
    turn = idx[PLACE] * (QUAD + 1)
    factors = merge_factors(lambda a, b: sums[0, jnp.bitwise_xor(QUAD * a + b, turn)])
    factors = [factor * scale for factor in factors]
    bit = 1 - idx[BIT] if flip else idx[BIT]
    columns = out.shape[1]
    for j in range(out.shape[0] // width):
        tile = (2 * (j // per_block) + bit) * per_block + j % per_block

        def strip(i, carry):
            there, here = strip_at(tile * width + i * STRIP), strip_at(j * width + i * STRIP)
            for lanes in lanes_of(columns):
                from_lanes = slice(at * columns + lanes.start, at * columns + lanes.stop)
                four = (own[there, from_lanes], grads[0, there, from_lanes])
                four += (grads[1, there, from_lanes], last[there, from_lanes])
                total = factors[0] * four[0].astype(jnp.float32)
                for factor, value in zip(factors[1:], four[1:]):
                    total = total + factor * value.astype(jnp.float32)
                out[here, lanes] = total.astype(out.dtype)
            return carry

        lax.fori_loop(0, width // STRIP, strip, 0)


def merge(idx, flip, sums, own, grads, last, scale, per_block, width, at, columns):
    return in_place(
        functools.partial(merge_kernel, scale, flip, per_block, width, at),
        [(pltpu.SMEM, idx), (pltpu.SMEM, sums)] + [(pltpu.VMEM, v) for v in (own, grads, last)],
        [jax.ShapeDtypeStruct((own.shape[0] // 2, columns), jnp.bfloat16)],
        [],
        "merge",
    )[0]


def partial_kernel(first_at, before, kept, received, out, acc):
    lane = lax.broadcasted_iota(jnp.int32, (1, LANES), 1)
    rows, columns = kept.shape

    def strip(i, sums):
        at = pl.ds(pl.multiple_of(i * 16, 16), 16)
        cross, mine, theirs = sums
        for c in range(columns // LANES):
            lanes = slice(c * LANES, (c + 1) * LANES)
            a = kept[at, lanes].astype(jnp.float32)
            b = received[at, lanes].astype(jnp.float32)
            cross, mine, theirs = cross + a * b, mine + a * a, theirs + b * b
        return cross, mine, theirs

    zero = jnp.zeros((16, LANES), jnp.float32)
    sums = lax.fori_loop(0, rows // 16, strip, (zero, zero, zero))
    result = before[...]
    for place, value in zip((0, 1 + first_at[0], 2 - first_at[0]), sums):
        total = jnp.sum(jnp.sum(value, axis=0, keepdims=True), axis=1, keepdims=True)
        result = result + jnp.where(lane == place, total, 0.0)
    out[...] = result


def partial_sums(bit, before, kept, received):
    return pl.pallas_call(
        partial_kernel,
        in_specs=[pl.BlockSpec(memory_space=pltpu.SMEM)] + [pl.BlockSpec(memory_space=pltpu.VMEM)] * 3,
        out_shape=jax.ShapeDtypeStruct((1, LANES), jnp.float32),
        scratch_shapes=[pltpu.VMEM((8, LANES), jnp.float32)],
        compiler_params=pltpu.CompilerParams(vmem_limit_bytes=VMEM_LIMIT),
        cost_estimate=SMALL,
        name="partial_sums",
    )(bit.reshape(1).astype(jnp.int32), before, kept, received)


def update_kernel(bit, sums, momentum, kept_0, kept_1, received_0, received_1, out):
    half = kept_0.shape[1]
    lower = bit[0] == 0
    lower_factor = 1.0 - sums[0, 0] / (2.0 * sums[0, 1])
    upper_factor = 1.0 - sums[0, 0] / (2.0 * sums[0, 2])
    factor = jnp.where(lower, lower_factor, upper_factor)
    other = jnp.where(lower, upper_factor, lower_factor)
    for at, a, b in ((slice(0, half), kept_0, received_0), (slice(half, 2 * half), kept_1, received_1)):
        out[:, at] = 0.9 * momentum[:, at] + (
            factor * a[...].astype(jnp.float32) + other * b[...].astype(jnp.float32)
        )


def update(bit, sums, momentum, kept, received):
    rows, columns = momentum.shape
    tile = math.gcd(rows, 128)
    spec = lambda width: pl.BlockSpec((tile, width), lambda i, *_: (i, 0))
    return pl.pallas_call(
        update_kernel,
        grid_spec=pltpu.PrefetchScalarGridSpec(
            num_scalar_prefetch=1,
            grid=(rows // tile,),
            in_specs=[pl.BlockSpec(sums.shape, lambda i, *_: (0, 0), memory_space=pltpu.SMEM), spec(columns)] + [spec(columns // 2)] * 4,
            out_specs=spec(columns),
        ),
        out_shape=jax.ShapeDtypeStruct(momentum.shape, jnp.float32),
        compiler_params=pltpu.CompilerParams(vmem_limit_bytes=VMEM_LIMIT),
        cost_estimate=SMALL,
        name="update",
    )(bit.reshape(1).astype(jnp.int32), sums, momentum, *kept, *received)


def body(inputs, weight, targets, momentum):
    groups = lax.axis_size("dp")
    parts = lax.axis_size("tensor")
    depth = groups.bit_length() - 1
    me = lax.axis_index("dp")
    part = lax.axis_index("tensor")
    rows, depth_width = inputs.shape
    columns = weight.shape[1]
    block = depth_width // groups
    width = depth_width // QUAD // parts
    per_block = block // width
    place = me % QUAD

    def columns_of(at, start, size):
        first = (QUAD * (start // block) + at) * block + start % block
        return lax.dynamic_slice(inputs, (0, first), (rows, size)).T

    slabs = [columns_of(place ^ k, part * width, width) for k in range(1, QUAD)]
    slabs, ready = lax.optimization_barrier((slabs, inputs))
    arrived = [exchange(s, "dp", k + 1) for k, s in enumerate(slabs)]

    left = forward(ready, in_hbm(weight), targets, 0, 2)
    arrived[:2], left, ready = lax.optimization_barrier((arrived[:2], left, ready))
    y_left, z_left = exchange(left, "dp", 1), exchange(left, "dp", 2)
    right = forward(ready, in_hbm(weight), targets, 1, 2)
    y_right, z_right = exchange(right, "dp", 1), exchange(right, "dp", 2)
    others, sources = [jnp.stack(arrived)], [part]
    mask = parts // 2
    while mask:
        sources = sources + [s ^ mask for s in sources]
        mask //= 2
    bit = me >> 2 & 1
    idx = jnp.stack([place, bit] + sources).astype(jnp.int32)
    sums, own = own_gram(idx, in_hbm(inputs), left, right, width, block)
    left, right, y_left, z_left, own = lax.optimization_barrier((left, right, y_left, z_left, own))
    part_grad = input_grad_part(in_hbm(weight), left, right)
    mask = parts // 2
    while mask:
        if mask == 1:
            others, part_grad, y_right, z_right, z_left = lax.optimization_barrier(
                (others, part_grad, y_right, z_right, z_left)
            )
        others = others + [exchange(o, "tensor", mask) for o in others]
        mask //= 2
    far_left, far_right = exchange(z_left, "dp", 1), exchange(y_right, "dp", 2)

    sums, grads = near_gram(idx, sums, own, others, (y_left, y_right, z_left, z_right))
    sums, last = far_gram(idx, sums, own, others, far_left, far_right, grads)
    sums = total_over(sums, 2)
    half = columns // 2

    def merged_half(flip, h):
        return merge(idx, flip, sums, own, grads, last, rows**-0.5, per_block, width, h, half)

    sent = [merged_half(True, h) for h in range(2)]
    received = [exchange(s, "dp", 4) for s in sent]
    _, sums = lax.optimization_barrier((sent, sums))
    kept = [merged_half(False, h) for h in range(2)]
    summed = lax.psum_scatter(part_grad, "tensor", scatter_dimension=0, tiled=True)

    for level in range(2, depth):
        if level > 2:
            lower = bit == 0
            lower_factor = 1.0 - sums[0, 0] / (2.0 * sums[0, 1])
            upper_factor = 1.0 - sums[0, 0] / (2.0 * sums[0, 2])
            factor = jnp.where(lower, lower_factor, upper_factor)
            other = jnp.where(lower, upper_factor, lower_factor)
            merged = [
                factor * a.astype(jnp.float32) + other * b.astype(jnp.float32) for a, b in zip(kept, received)
            ]
            bit = me >> level & 1
            paired = [v.reshape(v.shape[0] // (2 * block), 2, block, v.shape[1]) for v in merged]
            kept = [jnp.where(bit == 0, v[:, 0], v[:, 1]).reshape(-1, v.shape[-1]) for v in paired]
            sent = [jnp.where(bit == 0, v[:, 1], v[:, 0]).reshape(-1, v.shape[-1]) for v in paired]
            received = [exchange(s.astype(jnp.bfloat16), "dp", 2**level) for s in sent]
        sums = jnp.zeros((1, LANES), jnp.float32)
        for a, b in zip(kept, received):
            sums = partial_sums(bit, sums, a, b)
        sums = total_over(sums, level + 1)
    new_momentum = update(bit, sums, momentum, kept, received)
    return (summed, new_momentum, jnp.sqrt(sums[0, 1:3]) / depth_width)


def solution(mesh):
    return jax.shard_map(
        body,
        mesh=mesh,
        in_specs=(P("dp", None), P(None, "tensor"), P("dp", "tensor"), P("dp", "tensor")),
        out_specs=(P("tensor", "dp"), P("dp", "tensor"), P()),
        check_vma=False,
    )
```

time: 164 us -> 159 us (0.970)
  local copies, waits for them, and re-layouts: 11.7 us -> 5.51 us
  waiting for transfers between devices: 66 us -> 70.3 us
    unnamed x15 -> x9, local copies, waits for them, and re-layouts: 8.8 us -> 3.84 us
    ppermute x23, waiting for transfers between devices: 66 us -> 70.3 us  [exchange(): return lax.ppermute(value, axis, pairs)]
    pallas_call x6 -> x7, Pallas kernels: 24.7 us -> 22.4 us  [the longest x6 17.5 us: in_place(): pl.pallas_call(kernel, in_specs=[pl.BlockSpec(memory_space=m) for m, _ in...]
    pallas_call x1 -> x2, Pallas kernels: 9.17 us -> 8.96 us  [forward(): pl.pallas_call(forward_kernel, grid=(columns // tile,), in_specs=[pl.Bloc...]
  transfers between devices with their start and end apart: 24 -> 24, of which waited for: 17 -> 19; matrix products, arithmetic and copies ran while one was open for 3% -> 0% of each run, Pallas kernels for 27% -> 28%
where the time goes in v3:
time: 159 us
  waiting for transfers between devices  70.3 us (44%)
  Pallas kernels  43.8 us (28%)
  starting transfers between devices  24.2 us (15%)
  between operations  14.2 us (9%)
  local copies, waits for them, and re-layouts  5.51 us (3%)
    ppermute x23, waiting for transfers between devices, exchange(): return lax.ppermute(value, axis, pairs)  70.3 us
    ppermute x23, starting transfers between devices, exchange(): return lax.ppermute(value, axis, pairs)  24.2 us
    pallas_call x6, Pallas kernels, in_place(): pl.pallas_call(kernel, in_specs=[pl.BlockSpec(memory_space=m) for m, _ in...  17.5 us
    pallas_call x2, Pallas kernels, forward(): pl.pallas_call(forward_kernel, grid=(columns // tile,), in_specs=[pl.Bloc...  8.96 us
    pallas_call x1, Pallas kernels, input_grad_part(): pl.pallas_call(input_grad_kernel, grid=(inner // tile,), in_specs=[pl.Blo...  8.64 us
    pallas_call x1, Pallas kernels, own_gram(): pl.pallas_call(own_kernel, grid_spec=pltpu.PrefetchScalarGridSpec(num_sca...  4.87 us
    unnamed x9, local copies, waits for them, and re-layouts  3.84 us
  transfers between devices with their start and end apart: 24, of which 19 were waited for; matrix products, arithmetic and copies ran while one was open for 0% of the time, Pallas kernels for 28%

profile of v3, /device:TPU:0, one launch (start us, length us, event | category | flops | bytes accessed | tf_op | source)
XLA Modules:
  0.0 158.7 jit_solution(8277759531972767656)
XLA Ops:
  7.2 0.0 reduce-scatter.2.cloned.1.call-start
  7.3 1.6 %constant_dynamic-slice_fusion = (bf16[512,256]{1,0:T(8,128)(2,1)S(1)}, bf16[512,256]{1,0:T(8,128)(2,1)S(1)}, bf16[512,256]{1,0:T(8,128)(2,1)S(1)}) fusion(bf16[512,4096]{1,0:T(8,128)(2,1)} %x.3, s32[]{:T(128)S(6)} %select_n.35, s32[]{:T(128)S(6)} %select_n.34, s32[]{:T(128)S(6)} %select_n.33), kind=kLoop, calls=%fused_computation.1 | loop fusion | bytes 1572876 | tf_op jit(solution)/shard_map/dynamic_slice | solution.py:427
  8.9 0.1 copy.12
  9.0 0.1 copy.11
  9.1 0.1 copy.10
  9.3 3.0 %collective-permute-start = (bf16[256,512]{1,0:T(8,128)(2,1)S(1)}, bf16[256,512]{1,0:T(8,128)(2,1)S(1)}, u32[]{:S(2)}, u32[]{:S(2)}) collective-permute-start(bf16[256,512]{1,0:T(8,128)(2,1)S(1)} %bitcast.16), channel_id=1, source_target_pairs={{0,4},{4,0},{8,12},{12,8},{16,20},{20,16},{24,28},{28,24},{1,5},{5... | collective-permute-start | bytes 786440 | tf_op jit(solution)/shard_map/ppermute | solution.py:24
  12.3 1.6 collective-permute-start.1
  13.9 2.2 %copy-done = bf16[512,4096]{1,0:T(8,128)(2,1)S(1)} copy-done((bf16[512,4096]{1,0:T(8,128)(2,1)S(1)}, bf16[512,4096]{1,0:T(8,128)(2,1)}, u32[]{:S(2)}) %copy-start) | copy-done | bytes 4194328
  16.1 1.2 copy-done.1
  17.3 4.1 %forward.2.left = bf16[512,512]{1,0:T(8,128)(2,1)S(1)} custom-call(bf16[512,4096]{1,0:T(8,128)(2,1)S(1)} %copy-done, bf16[4096,1024]{1,0:T(8,128)(2,1)} %w.5, bf16[512,1024]{1,0:T(8,128)(2,1)S(1)} %copy-done.1), custom_call_target="tpu_custom_call" | custom-call | flops 1 | bytes 1 | tf_op jit(solution)/shard_map/forward/pallas_call | solution.py:82
  21.5 0.1 collective-permute-done.1
  21.6 3.9 %collective-permute-done.2 = bf16[256,512]{1,0:T(8,128)(2,1)S(1)} collective-permute-done((bf16[256,512]{1,0:T(8,128)(2,1)S(1)}, bf16[256,512]{1,0:T(8,128)(2,1)S(1)}, u32[]{:S(2)}, u32[]{:S(2)}) %collective-permute-start.2) | collective-permute-done | bytes 262176 | tf_op jit(solution)/shard_map/ppermute | solution.py:24
  25.5 0.1 pad_maximum_fusion.refs_0_
  25.6 1.7 %collective-permute-start.3 = (bf16[3,256,512]{2,1,0:T(8,128)(2,1)S(1)}, bf16[3,256,512]{2,1,0:T(8,128)(2,1)}, u32[]{:S(2)}, u32[]{:S(2)}) collective-permute-start(bf16[3,256,512]{2,1,0:T(8,128)(2,1)S(1)} %pad_maximum_fusion.refs_0_), channel_id=1, source_target_pairs={{0,2},{1,3},{2,0},{3,1},{4,6},{5,7},{6,4},{7,5},{8,10},{9,11},{10,... | collective-permute-start | bytes 2359304 | tf_op jit(solution)/shard_map/ppermute | solution.py:24
  27.3 1.6 collective-permute-start.5
  28.8 1.6 collective-permute-start.4
  30.4 4.8 %forward.3.right = bf16[512,512]{1,0:T(8,128)(2,1)} custom-call(bf16[512,4096]{1,0:T(8,128)(2,1)S(1)} %copy-done, bf16[4096,1024]{1,0:T(8,128)(2,1)} %w.5, bf16[512,1024]{1,0:T(8,128)(2,1)S(1)} %copy-done.1), custom_call_target="tpu_custom_call" | custom-call | flops 1 | bytes 1 | tf_op jit(solution)/shard_map/forward/pallas_call | solution.py:82
  35.2 0.4 collective-permute-start.7
  35.6 0.5 collective-permute-start.6
  36.1 0.1 stack.43.idx
  36.2 4.9 %own_gram.1 = (f32[1,128]{1,0:T(1,128)S(1)}, bf16[1024,1024]{1,0:T(8,128)(2,1)S(1)}) custom-call(s32[6]{0:T(128)S(1)} %stack.43.idx, bf16[512,4096]{1,0:T(8,128)(2,1)} %x.3, bf16[512,512]{1,0:T(8,128)(2,1)S(1)} %forward.2.left, bf16[512,512]{1,0:T(8,128)(2,1)} %forward.3.right), custom_call_target="tpu_custom_call" | custom-call | flops 1 | bytes 1 | tf_op jit(solution)/shard_map/own_gram/pallas_call | solution.py:174
  41.1 1.1 collective-permute-done.5.z_left
  42.2 1.6 collective-permute-done.4.y_left
  43.8 8.6 %input_grad_part.1 = bf16[4096,512]{1,0:T(8,128)(2,1)} custom-call(bf16[4096,1024]{1,0:T(8,128)(2,1)} %w.5, bf16[512,512]{1,0:T(8,128)(2,1)S(1)} %forward.2.left, bf16[512,512]{1,0:T(8,128)(2,1)} %forward.3.right), custom_call_target="tpu_custom_call" | custom-call | flops 1 | bytes 1 | tf_op jit(solution)/shard_map/input_grad_part/pallas_call | solution.py:113
  52.5 0.0 reduce-scatter.2.cloned.1.call-update
  52.5 0.1 collective-permute-start.8
  52.6 0.5 collective-permute-start.9
  53.1 0.5 collective-permute-start.11
  53.5 1.5 collective-permute-start.10
  55.0 0.1 collective-permute-done.8.refs_2_
  55.2 1.0 collective-permute-done.9.refs_3_
  56.2 7.5 %near_gram.1 = (f32[1,128]{1,0:T(1,128)S(1)}, bf16[2,1024,1024]{2,1,0:T(8,128)(2,1)S(1)}) custom-call(s32[6]{0:T(128)S(1)} %stack.43.idx, f32[1,128]{1,0:T(1,128)S(1)} %get-tuple-element.42.before, bf16[1024,1024]{1,0:T(8,128)(2,1)S(1)} %get-tuple-element.43.own, bf16[512,512]{1,0:T(8,128)(2,1)} %collective-permute-done.4.y_left, ...), custom_call_target="tpu_custom_call" | custom-call | flops 1 | bytes 1 | tf_op jit(solution)/shard_map/near_gram/pallas_call | solution.py:247
  63.6 3.5 %collective-permute-done.11.right = bf16[512,512]{1,0:T(8,128)(2,1)S(1)} collective-permute-done((bf16[512,512]{1,0:T(8,128)(2,1)}, bf16[512,512]{1,0:T(8,128)(2,1)S(1)}, u32[]{:S(2)}, u32[]{:S(2)}) %collective-permute-start.11) | collective-permute-done | bytes 524320 | tf_op jit(solution)/shard_map/ppermute | solution.py:24
  67.2 0.2 collective-permute-done.10.left
  67.4 4.9 %far_gram.1 = (f32[1,128]{1,0:T(1,128)S(1)}, bf16[1024,1024]{1,0:T(8,128)(2,1)S(1)}) custom-call(s32[6]{0:T(128)S(1)} %stack.43.idx, f32[1,128]{1,0:T(1,128)S(1)} %get-tuple-element.50.before, bf16[512,512]{1,0:T(8,128)(2,1)S(1)} %collective-permute-done.10.left, bf16[512,512]{1,0:T(8,128)(2,1)S(1)} %collective-permute-done.11.right, ...), custom_call_target="tpu_custom_call" | custom-call | flops 1 | bytes 1 | tf_op jit(solution)/shard_map/far_gram/pallas_call | solution.py:247
  72.3 0.0 collective-permute-start.12
  72.3 1.1 collective-permute-done.12
  73.4 0.4 collective-permute-start.13
  73.8 3.1 %collective-permute-done.13 = f32[1,128]{1,0:T(1,128)S(1)} collective-permute-done((f32[1,128]{1,0:T(1,128)S(1)}, f32[1,128]{1,0:T(1,128)S(1)}, u32[]{:S(2)}, u32[]{:S(2)}) %collective-permute-start.13) | collective-permute-done | bytes 544 | tf_op jit(solution)/shard_map/ppermute | solution.py:24
  77.0 1.5 collective-permute-start.14
  78.5 2.0 %collective-permute-done.14 = f32[1,128]{1,0:T(1,128)S(1)} collective-permute-done((f32[1,128]{1,0:T(1,128)S(1)}, f32[1,128]{1,0:T(1,128)S(1)}, u32[]{:S(2)}, u32[]{:S(2)}) %collective-permute-start.14) | collective-permute-done | bytes 544 | tf_op jit(solution)/shard_map/ppermute | solution.py:24
  80.5 1.6 collective-permute-start.15
  82.1 2.0 %collective-permute-done.15 = f32[1,128]{1,0:T(1,128)S(1)} collective-permute-done((f32[1,128]{1,0:T(1,128)S(1)}, f32[1,128]{1,0:T(1,128)S(1)}, u32[]{:S(2)}, u32[]{:S(2)}) %collective-permute-start.15) | collective-permute-done | bytes 544 | tf_op jit(solution)/shard_map/ppermute | solution.py:24
  84.0 1.3 merge.4
  85.3 2.7 %collective-permute-start.16 = (bf16[512,512]{1,0:T(8,128)(2,1)S(1)}, bf16[512,512]{1,0:T(8,128)(2,1)S(1)}, u32[]{:S(2)}, u32[]{:S(2)}) collective-permute-start(bf16[512,512]{1,0:T(8,128)(2,1)S(1)} %merge.4), channel_id=1, source_target_pairs={{0,16},{4,20},{8,24},{12,28},{16,0},{20,4},{24,8},{28,12},{1,17},{... | collective-permute-start | bytes 1572872 | tf_op jit(solution)/shard_map/ppermute | solution.py:24
  88.0 1.3 merge.5
  89.3 0.4 collective-permute-start.17
  89.7 1.3 merge.7.kept.kept_1
  91.0 1.3 merge.6.kept.kept_0
  92.3 29.4 %collective-permute-done.16.received.received_0 = bf16[512,512]{1,0:T(8,128)(2,1)S(1)} collective-permute-done((bf16[512,512]{1,0:T(8,128)(2,1)S(1)}, bf16[512,512]{1,0:T(8,128)(2,1)S(1)}, u32[]{:S(2)}, u32[]{:S(2)}) %collective-permute-start.16) | collective-permute-done | bytes 524320 | tf_op jit(solution)/shard_map/ppermute | solution.py:24
  121.7 0.5 partial_sums.2.before
  122.2 9.6 %collective-permute-done.17.received.received_1 = bf16[512,512]{1,0:T(8,128)(2,1)S(1)} collective-permute-done((bf16[512,512]{1,0:T(8,128)(2,1)S(1)}, bf16[512,512]{1,0:T(8,128)(2,1)S(1)}, u32[]{:S(2)}, u32[]{:S(2)}) %collective-permute-start.17) | collective-permute-done | bytes 524320 | tf_op jit(solution)/shard_map/ppermute | solution.py:24
  131.8 0.5 partial_sums.3
  132.3 1.1 collective-permute-done.18
  133.4 0.5 collective-permute-start.19
  133.9 3.0 %collective-permute-done.19 = f32[1,128]{1,0:T(1,128)S(1)} collective-permute-done((f32[1,128]{1,0:T(1,128)S(1)}, f32[1,128]{1,0:T(1,128)S(1)}, u32[]{:S(2)}, u32[]{:S(2)}) %collective-permute-start.19) | collective-permute-done | bytes 544 | tf_op jit(solution)/shard_map/ppermute | solution.py:24
  137.0 1.5 collective-permute-start.20
  138.5 2.0 %collective-permute-done.20 = f32[1,128]{1,0:T(1,128)S(1)} collective-permute-done((f32[1,128]{1,0:T(1,128)S(1)}, f32[1,128]{1,0:T(1,128)S(1)}, u32[]{:S(2)}, u32[]{:S(2)}) %collective-permute-start.20) | collective-permute-done | bytes 544 | tf_op jit(solution)/shard_map/ppermute | solution.py:24
  140.5 0.7 collective-permute-start.21
  141.2 2.9 %collective-permute-done.21 = f32[1,128]{1,0:T(1,128)S(1)} collective-permute-done((f32[1,128]{1,0:T(1,128)S(1)}, f32[1,128]{1,0:T(1,128)S(1)}, u32[]{:S(2)}, u32[]{:S(2)}) %collective-permute-start.21) | collective-permute-done | bytes 544 | tf_op jit(solution)/shard_map/ppermute | solution.py:24
  144.1 2.0 %collective-permute-start.22 = (f32[1,128]{1,0:T(1,128)S(1)}, f32[1,128]{1,0:T(1,128)S(1)}, u32[]{:S(2)}, u32[]{:S(2)}) collective-permute-start(f32[1,128]{1,0:T(1,128)S(1)} %add.84), channel_id=1, source_target_pairs={{0,16},{4,20},{8,24},{12,28},{16,0},{20,4},{24,8},{28,12},{1,17},{... | collective-permute-start | bytes 1544 | tf_op jit(solution)/shard_map/ppermute | solution.py:24
  146.1 2.4 %collective-permute-done.22 = f32[1,128]{1,0:T(1,128)S(1)} collective-permute-done((f32[1,128]{1,0:T(1,128)S(1)}, f32[1,128]{1,0:T(1,128)S(1)}, u32[]{:S(2)}, u32[]{:S(2)}) %collective-permute-start.22) | collective-permute-done | bytes 544 | tf_op jit(solution)/shard_map/ppermute | solution.py:24
  148.5 2.8 %update.1 = f32[512,1024]{1,0:T(8,128)} custom-call(s32[1]{0:T(128)} %bitcast.7.first_at.bit, f32[1,128]{1,0:T(1,128)S(1)} %add.85.sums, f32[512,1024]{1,0:T(8,128)S(1)} %copy-done.2, bf16[512,512]{1,0:T(8,128)(2,1)S(1)} %merge.6.kept.kept_0, bf16[512,512]{1,0:T(8,128)(2,1)S(1)} %merge.7.kept.kept_1, ...), custom_call_target="tpu_custom_call" | custom-call | flops 1 | bytes 1 | tf_op jit(solution)/shard_map/update/pallas_call | solution.py:397
  151.3 0.6 multiply_bitcast_fusion
  (21 shorter events, 0.1 us)
Async XLA Ops:
  7.2 144.7 %reduce-scatter.2.cloned.1.call-start = ((), (), s32[]{:S(2)}) async-start(), calls=%async_computation.1 | async-start | bytes 5242880 | tf_op jit(solution)/shard_map/reduce_scatter | solution.py:470
  9.3 12.2 %collective-permute-start = (bf16[256,512]{1,0:T(8,128)(2,1)S(1)}, bf16[256,512]{1,0:T(8,128)(2,1)S(1)}, u32[]{:S(2)}, u32[]{:S(2)}) collective-permute-start(bf16[256,512]{1,0:T(8,128)(2,1)S(1)} %bitcast.16), channel_id=1, source_target_pairs={{0,4},{4,0},{8,12},{12,8},{16,20},{20,16},{24,28},{28,24},{1,5},{5... | collective-permute-start | bytes 786440 | tf_op jit(solution)/shard_map/ppermute | solution.py:24
  12.3 9.2 %collective-permute-start.1 = (bf16[256,512]{1,0:T(8,128)(2,1)S(1)}, bf16[256,512]{1,0:T(8,128)(2,1)S(1)}, u32[]{:S(2)}, u32[]{:S(2)}) collective-permute-start(bf16[256,512]{1,0:T(8,128)(2,1)S(1)} %bitcast.15), channel_id=1, source_target_pairs={{0,8},{4,12},{8,0},{12,4},{16,24},{20,28},{24,16},{28,20},{1,9},{5... | collective-permute-start | bytes 786440 | tf_op jit(solution)/shard_map/ppermute | solution.py:24
  13.9 11.6 %collective-permute-start.2 = (bf16[256,512]{1,0:T(8,128)(2,1)S(1)}, bf16[256,512]{1,0:T(8,128)(2,1)S(1)}, u32[]{:S(2)}, u32[]{:S(2)}) collective-permute-start(bf16[256,512]{1,0:T(8,128)(2,1)S(1)} %bitcast.14), channel_id=1, source_target_pairs={{0,12},{4,8},{8,4},{12,0},{16,28},{20,24},{24,20},{28,16},{1,13},{... | collective-permute-start | bytes 786440 | tf_op jit(solution)/shard_map/ppermute | solution.py:24
  13.9 2.2 %copy-start = (bf16[512,4096]{1,0:T(8,128)(2,1)S(1)}, bf16[512,4096]{1,0:T(8,128)(2,1)}, u32[]{:S(2)}) copy-start(bf16[512,4096]{1,0:T(8,128)(2,1)} %x.3) | copy-start | bytes 12582916
  16.1 1.2 copy-start.1
  25.6 26.9 %collective-permute-start.3 = (bf16[3,256,512]{2,1,0:T(8,128)(2,1)S(1)}, bf16[3,256,512]{2,1,0:T(8,128)(2,1)}, u32[]{:S(2)}, u32[]{:S(2)}) collective-permute-start(bf16[3,256,512]{2,1,0:T(8,128)(2,1)S(1)} %pad_maximum_fusion.refs_0_), channel_id=1, source_target_pairs={{0,2},{1,3},{2,0},{3,1},{4,6},{5,7},{6,4},{7,5},{8,10},{9,11},{10,... | collective-permute-start | bytes 2359304 | tf_op jit(solution)/shard_map/ppermute | solution.py:24
  27.3 15.0 %collective-permute-start.5 = (bf16[512,512]{1,0:T(8,128)(2,1)S(1)}, bf16[512,512]{1,0:T(8,128)(2,1)}, u32[]{:S(2)}, u32[]{:S(2)}) collective-permute-start(bf16[512,512]{1,0:T(8,128)(2,1)S(1)} %forward.2.left), channel_id=1, source_target_pairs={{0,8},{4,12},{8,0},{12,4},{16,24},{20,28},{24,16},{28,20},{1,9},{5... | collective-permute-start | bytes 1572872 | tf_op jit(solution)/shard_map/ppermute | solution.py:24
  28.8 15.0 %collective-permute-start.4 = (bf16[512,512]{1,0:T(8,128)(2,1)S(1)}, bf16[512,512]{1,0:T(8,128)(2,1)}, u32[]{:S(2)}, u32[]{:S(2)}) collective-permute-start(bf16[512,512]{1,0:T(8,128)(2,1)S(1)} %forward.2.left), channel_id=1, source_target_pairs={{0,4},{4,0},{8,12},{12,8},{16,20},{20,16},{24,28},{28,24},{1,5},{5... | collective-permute-start | bytes 1572872 | tf_op jit(solution)/shard_map/ppermute | solution.py:24
  35.2 17.2 %collective-permute-start.7 = (bf16[512,512]{1,0:T(8,128)(2,1)}, bf16[512,512]{1,0:T(8,128)(2,1)}, u32[]{:S(2)}, u32[]{:S(2)}) collective-permute-start(bf16[512,512]{1,0:T(8,128)(2,1)} %forward.3.right), channel_id=1, source_target_pairs={{0,8},{4,12},{8,0},{12,4},{16,24},{20,28},{24,16},{28,20},{1,9},{5... | collective-permute-start | bytes 1572872 | tf_op jit(solution)/shard_map/ppermute | solution.py:24
  35.6 16.8 %collective-permute-start.6 = (bf16[512,512]{1,0:T(8,128)(2,1)}, bf16[512,512]{1,0:T(8,128)(2,1)}, u32[]{:S(2)}, u32[]{:S(2)}) collective-permute-start(bf16[512,512]{1,0:T(8,128)(2,1)} %forward.3.right), channel_id=1, source_target_pairs={{0,4},{4,0},{8,12},{12,8},{16,20},{20,16},{24,28},{28,24},{1,5},{5... | collective-permute-start | bytes 1572872 | tf_op jit(solution)/shard_map/ppermute | solution.py:24
  52.5 2.7 %collective-permute-start.8 = (bf16[3,256,512]{2,1,0:T(8,128)(2,1)S(1)}, bf16[3,256,512]{2,1,0:T(8,128)(2,1)S(1)}, u32[]{:S(2)}, u32[]{:S(2)}) collective-permute-start(bf16[3,256,512]{2,1,0:T(8,128)(2,1)S(1)} %pad_maximum_fusion.refs_0_), channel_id=1, source_target_pairs={{0,1},{1,0},{2,3},{3,2},{4,5},{5,4},{6,7},{7,6},{8,9},{9,8},{10,11... | collective-permute-start | bytes 2359304 | tf_op jit(solution)/shard_map/ppermute | solution.py:24
  52.6 3.6 %collective-permute-start.9 = (bf16[3,256,512]{2,1,0:T(8,128)(2,1)}, bf16[3,256,512]{2,1,0:T(8,128)(2,1)S(1)}, u32[]{:S(2)}, u32[]{:S(2)}) collective-permute-start(bf16[3,256,512]{2,1,0:T(8,128)(2,1)} %collective-permute-done.3.refs_1_), channel_id=1, source_target_pairs={{0,1},{1,0},{2,3},{3,2},{4,5},{5,4},{6,7},{7,6},{8,9},{9,8},{10,11... | collective-permute-start | bytes 2359304 | tf_op jit(solution)/shard_map/ppermute | solution.py:24
  53.1 14.1 %collective-permute-start.11 = (bf16[512,512]{1,0:T(8,128)(2,1)}, bf16[512,512]{1,0:T(8,128)(2,1)S(1)}, u32[]{:S(2)}, u32[]{:S(2)}) collective-permute-start(bf16[512,512]{1,0:T(8,128)(2,1)} %collective-permute-done.6.y_right), channel_id=1, source_target_pairs={{0,8},{4,12},{8,0},{12,4},{16,24},{20,28},{24,16},{28,20},{1,9},{5... | collective-permute-start | bytes 1572872 | tf_op jit(solution)/shard_map/ppermute | solution.py:24
  53.5 13.8 %collective-permute-start.10 = (bf16[512,512]{1,0:T(8,128)(2,1)}, bf16[512,512]{1,0:T(8,128)(2,1)S(1)}, u32[]{:S(2)}, u32[]{:S(2)}) collective-permute-start(bf16[512,512]{1,0:T(8,128)(2,1)} %collective-permute-done.5.z_left), channel_id=1, source_target_pairs={{0,4},{4,0},{8,12},{12,8},{16,20},{20,16},{24,28},{28,24},{1,5},{5... | collective-permute-start | bytes 1572872 | tf_op jit(solution)/shard_map/ppermute | solution.py:24
  72.3 1.1 collective-permute-start.12
  73.4 3.5 %collective-permute-start.13 = (f32[1,128]{1,0:T(1,128)S(1)}, f32[1,128]{1,0:T(1,128)S(1)}, u32[]{:S(2)}, u32[]{:S(2)}) collective-permute-start(f32[1,128]{1,0:T(1,128)S(1)} %add.77), channel_id=1, source_target_pairs={{0,2},{1,3},{2,0},{3,1},{4,6},{5,7},{6,4},{7,5},{8,10},{9,11},{10,... | collective-permute-start | bytes 1544 | tf_op jit(solution)/shard_map/ppermute | solution.py:24
  77.0 3.5 %collective-permute-start.14 = (f32[1,128]{1,0:T(1,128)S(1)}, f32[1,128]{1,0:T(1,128)S(1)}, u32[]{:S(2)}, u32[]{:S(2)}) collective-permute-start(f32[1,128]{1,0:T(1,128)S(1)} %add.78), channel_id=1, source_target_pairs={{0,4},{4,0},{8,12},{12,8},{16,20},{20,16},{24,28},{28,24},{1,5},{5... | collective-permute-start | bytes 1544 | tf_op jit(solution)/shard_map/ppermute | solution.py:24
  80.5 3.5 %collective-permute-start.15 = (f32[1,128]{1,0:T(1,128)S(1)}, f32[1,128]{1,0:T(1,128)S(1)}, u32[]{:S(2)}, u32[]{:S(2)}) collective-permute-start(f32[1,128]{1,0:T(1,128)S(1)} %add.79), channel_id=1, source_target_pairs={{0,8},{4,12},{8,0},{12,4},{16,24},{20,28},{24,16},{28,20},{1,9},{5... | collective-permute-start | bytes 1544 | tf_op jit(solution)/shard_map/ppermute | solution.py:24
  85.3 36.4 %collective-permute-start.16 = (bf16[512,512]{1,0:T(8,128)(2,1)S(1)}, bf16[512,512]{1,0:T(8,128)(2,1)S(1)}, u32[]{:S(2)}, u32[]{:S(2)}) collective-permute-start(bf16[512,512]{1,0:T(8,128)(2,1)S(1)} %merge.4), channel_id=1, source_target_pairs={{0,16},{4,20},{8,24},{12,28},{16,0},{20,4},{24,8},{28,12},{1,17},{... | collective-permute-start | bytes 1572872 | tf_op jit(solution)/shard_map/ppermute | solution.py:24
  89.3 42.5 %collective-permute-start.17 = (bf16[512,512]{1,0:T(8,128)(2,1)S(1)}, bf16[512,512]{1,0:T(8,128)(2,1)S(1)}, u32[]{:S(2)}, u32[]{:S(2)}) collective-permute-start(bf16[512,512]{1,0:T(8,128)(2,1)S(1)} %merge.5), channel_id=1, source_target_pairs={{0,16},{4,20},{8,24},{12,28},{16,0},{20,4},{24,8},{28,12},{1,17},{... | collective-permute-start | bytes 1572872 | tf_op jit(solution)/shard_map/ppermute | solution.py:24
  91.0 57.5 %copy-start.2 = (f32[512,1024]{1,0:T(8,128)S(1)}, f32[512,1024]{1,0:T(8,128)}, u32[]{:S(2)}) copy-start(f32[512,1024]{1,0:T(8,128)} %momentum.1) | copy-start | bytes 6291460
  132.3 1.1 collective-permute-start.18
  133.4 3.5 %collective-permute-start.19 = (f32[1,128]{1,0:T(1,128)S(1)}, f32[1,128]{1,0:T(1,128)S(1)}, u32[]{:S(2)}, u32[]{:S(2)}) collective-permute-start(f32[1,128]{1,0:T(1,128)S(1)} %add.81), channel_id=1, source_target_pairs={{0,2},{1,3},{2,0},{3,1},{4,6},{5,7},{6,4},{7,5},{8,10},{9,11},{10,... | collective-permute-start | bytes 1544 | tf_op jit(solution)/shard_map/ppermute | solution.py:24
  137.0 3.5 %collective-permute-start.20 = (f32[1,128]{1,0:T(1,128)S(1)}, f32[1,128]{1,0:T(1,128)S(1)}, u32[]{:S(2)}, u32[]{:S(2)}) collective-permute-start(f32[1,128]{1,0:T(1,128)S(1)} %add.82), channel_id=1, source_target_pairs={{0,4},{4,0},{8,12},{12,8},{16,20},{20,16},{24,28},{28,24},{1,5},{5... | collective-permute-start | bytes 1544 | tf_op jit(solution)/shard_map/ppermute | solution.py:24
  140.5 3.5 %collective-permute-start.21 = (f32[1,128]{1,0:T(1,128)S(1)}, f32[1,128]{1,0:T(1,128)S(1)}, u32[]{:S(2)}, u32[]{:S(2)}) collective-permute-start(f32[1,128]{1,0:T(1,128)S(1)} %add.83), channel_id=1, source_target_pairs={{0,8},{4,12},{8,0},{12,4},{16,24},{20,28},{24,16},{28,20},{1,9},{5... | collective-permute-start | bytes 1544 | tf_op jit(solution)/shard_map/ppermute | solution.py:24
  144.1 4.4 %collective-permute-start.22 = (f32[1,128]{1,0:T(1,128)S(1)}, f32[1,128]{1,0:T(1,128)S(1)}, u32[]{:S(2)}, u32[]{:S(2)}) collective-permute-start(f32[1,128]{1,0:T(1,128)S(1)} %add.84), channel_id=1, source_target_pairs={{0,16},{4,20},{8,24},{12,28},{16,0},{20,4},{24,8},{28,12},{1,17},{... | collective-permute-start | bytes 1544 | tf_op jit(solution)/shard_map/ppermute | solution.py:24
Sparse Core Ops, SparseCore 0:
  52.6 43.8 reduce-scatter.1

commit v4 on v3

--- a/solution.py
+++ b/solution.py
@@ -25,12 +25,13 @@
 
 
 def total_over(value, dp_bits):
-    mask = 1
+    hops = [("tensor", 1)] + [("dp", 2**bit) for bit in range(dp_bits)]
+    mask = 2
     while mask < lax.axis_size("tensor"):
-        value = value + exchange(value, "tensor", mask)
+        hops.append(("tensor", mask))
         mask *= 2
-    for bit in range(dp_bits):
-        value = value + exchange(value, "dp", 2**bit)
+    for axis, mask in hops:
+        value = value + exchange(value, axis, mask)
     return value
 
 
@@ -95,31 +96,48 @@
     )(inputs, weight, targets)
 
 
-def input_grad_kernel(w, left, right, out):
+def input_grad_kernel(idx, w_send, w_keep, left, right, send, keep):
     half = left.shape[1]
-    total = 0.0
-    for at, error in ((0, left), (half, right)):
-        total = total + lax.dot_general(
-            w[:, at:at + half], error[...], (((1,), (1,)), ((), ())), preferred_element_type=jnp.float32
-        )
-    out[...] = total.astype(out.dtype)
-
-
-def input_grad_part(weight, left, right):
+    for w, out in ((w_send, send), (w_keep, keep)):
+        total = 0.0
+        for at, error in ((0, left), (half, right)):
+            total = total + lax.dot_general(
+                w[:, at:at + half],
+                error[...],
+                (((1,), (1,)), ((), ())),
+                preferred_element_type=jnp.float32,
+            )
+        out[0] = total.astype(out.dtype)
+
+
+def input_grad_part(idx, parts, weight, left, right):
     inner, columns = weight.shape
     rows = left.shape[0]
-    tile = math.gcd(inner, 1024)
-    whole = pl.BlockSpec(left.shape, lambda j: (0, 0), pipeline_mode=pl.Buffered(1))
+    block = inner // parts
+    tile = math.gcd(block, 512)
+    per_block = block // tile
+
+    def blocks_of(flip):
+        def at(j, idx):
+            parity = 1 - idx[PARITY] if flip else idx[PARITY]
+            return ((2 * (j // per_block) + parity) * per_block + j % per_block, 0)
+
+        return pl.BlockSpec((tile, columns), at)
+
+    out = pltpu.HBM((parts // 2, block, rows), jnp.bfloat16)
     return pl.pallas_call(
         input_grad_kernel,
-        grid=(inner // tile,),
-        in_specs=[pl.BlockSpec((tile, columns), lambda j: (j, 0)), whole, whole],
-        out_specs=pl.BlockSpec((tile, rows), lambda j: (j, 0)),
-        out_shape=pltpu.HBM((inner, rows), jnp.bfloat16),
-        compiler_params=pltpu.CompilerParams(vmem_limit_bytes=FULL_VMEM),
+        grid_spec=pltpu.PrefetchScalarGridSpec(
+            num_scalar_prefetch=1,
+            grid=(parts // 2 * per_block,),
+            in_specs=[blocks_of(True), blocks_of(False)] + [once(left.shape, (0, 0))] * 2,
+            out_specs=[pl.BlockSpec((1, tile, rows), lambda j, idx: (j // per_block, j % per_block, 0))] * 2,
+        ),
+        out_shape=[out, out],
+        compiler_params=pltpu.CompilerParams(vmem_limit_bytes=VMEM_LIMIT),
         cost_estimate=SMALL,
         name="input_grad_part",
-    )(weight, left, right)
+    )(idx, weight, weight, left, right)
 
 
 def fill(tile, xt, left, right):
@@ -191,7 +209,7 @@
             jax.ShapeDtypeStruct((1, LANES), jnp.float32),
             jax.ShapeDtypeStruct((steps * width, columns), jnp.bfloat16),
         ],
-        compiler_params=pltpu.CompilerParams(vmem_limit_bytes=FULL_VMEM),
+        compiler_params=pltpu.CompilerParams(vmem_limit_bytes=VMEM_LIMIT),
         cost_estimate=SMALL,
         name="own_gram",
     )(idx, inputs, left, right)
@@ -222,7 +240,7 @@
     width = tile.shape[0]
     acc[...] = jnp.zeros_like(acc)
     for q, other in enumerate(others):
-        fill(tile, other[QUAD - 2], left, right)
+        fill(tile, other[...], left, right)
 
         def load(first):
             at, there = strip_at(first), strip_at(idx[TILE + q] * width + first)
@@ -240,7 +258,7 @@
     return pl.BlockSpec(shape, lambda j, idx: at, pipeline_mode=pl.Buffered(1))
 
 
-PLACE, BIT, TILE = 0, 1, 2
+PLACE, BIT, PARITY, TILE = 0, 1, 2, 3
 
 
 def in_place(kernel, inputs, out_shape, scratch_shapes, name):
@@ -257,7 +275,7 @@
 
 
 def near_gram(idx, before, own, others, errors):
-    _, width, _ = others[0].shape
+    width = others[0].shape[-2]
     rows, columns = own.shape
     return in_place(
         functools.partial(near_kernel, len(others)),
@@ -275,7 +293,7 @@
 
 
 def far_gram(idx, before, own, others, left, right, grads):
-    _, width, _ = others[0].shape
+    width = others[0].shape[-2]
     rows, columns = own.shape
     return in_place(
         functools.partial(far_kernel, len(others)),
@@ -430,34 +448,69 @@
     slabs, ready = lax.optimization_barrier((slabs, inputs))
     arrived = [exchange(s, "dp", k + 1) for k, s in enumerate(slabs)]
 
+    def shared_far(piece):
+        pieces, mask = [piece], parts // 2
+        while mask > 1:
+            pieces = pieces + [exchange(p, "tensor", mask) for p in pieces]
+            mask //= 2
+        return pieces
+
+    def shared_near(pieces):
+        return pieces + [exchange(p, "tensor", 1) for p in pieces]
+
     left = forward(ready, in_hbm(weight), targets, 0, 2)
     arrived[:2], left, ready = lax.optimization_barrier((arrived[:2], left, ready))
     y_left, z_left = exchange(left, "dp", 1), exchange(left, "dp", 2)
     right = forward(ready, in_hbm(weight), targets, 1, 2)
     y_right, z_right = exchange(right, "dp", 1), exchange(right, "dp", 2)
-    others, sources = [jnp.stack(arrived)], [part]
+    near_inputs = shared_far(jnp.stack(arrived[:2]))
+    sources = [part]
     mask = parts // 2
     while mask:
         sources = sources + [s ^ mask for s in sources]
         mask //= 2
     bit = me >> 2 & 1
-    idx = jnp.stack([place, bit] + sources).astype(jnp.int32)
+    idx = jnp.stack([place, bit, part & 1] + sources).astype(jnp.int32)
     sums, own = own_gram(idx, in_hbm(inputs), left, right, width, block)
-    left, right, y_left, z_left, own = lax.optimization_barrier((left, right, y_left, z_left, own))
-    part_grad = input_grad_part(in_hbm(weight), left, right)
-    mask = parts // 2
-    while mask:
-        if mask == 1:
-            others, part_grad, y_right, z_right, z_left = lax.optimization_barrier(
-                (others, part_grad, y_right, z_right, z_left)
-            )
-        others = others + [exchange(o, "tensor", mask) for o in others]
-        mask //= 2
+    left, right, y_left, z_left, own, near_inputs, arrived[2] = lax.optimization_barrier(
+        (left, right, y_left, z_left, own, near_inputs, arrived[2])
+    )
+    near_inputs = shared_near(near_inputs)
+    send, keep = input_grad_part(idx, parts, in_hbm(weight), left, right)
+    send, keep, y_right, z_right, z_left, far_inputs = lax.optimization_barrier(
+        (send, keep, y_right, z_right, z_left, arrived[2])
+    )
+    away = exchange(send, "tensor", 1)
     far_left, far_right = exchange(z_left, "dp", 1), exchange(y_right, "dp", 2)
-
-    sums, grads = near_gram(idx, sums, own, others, (y_left, y_right, z_left, z_right))
-    sums, last = far_gram(idx, sums, own, others, far_left, far_right, grads)
+    far_inputs = shared_far(far_inputs)
+
+    def summed_terms(terms):
+        total = sum(term.astype(jnp.float32) for term in terms)
+        return total.astype(jnp.bfloat16)
+
+    def halved(terms, mask):
+        terms = [t.reshape(t.shape[0] // 2, 2, *t.shape[1:]) for t in terms]
+        high = (part & mask) // mask
+        sent = summed_terms([lax.dynamic_index_in_dim(t, 1 - high, 1, False) for t in terms])
+        return sent, [lax.dynamic_index_in_dim(t, high, 1, False) for t in terms]
+
+    send, terms = halved([keep, away], 2)
+    send, sums = lax.optimization_barrier((send, sums))
+
+    sums, grads = near_gram(idx, sums, own, near_inputs, (y_left, y_right, z_left, z_right))
+    far_inputs, sums = lax.optimization_barrier((far_inputs, sums))
+    far_inputs = shared_near(far_inputs)
+    sums, last = far_gram(idx, sums, own, far_inputs, far_left, far_right, grads)
     sums = total_over(sums, 2)
+    send, sums = lax.optimization_barrier((send, sums))
+    terms.append(exchange(send, "tensor", 2))
+    mask = 4
+    while mask < parts:
+        send, terms = halved(terms, mask)
+        terms.append(exchange(send, "tensor", mask))
+        mask *= 2
+    summed = summed_terms(terms)[0]
+
     half = columns // 2
 
     def merged_half(flip, h):
@@ -467,8 +520,6 @@
     received = [exchange(s, "dp", 4) for s in sent]
     _, sums = lax.optimization_barrier((sent, sums))
     kept = [merged_half(False, h) for h in range(2)]
-    summed = lax.psum_scatter(part_grad, "tensor", scatter_dimension=0, tiled=True)
-
     for level in range(2, depth):
         if level > 2:
             lower = bit == 0
@@ -484,7 +535,7 @@
             kept = [jnp.where(bit == 0, v[:, 0], v[:, 1]).reshape(-1, v.shape[-1]) for v in paired]
             sent = [jnp.where(bit == 0, v[:, 1], v[:, 0]).reshape(-1, v.shape[-1]) for v in paired]
             received = [exchange(s.astype(jnp.bfloat16), "dp", 2**level) for s in sent]
-        sums = jnp.zeros((1, LANES), jnp.float32)
+        sums, summed = lax.optimization_barrier((jnp.zeros((1, LANES), jnp.float32), summed))
         for a, b in zip(kept, received):
             sums = partial_sums(bit, sums, a, b)
         sums = total_over(sums, level + 1)

time: 159 us -> 146 us (0.918)
  waiting for transfers between devices: 70.3 us -> 55.9 us
  between operations: 14.2 us -> 0.84 us
  other arithmetic: 0.71 us -> 7.2 us
  starting transfers between devices: 24.2 us -> 29.5 us
  local copies, waits for them, and re-layouts: 5.51 us -> 8.16 us
    ppermute x23 -> x28, waiting for transfers between devices: 70.3 us -> 55.9 us  [exchange(): return lax.ppermute(value, axis, pairs)]
    ppermute x23 -> x28, starting transfers between devices: 24.2 us -> 29.5 us  [exchange(): return lax.ppermute(value, axis, pairs)]
    squeeze x0 -> x1, other arithmetic: none -> 2.93 us  [body(): summed = summed_terms(terms)[0]]
    convert_element_type x0 -> x1, other arithmetic: none -> 2.79 us  [summed_terms(): return total.astype(jnp.bfloat16)]
    unnamed x9 -> x19, local copies, waits for them, and re-layouts: 3.84 us -> 6.41 us
  transfers between devices with their start and end apart: 24 -> 28, of which waited for: 19 -> 18; matrix products, arithmetic and copies ran while one was open for 0% -> 5% of each run, Pallas kernels for 28% -> 25%
where the time goes in v4:
time: 146 us
  waiting for transfers between devices  55.9 us (38%)
  Pallas kernels  44.1 us (30%)
  starting transfers between devices  29.5 us (20%)
  local copies, waits for them, and re-layouts  8.16 us (6%)
  other arithmetic  7.2 us (5%)
    ppermute x28, waiting for transfers between devices, exchange(): return lax.ppermute(value, axis, pairs)  55.9 us
    ppermute x28, starting transfers between devices, exchange(): return lax.ppermute(value, axis, pairs)  29.5 us
    pallas_call x6, Pallas kernels, in_place(): pl.pallas_call(kernel, in_specs=[pl.BlockSpec(memory_space=m) for m, _ in...  18.7 us
    pallas_call x1, Pallas kernels, input_grad_part(): pl.pallas_call(input_grad_kernel, grid_spec=pltpu.PrefetchScalarGridSpec(...  8.67 us
    pallas_call x2, Pallas kernels, forward(): pl.pallas_call(forward_kernel, grid=(columns // tile,), in_specs=[pl.Bloc...  8.29 us
    unnamed x19, local copies, waits for them, and re-layouts  6.41 us
    pallas_call x1, Pallas kernels, own_gram(): pl.pallas_call(own_kernel, grid_spec=pltpu.PrefetchScalarGridSpec(num_sca...  4.67 us
    squeeze x1, other arithmetic, body(): summed = summed_terms(terms)[0]  2.93 us
  transfers between devices with their start and end apart: 28, of which 18 were waited for; matrix products, arithmetic and copies ran while one was open for 5% of the time, Pallas kernels for 25%

profile of v4, /device:TPU:0, one launch (start us, length us, event | category | flops | bytes accessed | tf_op | source)
XLA Modules:
  0.0 145.7 jit_solution(14778092837621167443)
XLA Ops:
  0.7 1.7 %constant_dynamic-slice_fusion = (bf16[512,256]{1,0:T(8,128)(2,1)S(1)}, bf16[512,256]{1,0:T(8,128)(2,1)S(1)}, bf16[512,256]{1,0:T(8,128)(2,1)S(1)}) fusion(bf16[512,4096]{1,0:T(8,128)(2,1)} %x.3, s32[]{:T(128)S(6)} %select_n.47, s32[]{:T(128)S(6)} %select_n.46, s32[]{:T(128)S(6)} %select_n.45), kind=kLoop, calls=%fused_computation.4 | loop fusion | bytes 1572876 | tf_op jit(solution)/shard_map/dynamic_slice | solution.py:445
  2.4 0.1 copy.10
  2.5 0.1 copy.11
  2.6 0.1 copy.12
  2.8 3.0 %collective-permute-start = (bf16[256,512]{1,0:T(8,128)(2,1)S(1)}, bf16[256,512]{1,0:T(8,128)(2,1)S(1)}, u32[]{:S(2)}, u32[]{:S(2)}) collective-permute-start(bf16[256,512]{1,0:T(8,128)(2,1)S(1)} %bitcast.18), channel_id=1, source_target_pairs={{0,4},{4,0},{8,12},{12,8},{16,20},{20,16},{24,28},{28,24},{1,5},{5... | collective-permute-start | bytes 786440 | tf_op jit(solution)/shard_map/ppermute | solution.py:24
  5.8 1.6 %collective-permute-start.1 = (bf16[256,512]{1,0:T(8,128)(2,1)S(1)}, bf16[256,512]{1,0:T(8,128)(2,1)S(1)}, u32[]{:S(2)}, u32[]{:S(2)}) collective-permute-start(bf16[256,512]{1,0:T(8,128)(2,1)S(1)} %bitcast.17), channel_id=1, source_target_pairs={{0,8},{4,12},{8,0},{12,4},{16,24},{20,28},{24,16},{28,20},{1,9},{5... | collective-permute-start | bytes 786440 | tf_op jit(solution)/shard_map/ppermute | solution.py:24
  7.4 2.2 %copy-done.2 = bf16[512,4096]{1,0:T(8,128)(2,1)S(1)} copy-done((bf16[512,4096]{1,0:T(8,128)(2,1)S(1)}, bf16[512,4096]{1,0:T(8,128)(2,1)}, u32[]{:S(2)}) %copy-start.2) | copy-done | bytes 4194328
  9.6 4.1 %forward.2.left = bf16[512,512]{1,0:T(8,128)(2,1)S(1)} custom-call(bf16[512,4096]{1,0:T(8,128)(2,1)S(1)} %copy-done.2, bf16[4096,1024]{1,0:T(8,128)(2,1)} %w_keep.1, bf16[512,1024]{1,0:T(8,128)(2,1)S(1)} %copy-done.5), custom_call_target="tpu_custom_call" | custom-call | flops 1 | bytes 1 | tf_op jit(solution)/shard_map/forward/pallas_call | solution.py:83
  13.8 1.3 collective-permute-done.1
  15.1 0.9 pad_maximum_fusion.refs_0_
  15.9 1.5 %collective-permute-start.4 = (bf16[2,256,512]{2,1,0:T(8,128)(2,1)}, bf16[2,256,512]{2,1,0:T(8,128)(2,1)}, u32[]{:S(2)}, u32[]{:S(2)}) collective-permute-start(bf16[2,256,512]{2,1,0:T(8,128)(2,1)} %pad_maximum_fusion.refs_0_), channel_id=1, source_target_pairs={{0,2},{1,3},{2,0},{3,1},{4,6},{5,7},{6,4},{7,5},{8,10},{9,11},{10,... | collective-permute-start | bytes 1572872 | tf_op jit(solution)/shard_map/ppermute | solution.py:24
  17.4 0.6 collective-permute-start.2
  18.0 1.6 %collective-permute-start.3 = (bf16[512,512]{1,0:T(8,128)(2,1)S(1)}, bf16[512,512]{1,0:T(8,128)(2,1)}, u32[]{:S(2)}, u32[]{:S(2)}) collective-permute-start(bf16[512,512]{1,0:T(8,128)(2,1)S(1)} %forward.2.left), channel_id=1, source_target_pairs={{0,8},{4,12},{8,0},{12,4},{16,24},{20,28},{24,16},{28,20},{1,9},{5... | collective-permute-start | bytes 1572872 | tf_op jit(solution)/shard_map/ppermute | solution.py:24
  19.6 4.1 %forward.3.right = bf16[512,512]{1,0:T(8,128)(2,1)S(1)} custom-call(bf16[512,4096]{1,0:T(8,128)(2,1)S(1)} %copy-done.2, bf16[4096,1024]{1,0:T(8,128)(2,1)} %w_keep.1, bf16[512,1024]{1,0:T(8,128)(2,1)S(1)} %copy-done.5), custom_call_target="tpu_custom_call" | custom-call | flops 1 | bytes 1 | tf_op jit(solution)/shard_map/forward/pallas_call | solution.py:83
  23.8 1.5 %collective-permute-start.6 = (bf16[512,512]{1,0:T(8,128)(2,1)S(1)}, bf16[512,512]{1,0:T(8,128)(2,1)}, u32[]{:S(2)}, u32[]{:S(2)}) collective-permute-start(bf16[512,512]{1,0:T(8,128)(2,1)S(1)} %forward.3.right), channel_id=1, source_target_pairs={{0,4},{4,0},{8,12},{12,8},{16,20},{20,16},{24,28},{28,24},{1,5},{5... | collective-permute-start | bytes 1572872 | tf_op jit(solution)/shard_map/ppermute | solution.py:24
  25.2 0.5 collective-permute-start.7
  25.8 4.7 %own_gram.1 = (f32[1,128]{1,0:T(1,128)S(1)}, bf16[1024,1024]{1,0:T(8,128)(2,1)S(1)}) custom-call(s32[7]{0:T(128)S(1)} %stack.40.idx, bf16[512,4096]{1,0:T(8,128)(2,1)} %x.3, bf16[512,512]{1,0:T(8,128)(2,1)S(1)} %forward.2.left, bf16[512,512]{1,0:T(8,128)(2,1)S(1)} %forward.3.right), custom_call_target="tpu_custom_call" | custom-call | flops 1 | bytes 1 | tf_op jit(solution)/shard_map/own_gram/pallas_call | solution.py:192
  30.5 1.9 %collective-permute-done.2.y_left = bf16[512,512]{1,0:T(8,128)(2,1)} collective-permute-done((bf16[512,512]{1,0:T(8,128)(2,1)S(1)}, bf16[512,512]{1,0:T(8,128)(2,1)}, u32[]{:S(2)}, u32[]{:S(2)}) %collective-permute-start.2) | collective-permute-done | bytes 524320 | tf_op jit(solution)/shard_map/ppermute | solution.py:24
  32.4 0.6 collective-permute-done.3.z_left
  33.0 8.7 %input_grad_part.1 = (bf16[2,1024,512]{2,1,0:T(8,128)(2,1)}, bf16[2,1024,512]{2,1,0:T(8,128)(2,1)}) custom-call(s32[7]{0:T(128)S(1)} %stack.40.idx, bf16[4096,1024]{1,0:T(8,128)(2,1)} %w_keep.1, bf16[4096,1024]{1,0:T(8,128)(2,1)} %w_keep.1, bf16[512,512]{1,0:T(8,128)(2,1)S(1)} %forward.2.left, bf16[512,512]{1,0:T(8,128)(2,1)S(1)} %forward.3.right), custom_call_target="tpu_custom_call" | custom-call | flops 1 | bytes 1 | tf_op jit(solution)/shard_map/input_grad_part/pallas_call | solution.py:128
  41.7 0.1 collective-permute-done.7.z_right
  41.8 0.5 collective-permute-start.10
  42.3 1.4 collective-permute-start.9
  43.8 1.5 %collective-permute-start.12 = (bf16[512,512]{1,0:T(8,128)(2,1)}, bf16[512,512]{1,0:T(8,128)(2,1)S(1)}, u32[]{:S(2)}, u32[]{:S(2)}) collective-permute-start(bf16[512,512]{1,0:T(8,128)(2,1)} %collective-permute-done.3.z_left), channel_id=1, source_target_pairs={{0,4},{4,0},{8,12},{12,8},{16,20},{20,16},{24,28},{28,24},{1,5},{5... | collective-permute-start | bytes 1572872 | tf_op jit(solution)/shard_map/ppermute | solution.py:24
  45.2 1.1 collective-permute-done.8
  46.3 1.6 %collective-permute-start.13 = (bf16[512,512]{1,0:T(8,128)(2,1)}, bf16[512,512]{1,0:T(8,128)(2,1)S(1)}, u32[]{:S(2)}, u32[]{:S(2)}) collective-permute-start(bf16[512,512]{1,0:T(8,128)(2,1)} %collective-permute-done.6.y_right), channel_id=1, source_target_pairs={{0,8},{4,12},{8,0},{12,4},{16,24},{20,28},{24,16},{28,20},{1,9},{5... | collective-permute-start | bytes 1572872 | tf_op jit(solution)/shard_map/ppermute | solution.py:24
  47.9 2.8 %add_convert_fusion.1 = bf16[1,1024,512]{2,1,0:T(8,128)(2,1)} fusion(bf16[2,1024,512]{2,1,0:T(8,128)(2,1)} %collective-permute-done.8, s32[]{:T(128)S(6)} %select_n.50, bf16[2,1024,512]{2,1,0:T(8,128)(2,1)} %get-tuple-element.58), kind=kLoop, calls=%fused_computation.1 | loop fusion | flops 2097152 | bytes 3145732 | tf_op jit(solution)/shard_map/convert_element_type | solution.py:489
  50.7 7.2 %near_gram.1 = (f32[1,128]{1,0:T(1,128)S(1)}, bf16[2,1024,1024]{2,1,0:T(8,128)(2,1)S(1)}) custom-call(s32[7]{0:T(128)S(1)} %stack.40.idx, f32[1,128]{1,0:T(1,128)S(1)} %get-tuple-element.63.before, bf16[1024,1024]{1,0:T(8,128)(2,1)S(1)} %get-tuple-element.64.own, bf16[512,512]{1,0:T(8,128)(2,1)} %collective-permute-done.2.y_left, ...), custom_call_target="tpu_custom_call" | custom-call | flops 1 | bytes 1 | tf_op jit(solution)/shard_map/near_gram/pallas_call | solution.py:265
  57.9 0.5 collective-permute-start.15
  58.4 2.0 %collective-permute-done.13.right = bf16[512,512]{1,0:T(8,128)(2,1)S(1)} collective-permute-done((bf16[512,512]{1,0:T(8,128)(2,1)}, bf16[512,512]{1,0:T(8,128)(2,1)S(1)}, u32[]{:S(2)}, u32[]{:S(2)}) %collective-permute-start.13) | collective-permute-done | bytes 524320 | tf_op jit(solution)/shard_map/ppermute | solution.py:24
  60.5 4.7 %far_gram.1 = (f32[1,128]{1,0:T(1,128)S(1)}, bf16[1024,1024]{1,0:T(8,128)(2,1)S(1)}) custom-call(s32[7]{0:T(128)S(1)} %stack.40.idx, f32[1,128]{1,0:T(1,128)S(1)} %get-tuple-element.72.before, bf16[512,512]{1,0:T(8,128)(2,1)S(1)} %collective-permute-done.12.left, bf16[512,512]{1,0:T(8,128)(2,1)S(1)} %collective-permute-done.13.right, ...), custom_call_target="tpu_custom_call" | custom-call | flops 1 | bytes 1 | tf_op jit(solution)/shard_map/far_gram/pallas_call | solution.py:265
  65.2 1.1 collective-permute-done.16
  66.4 1.5 %collective-permute-start.17 = (f32[1,128]{1,0:T(1,128)S(1)}, f32[1,128]{1,0:T(1,128)S(1)}, u32[]{:S(2)}, u32[]{:S(2)}) collective-permute-start(f32[1,128]{1,0:T(1,128)S(1)} %add.103), channel_id=1, source_target_pairs={{0,4},{4,0},{8,12},{12,8},{16,20},{20,16},{24,28},{28,24},{1,5},{5... | collective-permute-start | bytes 1544 | tf_op jit(solution)/shard_map/ppermute | solution.py:24
  67.8 2.1 %collective-permute-done.17 = f32[1,128]{1,0:T(1,128)S(1)} collective-permute-done((f32[1,128]{1,0:T(1,128)S(1)}, f32[1,128]{1,0:T(1,128)S(1)}, u32[]{:S(2)}, u32[]{:S(2)}) %collective-permute-start.17) | collective-permute-done | bytes 544 | tf_op jit(solution)/shard_map/ppermute | solution.py:24
  69.9 1.6 %collective-permute-start.18 = (f32[1,128]{1,0:T(1,128)S(1)}, f32[1,128]{1,0:T(1,128)S(1)}, u32[]{:S(2)}, u32[]{:S(2)}) collective-permute-start(f32[1,128]{1,0:T(1,128)S(1)} %add.104), channel_id=1, source_target_pairs={{0,8},{4,12},{8,0},{12,4},{16,24},{20,28},{24,16},{28,20},{1,9},{5... | collective-permute-start | bytes 1544 | tf_op jit(solution)/shard_map/ppermute | solution.py:24
  71.5 2.0 %collective-permute-done.18 = f32[1,128]{1,0:T(1,128)S(1)} collective-permute-done((f32[1,128]{1,0:T(1,128)S(1)}, f32[1,128]{1,0:T(1,128)S(1)}, u32[]{:S(2)}, u32[]{:S(2)}) %collective-permute-start.18) | collective-permute-done | bytes 544 | tf_op jit(solution)/shard_map/ppermute | solution.py:24
  73.5 1.5 collective-permute-start.19
  74.9 2.1 %collective-permute-done.19 = f32[1,128]{1,0:T(1,128)S(1)} collective-permute-done((f32[1,128]{1,0:T(1,128)S(1)}, f32[1,128]{1,0:T(1,128)S(1)}, u32[]{:S(2)}, u32[]{:S(2)}) %collective-permute-start.19) | collective-permute-done | bytes 544 | tf_op jit(solution)/shard_map/ppermute | solution.py:24
  77.0 1.5 collective-permute-start.20
  78.4 2.1 %merge.4 = bf16[512,512]{1,0:T(8,128)(2,1)} custom-call(s32[7]{0:T(128)S(1)} %stack.40.idx, f32[1,128]{1,0:T(1,128)S(1)} %add.106.sums, bf16[1024,1024]{1,0:T(8,128)(2,1)S(1)} %get-tuple-element.64.own, bf16[2,1024,1024]{2,1,0:T(8,128)(2,1)S(1)} %get-tuple-element.73.grads, bf16[1024,1024]{1,0:T(8,128)(2,1)S(1)} %get-tuple-element.81.last), custom_call_target="tpu_custom_call" | custom-call | flops 1 | bytes 1 | tf_op jit(solution)/shard_map/merge/pallas_call | solution.py:265
  80.5 2.6 %collective-permute-start.21 = (bf16[512,512]{1,0:T(8,128)(2,1)}, bf16[512,512]{1,0:T(8,128)(2,1)S(1)}, u32[]{:S(2)}, u32[]{:S(2)}) collective-permute-start(bf16[512,512]{1,0:T(8,128)(2,1)} %merge.4), channel_id=1, source_target_pairs={{0,16},{4,20},{8,24},{12,28},{16,0},{20,4},{24,8},{28,12},{1,17},{... | collective-permute-start | bytes 1572872 | tf_op jit(solution)/shard_map/ppermute | solution.py:24
  83.1 2.1 %merge.5 = bf16[512,512]{1,0:T(8,128)(2,1)} custom-call(s32[7]{0:T(128)S(1)} %stack.40.idx, f32[1,128]{1,0:T(1,128)S(1)} %add.106.sums, bf16[1024,1024]{1,0:T(8,128)(2,1)S(1)} %get-tuple-element.64.own, bf16[2,1024,1024]{2,1,0:T(8,128)(2,1)S(1)} %get-tuple-element.73.grads, bf16[1024,1024]{1,0:T(8,128)(2,1)S(1)} %get-tuple-element.81.last), custom_call_target="tpu_custom_call" | custom-call | flops 1 | bytes 1 | tf_op jit(solution)/shard_map/merge/pallas_call | solution.py:265
  85.2 0.3 collective-permute-start.22
  85.6 2.2 %copy-done.1 = bf16[2,1024,1024]{2,1,0:T(8,128)(2,1)S(1)} copy-done((bf16[2,1024,1024]{2,1,0:T(8,128)(2,1)S(1)}, bf16[2,1024,1024]{2,1,0:T(8,128)(2,1)}, u32[]{:S(2)}) %copy-start.1) | copy-done | bytes 4194328
  87.8 1.6 %copy-done.4 = bf16[1024,1024]{1,0:T(8,128)(2,1)S(1)} copy-done((bf16[1024,1024]{1,0:T(8,128)(2,1)S(1)}, bf16[1024,1024]{1,0:T(8,128)(2,1)}, u32[]{:S(2)}) %copy-start.4) | copy-done | bytes 2097176
  89.4 1.3 merge.7.kept.kept_1
  90.7 1.3 merge.6.kept.kept_0
  92.0 7.2 %collective-permute-done.20 = bf16[1,1024,512]{2,1,0:T(8,128)(2,1)} collective-permute-done((bf16[1,1024,512]{2,1,0:T(8,128)(2,1)}, bf16[1,1024,512]{2,1,0:T(8,128)(2,1)}, u32[]{:S(2)}, u32[]{:S(2)}) %collective-permute-start.20) | collective-permute-done | bytes 1048608 | tf_op jit(solution)/shard_map/ppermute | solution.py:24
  99.1 2.9 %fusion = bf16[1024,512]{1,0:T(8,128)(2,1)} fusion(bf16[1,1024,512]{2,1,0:T(8,128)(2,1)} %collective-permute-done.20, bf16[2,1024,512]{2,1,0:T(8,128)(2,1)} %collective-permute-done.8, s32[]{:T(128)S(6)} %select_n.49, bf16[2,1024,512]{2,1,0:T(8,128)(2,1)S(1)} %copy-done.7), kind=kLoop, calls=%fused_computation.2 | loop fusion | flops 3145728 | bytes 4194308 | tf_op jit(solution)/shard_map/squeeze | solution.py:512
  102.1 13.6 %collective-permute-done.21.received.received_0 = bf16[512,512]{1,0:T(8,128)(2,1)S(1)} collective-permute-done((bf16[512,512]{1,0:T(8,128)(2,1)}, bf16[512,512]{1,0:T(8,128)(2,1)S(1)}, u32[]{:S(2)}, u32[]{:S(2)}) %collective-permute-start.21) | collective-permute-done | bytes 524320 | tf_op jit(solution)/shard_map/ppermute | solution.py:24
  115.6 0.5 partial_sums.2.before
  116.1 9.5 %collective-permute-done.22.received.received_1 = bf16[512,512]{1,0:T(8,128)(2,1)S(1)} collective-permute-done((bf16[512,512]{1,0:T(8,128)(2,1)}, bf16[512,512]{1,0:T(8,128)(2,1)S(1)}, u32[]{:S(2)}, u32[]{:S(2)}) %collective-permute-start.22) | collective-permute-done | bytes 524320 | tf_op jit(solution)/shard_map/ppermute | solution.py:24
  125.7 0.5 partial_sums.3
  126.2 1.1 collective-permute-done.23
  127.3 1.5 %collective-permute-start.24 = (f32[1,128]{1,0:T(1,128)S(1)}, f32[1,128]{1,0:T(1,128)S(1)}, u32[]{:S(2)}, u32[]{:S(2)}) collective-permute-start(f32[1,128]{1,0:T(1,128)S(1)} %add.108), channel_id=1, source_target_pairs={{0,4},{4,0},{8,12},{12,8},{16,20},{20,16},{24,28},{28,24},{1,5},{5... | collective-permute-start | bytes 1544 | tf_op jit(solution)/shard_map/ppermute | solution.py:24
  128.7 2.1 %collective-permute-done.24 = f32[1,128]{1,0:T(1,128)S(1)} collective-permute-done((f32[1,128]{1,0:T(1,128)S(1)}, f32[1,128]{1,0:T(1,128)S(1)}, u32[]{:S(2)}, u32[]{:S(2)}) %collective-permute-start.24) | collective-permute-done | bytes 544 | tf_op jit(solution)/shard_map/ppermute | solution.py:24
  130.8 0.8 collective-permute-start.25
  131.6 2.8 %collective-permute-done.25 = f32[1,128]{1,0:T(1,128)S(1)} collective-permute-done((f32[1,128]{1,0:T(1,128)S(1)}, f32[1,128]{1,0:T(1,128)S(1)}, u32[]{:S(2)}, u32[]{:S(2)}) %collective-permute-start.25) | collective-permute-done | bytes 544 | tf_op jit(solution)/shard_map/ppermute | solution.py:24
  134.4 2.0 %collective-permute-start.26 = (f32[1,128]{1,0:T(1,128)S(1)}, f32[1,128]{1,0:T(1,128)S(1)}, u32[]{:S(2)}, u32[]{:S(2)}) collective-permute-start(f32[1,128]{1,0:T(1,128)S(1)} %add.110), channel_id=1, source_target_pairs={{0,16},{4,20},{8,24},{12,28},{16,0},{20,4},{24,8},{28,12},{1,17},{... | collective-permute-start | bytes 1544 | tf_op jit(solution)/shard_map/ppermute | solution.py:24
  136.4 2.4 %collective-permute-done.26 = f32[1,128]{1,0:T(1,128)S(1)} collective-permute-done((f32[1,128]{1,0:T(1,128)S(1)}, f32[1,128]{1,0:T(1,128)S(1)}, u32[]{:S(2)}, u32[]{:S(2)}) %collective-permute-start.26) | collective-permute-done | bytes 544 | tf_op jit(solution)/shard_map/ppermute | solution.py:24
  138.8 0.6 collective-permute-start.27
  139.4 3.0 %collective-permute-done.27 = f32[1,128]{1,0:T(1,128)S(1)} collective-permute-done((f32[1,128]{1,0:T(1,128)S(1)}, f32[1,128]{1,0:T(1,128)S(1)}, u32[]{:S(2)}, u32[]{:S(2)}) %collective-permute-start.27) | collective-permute-done | bytes 544 | tf_op jit(solution)/shard_map/ppermute | solution.py:24
  142.4 0.6 multiply_bitcast_fusion
  142.9 2.8 %update.1 = f32[512,1024]{1,0:T(8,128)} custom-call(s32[1]{0:T(128)} %bitcast.1.first_at.bit, f32[1,128]{1,0:T(1,128)S(1)} %add.112.sums, f32[512,1024]{1,0:T(8,128)S(1)} %copy-done.6, bf16[512,512]{1,0:T(8,128)(2,1)S(1)} %merge.6.kept.kept_0, bf16[512,512]{1,0:T(8,128)(2,1)S(1)} %merge.7.kept.kept_1, ...), custom_call_target="tpu_custom_call" | custom-call | flops 1 | bytes 1 | tf_op jit(solution)/shard_map/update/pallas_call | solution.py:415
  (40 shorter events, 0.3 us)
Async XLA Ops:
  0.6 6.8 %copy-start.5 = (bf16[512,1024]{1,0:T(8,128)(2,1)S(1)}, bf16[512,1024]{1,0:T(8,128)(2,1)}, u32[]{:S(2)}) copy-start(bf16[512,1024]{1,0:T(8,128)(2,1)} %targets.3) | copy-start | bytes 3145732
  2.8 11.0 %collective-permute-start = (bf16[256,512]{1,0:T(8,128)(2,1)S(1)}, bf16[256,512]{1,0:T(8,128)(2,1)S(1)}, u32[]{:S(2)}, u32[]{:S(2)}) collective-permute-start(bf16[256,512]{1,0:T(8,128)(2,1)S(1)} %bitcast.18), channel_id=1, source_target_pairs={{0,4},{4,0},{8,12},{12,8},{16,20},{20,16},{24,28},{28,24},{1,5},{5... | collective-permute-start | bytes 786440 | tf_op jit(solution)/shard_map/ppermute | solution.py:24
  5.8 9.2 %collective-permute-start.1 = (bf16[256,512]{1,0:T(8,128)(2,1)S(1)}, bf16[256,512]{1,0:T(8,128)(2,1)S(1)}, u32[]{:S(2)}, u32[]{:S(2)}) collective-permute-start(bf16[256,512]{1,0:T(8,128)(2,1)S(1)} %bitcast.17), channel_id=1, source_target_pairs={{0,8},{4,12},{8,0},{12,4},{16,24},{20,28},{24,16},{28,20},{1,9},{5... | collective-permute-start | bytes 786440 | tf_op jit(solution)/shard_map/ppermute | solution.py:24
  7.4 17.8 %collective-permute-start.5 = (bf16[256,512]{1,0:T(8,128)(2,1)S(1)}, bf16[256,512]{1,0:T(8,128)(2,1)S(1)}, u32[]{:S(2)}, u32[]{:S(2)}) collective-permute-start(bf16[256,512]{1,0:T(8,128)(2,1)S(1)} %bitcast.16), channel_id=1, source_target_pairs={{0,12},{4,8},{8,4},{12,0},{16,28},{20,24},{24,20},{28,16},{1,13},{... | collective-permute-start | bytes 786440 | tf_op jit(solution)/shard_map/ppermute | solution.py:24
  7.4 2.2 %copy-start.2 = (bf16[512,4096]{1,0:T(8,128)(2,1)S(1)}, bf16[512,4096]{1,0:T(8,128)(2,1)}, u32[]{:S(2)}) copy-start(bf16[512,4096]{1,0:T(8,128)(2,1)} %x.3) | copy-start | bytes 12582916
  15.9 14.5 %collective-permute-start.4 = (bf16[2,256,512]{2,1,0:T(8,128)(2,1)}, bf16[2,256,512]{2,1,0:T(8,128)(2,1)}, u32[]{:S(2)}, u32[]{:S(2)}) collective-permute-start(bf16[2,256,512]{2,1,0:T(8,128)(2,1)} %pad_maximum_fusion.refs_0_), channel_id=1, source_target_pairs={{0,2},{1,3},{2,0},{3,1},{4,6},{5,7},{6,4},{7,5},{8,10},{9,11},{10,... | collective-permute-start | bytes 1572872 | tf_op jit(solution)/shard_map/ppermute | solution.py:24
  17.4 15.0 %collective-permute-start.2 = (bf16[512,512]{1,0:T(8,128)(2,1)S(1)}, bf16[512,512]{1,0:T(8,128)(2,1)}, u32[]{:S(2)}, u32[]{:S(2)}) collective-permute-start(bf16[512,512]{1,0:T(8,128)(2,1)S(1)} %forward.2.left), channel_id=1, source_target_pairs={{0,4},{4,0},{8,12},{12,8},{16,20},{20,16},{24,28},{28,24},{1,5},{5... | collective-permute-start | bytes 1572872 | tf_op jit(solution)/shard_map/ppermute | solution.py:24
  18.0 15.0 %collective-permute-start.3 = (bf16[512,512]{1,0:T(8,128)(2,1)S(1)}, bf16[512,512]{1,0:T(8,128)(2,1)}, u32[]{:S(2)}, u32[]{:S(2)}) collective-permute-start(bf16[512,512]{1,0:T(8,128)(2,1)S(1)} %forward.2.left), channel_id=1, source_target_pairs={{0,8},{4,12},{8,0},{12,4},{16,24},{20,28},{24,16},{28,20},{1,9},{5... | collective-permute-start | bytes 1572872 | tf_op jit(solution)/shard_map/ppermute | solution.py:24
  23.8 17.9 %collective-permute-start.6 = (bf16[512,512]{1,0:T(8,128)(2,1)S(1)}, bf16[512,512]{1,0:T(8,128)(2,1)}, u32[]{:S(2)}, u32[]{:S(2)}) collective-permute-start(bf16[512,512]{1,0:T(8,128)(2,1)S(1)} %forward.3.right), channel_id=1, source_target_pairs={{0,4},{4,0},{8,12},{12,8},{16,20},{20,16},{24,28},{28,24},{1,5},{5... | collective-permute-start | bytes 1572872 | tf_op jit(solution)/shard_map/ppermute | solution.py:24
  25.2 16.6 %collective-permute-start.7 = (bf16[512,512]{1,0:T(8,128)(2,1)S(1)}, bf16[512,512]{1,0:T(8,128)(2,1)}, u32[]{:S(2)}, u32[]{:S(2)}) collective-permute-start(bf16[512,512]{1,0:T(8,128)(2,1)S(1)} %forward.3.right), channel_id=1, source_target_pairs={{0,8},{4,12},{8,0},{12,4},{16,24},{20,28},{24,16},{28,20},{1,9},{5... | collective-permute-start | bytes 1572872 | tf_op jit(solution)/shard_map/ppermute | solution.py:24
  41.8 4.5 %collective-permute-start.8 = (bf16[2,1024,512]{2,1,0:T(8,128)(2,1)}, bf16[2,1024,512]{2,1,0:T(8,128)(2,1)}, u32[]{:S(2)}, u32[]{:S(2)}) collective-permute-start(bf16[2,1024,512]{2,1,0:T(8,128)(2,1)} %get-tuple-element.59), channel_id=1, source_target_pairs={{0,1},{1,0},{2,3},{3,2},{4,5},{5,4},{6,7},{7,6},{8,9},{9,8},{10,11... | collective-permute-start | bytes 6291464 | tf_op jit(solution)/shard_map/ppermute | solution.py:24
  41.8 8.9 %collective-permute-start.10 = (bf16[2,256,512]{2,1,0:T(8,128)(2,1)}, bf16[2,256,512]{2,1,0:T(8,128)(2,1)}, u32[]{:S(2)}, u32[]{:S(2)}) collective-permute-start(bf16[2,256,512]{2,1,0:T(8,128)(2,1)} %pad_maximum_fusion.refs_0_), channel_id=1, source_target_pairs={{0,1},{1,0},{2,3},{3,2},{4,5},{5,4},{6,7},{7,6},{8,9},{9,8},{10,11... | collective-permute-start | bytes 1572872 | tf_op jit(solution)/shard_map/ppermute | solution.py:24
  42.3 8.4 %collective-permute-start.11 = (bf16[2,256,512]{2,1,0:T(8,128)(2,1)}, bf16[2,256,512]{2,1,0:T(8,128)(2,1)}, u32[]{:S(2)}, u32[]{:S(2)}) collective-permute-start(bf16[2,256,512]{2,1,0:T(8,128)(2,1)} %collective-permute-done.4.refs_1_), channel_id=1, source_target_pairs={{0,1},{1,0},{2,3},{3,2},{4,5},{5,4},{6,7},{7,6},{8,9},{9,8},{10,11... | collective-permute-start | bytes 1572872 | tf_op jit(solution)/shard_map/ppermute | solution.py:24
  42.3 15.5 %collective-permute-start.9 = (bf16[256,512]{1,0:T(8,128)(2,1)S(1)}, bf16[256,512]{1,0:T(8,128)(2,1)}, u32[]{:S(2)}, u32[]{:S(2)}) collective-permute-start(bf16[256,512]{1,0:T(8,128)(2,1)S(1)} %collective-permute-done.5.refs_0_), channel_id=1, source_target_pairs={{0,2},{1,3},{2,0},{3,1},{4,6},{5,7},{6,4},{7,5},{8,10},{9,11},{10,... | collective-permute-start | bytes 786440 | tf_op jit(solution)/shard_map/ppermute | solution.py:24
  43.8 14.7 %collective-permute-start.12 = (bf16[512,512]{1,0:T(8,128)(2,1)}, bf16[512,512]{1,0:T(8,128)(2,1)S(1)}, u32[]{:S(2)}, u32[]{:S(2)}) collective-permute-start(bf16[512,512]{1,0:T(8,128)(2,1)} %collective-permute-done.3.z_left), channel_id=1, source_target_pairs={{0,4},{4,0},{8,12},{12,8},{16,20},{20,16},{24,28},{28,24},{1,5},{5... | collective-permute-start | bytes 1572872 | tf_op jit(solution)/shard_map/ppermute | solution.py:24
  46.3 14.2 %collective-permute-start.13 = (bf16[512,512]{1,0:T(8,128)(2,1)}, bf16[512,512]{1,0:T(8,128)(2,1)S(1)}, u32[]{:S(2)}, u32[]{:S(2)}) collective-permute-start(bf16[512,512]{1,0:T(8,128)(2,1)} %collective-permute-done.6.y_right), channel_id=1, source_target_pairs={{0,8},{4,12},{8,0},{12,4},{16,24},{20,28},{24,16},{28,20},{1,9},{5... | collective-permute-start | bytes 1572872 | tf_op jit(solution)/shard_map/ppermute | solution.py:24
  57.8 25.3 %copy-start = (bf16[2,1024,1024]{2,1,0:T(8,128)(2,1)}, bf16[2,1024,1024]{2,1,0:T(8,128)(2,1)S(1)}, u32[]{:S(2)}) copy-start(bf16[2,1024,1024]{2,1,0:T(8,128)(2,1)S(1)} %get-tuple-element.73.grads) | copy-start | bytes 12582916
  57.9 2.6 %collective-permute-start.14 = (bf16[256,512]{1,0:T(8,128)(2,1)S(1)}, bf16[256,512]{1,0:T(8,128)(2,1)S(1)}, u32[]{:S(2)}, u32[]{:S(2)}) collective-permute-start(bf16[256,512]{1,0:T(8,128)(2,1)S(1)} %collective-permute-done.5.refs_0_), channel_id=1, source_target_pairs={{0,1},{1,0},{2,3},{3,2},{4,5},{5,4},{6,7},{7,6},{8,9},{9,8},{10,11... | collective-permute-start | bytes 786440 | tf_op jit(solution)/shard_map/ppermute | solution.py:24
  57.9 2.5 %collective-permute-start.15 = (bf16[256,512]{1,0:T(8,128)(2,1)}, bf16[256,512]{1,0:T(8,128)(2,1)S(1)}, u32[]{:S(2)}, u32[]{:S(2)}) collective-permute-start(bf16[256,512]{1,0:T(8,128)(2,1)} %collective-permute-done.9.refs_1_), channel_id=1, source_target_pairs={{0,1},{1,0},{2,3},{3,2},{4,5},{5,4},{6,7},{7,6},{8,9},{9,8},{10,11... | collective-permute-start | bytes 786440 | tf_op jit(solution)/shard_map/ppermute | solution.py:24
  65.2 17.9 %copy-start.3 = (bf16[1024,1024]{1,0:T(8,128)(2,1)}, bf16[1024,1024]{1,0:T(8,128)(2,1)S(1)}, u32[]{:S(2)}) copy-start(bf16[1024,1024]{1,0:T(8,128)(2,1)S(1)} %get-tuple-element.81.last) | copy-start | bytes 6291460
  65.2 1.1 collective-permute-start.16
  66.4 3.5 %collective-permute-start.17 = (f32[1,128]{1,0:T(1,128)S(1)}, f32[1,128]{1,0:T(1,128)S(1)}, u32[]{:S(2)}, u32[]{:S(2)}) collective-permute-start(f32[1,128]{1,0:T(1,128)S(1)} %add.103), channel_id=1, source_target_pairs={{0,4},{4,0},{8,12},{12,8},{16,20},{20,16},{24,28},{28,24},{1,5},{5... | collective-permute-start | bytes 1544 | tf_op jit(solution)/shard_map/ppermute | solution.py:24
  69.9 3.5 %collective-permute-start.18 = (f32[1,128]{1,0:T(1,128)S(1)}, f32[1,128]{1,0:T(1,128)S(1)}, u32[]{:S(2)}, u32[]{:S(2)}) collective-permute-start(f32[1,128]{1,0:T(1,128)S(1)} %add.104), channel_id=1, source_target_pairs={{0,8},{4,12},{8,0},{12,4},{16,24},{20,28},{24,16},{28,20},{1,9},{5... | collective-permute-start | bytes 1544 | tf_op jit(solution)/shard_map/ppermute | solution.py:24
  73.5 3.5 %collective-permute-start.19 = (f32[1,128]{1,0:T(1,128)S(1)}, f32[1,128]{1,0:T(1,128)S(1)}, u32[]{:S(2)}, u32[]{:S(2)}) collective-permute-start(f32[1,128]{1,0:T(1,128)S(1)} %add.105), channel_id=1, source_target_pairs={{0,2},{1,3},{2,0},{3,1},{4,6},{5,7},{6,4},{7,5},{8,10},{9,11},{10,... | collective-permute-start | bytes 1544 | tf_op jit(solution)/shard_map/ppermute | solution.py:24
  77.0 22.1 %collective-permute-start.20 = (bf16[1,1024,512]{2,1,0:T(8,128)(2,1)}, bf16[1,1024,512]{2,1,0:T(8,128)(2,1)}, u32[]{:S(2)}, u32[]{:S(2)}) collective-permute-start(bf16[1,1024,512]{2,1,0:T(8,128)(2,1)} %add_convert_fusion.1), channel_id=1, source_target_pairs={{0,2},{1,3},{2,0},{3,1},{4,6},{5,7},{6,4},{7,5},{8,10},{9,11},{10,... | collective-permute-start | bytes 3145736 | tf_op jit(solution)/shard_map/ppermute | solution.py:24
  80.5 35.1 %collective-permute-start.21 = (bf16[512,512]{1,0:T(8,128)(2,1)}, bf16[512,512]{1,0:T(8,128)(2,1)S(1)}, u32[]{:S(2)}, u32[]{:S(2)}) collective-permute-start(bf16[512,512]{1,0:T(8,128)(2,1)} %merge.4), channel_id=1, source_target_pairs={{0,16},{4,20},{8,24},{12,28},{16,0},{20,4},{24,8},{28,12},{1,17},{... | collective-permute-start | bytes 1572872 | tf_op jit(solution)/shard_map/ppermute | solution.py:24
  85.2 40.4 %collective-permute-start.22 = (bf16[512,512]{1,0:T(8,128)(2,1)}, bf16[512,512]{1,0:T(8,128)(2,1)S(1)}, u32[]{:S(2)}, u32[]{:S(2)}) collective-permute-start(bf16[512,512]{1,0:T(8,128)(2,1)} %merge.5), channel_id=1, source_target_pairs={{0,16},{4,20},{8,24},{12,28},{16,0},{20,4},{24,8},{28,12},{1,17},{... | collective-permute-start | bytes 1572872 | tf_op jit(solution)/shard_map/ppermute | solution.py:24
  85.6 2.2 %copy-start.1 = (bf16[2,1024,1024]{2,1,0:T(8,128)(2,1)S(1)}, bf16[2,1024,1024]{2,1,0:T(8,128)(2,1)}, u32[]{:S(2)}) copy-start(bf16[2,1024,1024]{2,1,0:T(8,128)(2,1)} %copy-done) | copy-start | bytes 12582916
  87.8 1.6 %copy-start.4 = (bf16[1024,1024]{1,0:T(8,128)(2,1)S(1)}, bf16[1024,1024]{1,0:T(8,128)(2,1)}, u32[]{:S(2)}) copy-start(bf16[1024,1024]{1,0:T(8,128)(2,1)} %copy-done.3) | copy-start | bytes 6291460
  90.7 8.5 %copy-start.7 = (bf16[2,1024,512]{2,1,0:T(8,128)(2,1)S(1)}, bf16[2,1024,512]{2,1,0:T(8,128)(2,1)}, u32[]{:S(2)}) copy-start(bf16[2,1024,512]{2,1,0:T(8,128)(2,1)} %get-tuple-element.58) | copy-start | bytes 6291460
  102.1 40.9 %copy-start.6 = (f32[512,1024]{1,0:T(8,128)S(1)}, f32[512,1024]{1,0:T(8,128)}, u32[]{:S(2)}) copy-start(f32[512,1024]{1,0:T(8,128)} %momentum.1) | copy-start | bytes 6291460
  126.1 1.1 collective-permute-start.23
  127.3 3.5 %collective-permute-start.24 = (f32[1,128]{1,0:T(1,128)S(1)}, f32[1,128]{1,0:T(1,128)S(1)}, u32[]{:S(2)}, u32[]{:S(2)}) collective-permute-start(f32[1,128]{1,0:T(1,128)S(1)} %add.108), channel_id=1, source_target_pairs={{0,4},{4,0},{8,12},{12,8},{16,20},{20,16},{24,28},{28,24},{1,5},{5... | collective-permute-start | bytes 1544 | tf_op jit(solution)/shard_map/ppermute | solution.py:24
  130.8 3.5 %collective-permute-start.25 = (f32[1,128]{1,0:T(1,128)S(1)}, f32[1,128]{1,0:T(1,128)S(1)}, u32[]{:S(2)}, u32[]{:S(2)}) collective-permute-start(f32[1,128]{1,0:T(1,128)S(1)} %add.109), channel_id=1, source_target_pairs={{0,8},{4,12},{8,0},{12,4},{16,24},{20,28},{24,16},{28,20},{1,9},{5... | collective-permute-start | bytes 1544 | tf_op jit(solution)/shard_map/ppermute | solution.py:24
  134.4 4.4 %collective-permute-start.26 = (f32[1,128]{1,0:T(1,128)S(1)}, f32[1,128]{1,0:T(1,128)S(1)}, u32[]{:S(2)}, u32[]{:S(2)}) collective-permute-start(f32[1,128]{1,0:T(1,128)S(1)} %add.110), channel_id=1, source_target_pairs={{0,16},{4,20},{8,24},{12,28},{16,0},{20,4},{24,8},{28,12},{1,17},{... | collective-permute-start | bytes 1544 | tf_op jit(solution)/shard_map/ppermute | solution.py:24
  138.8 3.5 %collective-permute-start.27 = (f32[1,128]{1,0:T(1,128)S(1)}, f32[1,128]{1,0:T(1,128)S(1)}, u32[]{:S(2)}, u32[]{:S(2)}) collective-permute-start(f32[1,128]{1,0:T(1,128)S(1)} %add.111), channel_id=1, source_target_pairs={{0,2},{1,3},{2,0},{3,1},{4,6},{5,7},{6,4},{7,5},{8,10},{9,11},{10,... | collective-permute-start | bytes 1544 | tf_op jit(solution)/shard_map/ppermute | solution.py:24

commit v5 on v4

--- a/solution.py
+++ b/solution.py
@@ -12,7 +12,8 @@
 LANES = 128
 SMALL = pl.CostEstimate(flops=1, bytes_accessed=1, transcendentals=0)
 VMEM_LIMIT = 18 * 2**20
-FULL_VMEM = 44 * 2**20
+IN_PLACE_VMEM = 8 * 2**20
+FULL_VMEM = 20 * 2**20
 
 
 def in_hbm(value):
@@ -96,18 +97,16 @@
     )(inputs, weight, targets)
 
 
-def input_grad_kernel(idx, w_send, w_keep, left, right, send, keep):
+def input_grad_kernel(idx, w_send, w_keep, left, right, send, keep, turned):
     half = left.shape[1]
+
+    @pl.when(pl.program_id(0) == 0)
+    def _():
+        turned[:half] = left[...].T
+        turned[half:] = right[...].T
+
     for w, out in ((w_send, send), (w_keep, keep)):
-        total = 0.0
-        for at, error in ((0, left), (half, right)):
-            total = total + lax.dot_general(
-                w[:, at:at + half],
-                error[...],
-                (((1,), (1,)), ((), ())),
-                preferred_element_type=jnp.float32,
-            )
-        out[0] = total.astype(out.dtype)
+        out[0] = dot(w[...], turned[...]).astype(out.dtype)
 
 
 def input_grad_part(idx, parts, weight, left, right):
@@ -132,6 +131,7 @@
             grid=(parts // 2 * per_block,),
             in_specs=[blocks_of(True), blocks_of(False)] + [once(left.shape, (0, 0))] * 2,
             out_specs=[pl.BlockSpec((1, tile, rows), lambda j, idx: (j // per_block, j % per_block, 0))] * 2,
+            scratch_shapes=[pltpu.VMEM((columns, rows), jnp.bfloat16)],
         ),
         out_shape=[out, out],
         compiler_params=pltpu.CompilerParams(vmem_limit_bytes=VMEM_LIMIT),
@@ -268,7 +268,7 @@
         out_specs=[pl.BlockSpec(memory_space=pltpu.VMEM)] * len(out_shape),
         out_shape=out_shape,
         scratch_shapes=scratch_shapes,
-        compiler_params=pltpu.CompilerParams(vmem_limit_bytes=VMEM_LIMIT),
+        compiler_params=pltpu.CompilerParams(vmem_limit_bytes=IN_PLACE_VMEM),
         cost_estimate=SMALL,
         name=name,
     )(*[v for _, v in inputs])
@@ -395,32 +395,40 @@
     )(bit.reshape(1).astype(jnp.int32), before, kept, received)
 
 
-def update_kernel(bit, sums, momentum, kept_0, kept_1, received_0, received_1, out):
+def update_kernel(norm, bit, sums, momentum, kept_0, kept_1, received_0, received_1, out, norms):
     half = kept_0.shape[1]
     lower = bit[0] == 0
     lower_factor = 1.0 - sums[0, 0] / (2.0 * sums[0, 1])
     upper_factor = 1.0 - sums[0, 0] / (2.0 * sums[0, 2])
     factor = jnp.where(lower, lower_factor, upper_factor)
     other = jnp.where(lower, upper_factor, lower_factor)
-    for at, a, b in ((slice(0, half), kept_0, received_0), (slice(half, 2 * half), kept_1, received_1)):
-        out[:, at] = 0.9 * momentum[:, at] + (
-            factor * a[...].astype(jnp.float32) + other * b[...].astype(jnp.float32)
-        )
-
-
-def update(bit, sums, momentum, kept, received):
-    rows, columns = momentum.shape
-    tile = math.gcd(rows, 128)
-    spec = lambda width: pl.BlockSpec((tile, width), lambda i, *_: (i, 0))
+
+    def strip(i, carry):
+        at = strip_at(i * STRIP)
+        for left, a, b in ((0, kept_0, received_0), (half, kept_1, received_1)):
+            for lanes in lanes_of(half):
+                to = slice(left + lanes.start, left + lanes.stop)
+                out[at, to] = 0.9 * momentum[at, to] + (
+                    factor * a[at, lanes].astype(jnp.float32) + other * b[at, lanes].astype(jnp.float32)
+                )
+        return carry
+
+    lax.fori_loop(0, out.shape[0] // STRIP, strip, 0)
+    for n in range(2):
+        norms[n] = jnp.sqrt(sums[0, 1 + n]) / norm
+
+
+def update(bit, sums, momentum, kept, received, norm):
+    vmem = pl.BlockSpec(memory_space=pltpu.VMEM)
+    smem = pl.BlockSpec(memory_space=pltpu.SMEM)
     return pl.pallas_call(
-        update_kernel,
-        grid_spec=pltpu.PrefetchScalarGridSpec(
-            num_scalar_prefetch=1,
-            grid=(rows // tile,),
-            in_specs=[pl.BlockSpec(sums.shape, lambda i, *_: (0, 0), memory_space=pltpu.SMEM), spec(columns)] + [spec(columns // 2)] * 4,
-            out_specs=spec(columns),
-        ),
-        out_shape=jax.ShapeDtypeStruct(momentum.shape, jnp.float32),
+        functools.partial(update_kernel, norm),
+        in_specs=[smem, smem] + [vmem] * 5,
+        out_specs=[vmem, smem],
+        out_shape=[
+            jax.ShapeDtypeStruct(momentum.shape, jnp.float32),
+            jax.ShapeDtypeStruct((2,), jnp.float32),
+        ],
         compiler_params=pltpu.CompilerParams(vmem_limit_bytes=VMEM_LIMIT),
         cost_estimate=SMALL,
         name="update",
@@ -502,7 +510,14 @@
     far_inputs = shared_near(far_inputs)
     sums, last = far_gram(idx, sums, own, far_inputs, far_left, far_right, grads)
     sums = total_over(sums, 2)
-    send, sums = lax.optimization_barrier((send, sums))
+    half = columns // 2
+
+    def merged_half(flip, h):
+        return merge(idx, flip, sums, own, grads, last, rows**-0.5, per_block, width, h, half)
+
+    sent = [merged_half(True, h) for h in range(2)]
+    received = [exchange(s, "dp", 4) for s in sent]
+    send, _ = lax.optimization_barrier((send, sent[0]))
     terms.append(exchange(send, "tensor", 2))
     mask = 4
     while mask < parts:
@@ -510,14 +525,6 @@
         terms.append(exchange(send, "tensor", mask))
         mask *= 2
     summed = summed_terms(terms)[0]
-
-    half = columns // 2
-
-    def merged_half(flip, h):
-        return merge(idx, flip, sums, own, grads, last, rows**-0.5, per_block, width, h, half)
-
-    sent = [merged_half(True, h) for h in range(2)]
-    received = [exchange(s, "dp", 4) for s in sent]
     _, sums = lax.optimization_barrier((sent, sums))
     kept = [merged_half(False, h) for h in range(2)]
     for level in range(2, depth):
@@ -539,8 +546,8 @@
         for a, b in zip(kept, received):
             sums = partial_sums(bit, sums, a, b)
         sums = total_over(sums, level + 1)
-    new_momentum = update(bit, sums, momentum, kept, received)
-    return (summed, new_momentum, jnp.sqrt(sums[0, 1:3]) / depth_width)
+    new_momentum, tree_norms = update(bit, sums, momentum, kept, received, depth_width)
+    return (summed, new_momentum, tree_norms)
 
 
 def solution(mesh):

time: 146 us -> 145 us (level)
  transfers between devices with their start and end apart: 28 -> 28, of which waited for: 18 -> 17; matrix products, arithmetic and copies ran while one was open for 5% -> 5% of each run, Pallas kernels for 25% -> 24%
where the time goes in v5:
time: 145 us
  waiting for transfers between devices  56.1 us (39%)
  Pallas kernels  44.1 us (30%)
  starting transfers between devices  29.1 us (20%)
  local copies, waits for them, and re-layouts  8.16 us (6%)
  other arithmetic  6.62 us (5%)
    ppermute x28, waiting for transfers between devices, exchange(): return lax.ppermute(value, axis, pairs)  56.1 us
    ppermute x28, starting transfers between devices, exchange(): return lax.ppermute(value, axis, pairs)  29.1 us
    pallas_call x6, Pallas kernels, in_place(): pl.pallas_call(kernel, in_specs=[pl.BlockSpec(memory_space=m) for m, _ in...  18.7 us
    pallas_call x1, Pallas kernels, input_grad_part(): pl.pallas_call(input_grad_kernel, grid_spec=pltpu.PrefetchScalarGridSpec(...  8.91 us
    pallas_call x2, Pallas kernels, forward(): pl.pallas_call(forward_kernel, grid=(columns // tile,), in_specs=[pl.Bloc...  8.29 us
    unnamed x19, local copies, waits for them, and re-layouts  6.41 us
    pallas_call x1, Pallas kernels, own_gram(): pl.pallas_call(own_kernel, grid_spec=pltpu.PrefetchScalarGridSpec(num_sca...  4.67 us
    squeeze x1, other arithmetic, body(): summed = summed_terms(terms)[0]  2.93 us
  transfers between devices with their start and end apart: 28, of which 17 were waited for; matrix products, arithmetic and copies ran while one was open for 5% of the time, Pallas kernels for 24%

profile of v5, /device:TPU:0, one launch (start us, length us, event | category | flops | bytes accessed | tf_op | source)
XLA Modules:
  0.0 144.9 jit_solution(5508562598928278830)
XLA Ops:
  0.7 1.7 %constant_dynamic-slice_fusion = (bf16[512,256]{1,0:T(8,128)(2,1)S(1)}, bf16[512,256]{1,0:T(8,128)(2,1)S(1)}, bf16[512,256]{1,0:T(8,128)(2,1)S(1)}) fusion(bf16[512,4096]{1,0:T(8,128)(2,1)} %x.3, s32[]{:T(128)S(6)} %select_n.47, s32[]{:T(128)S(6)} %select_n.46, s32[]{:T(128)S(6)} %select_n.45), kind=kLoop, calls=%fused_computation.4 | loop fusion | bytes 1572876 | tf_op jit(solution)/shard_map/dynamic_slice | solution.py:453
  2.4 0.1 copy.10
  2.5 0.1 copy.11
  2.6 0.1 copy.12
  2.8 3.0 %collective-permute-start = (bf16[256,512]{1,0:T(8,128)(2,1)S(1)}, bf16[256,512]{1,0:T(8,128)(2,1)S(1)}, u32[]{:S(2)}, u32[]{:S(2)}) collective-permute-start(bf16[256,512]{1,0:T(8,128)(2,1)S(1)} %bitcast.16), channel_id=1, source_target_pairs={{0,4},{4,0},{8,12},{12,8},{16,20},{20,16},{24,28},{28,24},{1,5},{5... | collective-permute-start | bytes 786440 | tf_op jit(solution)/shard_map/ppermute | solution.py:25
  5.8 1.6 %collective-permute-start.1 = (bf16[256,512]{1,0:T(8,128)(2,1)S(1)}, bf16[256,512]{1,0:T(8,128)(2,1)S(1)}, u32[]{:S(2)}, u32[]{:S(2)}) collective-permute-start(bf16[256,512]{1,0:T(8,128)(2,1)S(1)} %bitcast.15), channel_id=1, source_target_pairs={{0,8},{4,12},{8,0},{12,4},{16,24},{20,28},{24,16},{28,20},{1,9},{5... | collective-permute-start | bytes 786440 | tf_op jit(solution)/shard_map/ppermute | solution.py:25
  7.4 2.2 %copy-done.2 = bf16[512,4096]{1,0:T(8,128)(2,1)S(1)} copy-done((bf16[512,4096]{1,0:T(8,128)(2,1)S(1)}, bf16[512,4096]{1,0:T(8,128)(2,1)}, u32[]{:S(2)}) %copy-start.2) | copy-done | bytes 4194328
  9.6 4.1 %forward.2.left = bf16[512,512]{1,0:T(8,128)(2,1)S(1)} custom-call(bf16[512,4096]{1,0:T(8,128)(2,1)S(1)} %copy-done.2, bf16[4096,1024]{1,0:T(8,128)(2,1)} %w_keep.1, bf16[512,1024]{1,0:T(8,128)(2,1)S(1)} %copy-done.5), custom_call_target="tpu_custom_call" | custom-call | flops 1 | bytes 1 | tf_op jit(solution)/shard_map/forward/pallas_call | solution.py:84
  13.8 1.3 collective-permute-done.1
  15.1 0.9 pad_maximum_fusion.refs_0_
  15.9 1.5 %collective-permute-start.4 = (bf16[2,256,512]{2,1,0:T(8,128)(2,1)}, bf16[2,256,512]{2,1,0:T(8,128)(2,1)}, u32[]{:S(2)}, u32[]{:S(2)}) collective-permute-start(bf16[2,256,512]{2,1,0:T(8,128)(2,1)} %pad_maximum_fusion.refs_0_), channel_id=1, source_target_pairs={{0,2},{1,3},{2,0},{3,1},{4,6},{5,7},{6,4},{7,5},{8,10},{9,11},{10,... | collective-permute-start | bytes 1572872 | tf_op jit(solution)/shard_map/ppermute | solution.py:25
  17.4 0.6 collective-permute-start.2
  18.0 1.6 %collective-permute-start.3 = (bf16[512,512]{1,0:T(8,128)(2,1)S(1)}, bf16[512,512]{1,0:T(8,128)(2,1)}, u32[]{:S(2)}, u32[]{:S(2)}) collective-permute-start(bf16[512,512]{1,0:T(8,128)(2,1)S(1)} %forward.2.left), channel_id=1, source_target_pairs={{0,8},{4,12},{8,0},{12,4},{16,24},{20,28},{24,16},{28,20},{1,9},{5... | collective-permute-start | bytes 1572872 | tf_op jit(solution)/shard_map/ppermute | solution.py:25
  19.6 4.1 %forward.3.right = bf16[512,512]{1,0:T(8,128)(2,1)S(1)} custom-call(bf16[512,4096]{1,0:T(8,128)(2,1)S(1)} %copy-done.2, bf16[4096,1024]{1,0:T(8,128)(2,1)} %w_keep.1, bf16[512,1024]{1,0:T(8,128)(2,1)S(1)} %copy-done.5), custom_call_target="tpu_custom_call" | custom-call | flops 1 | bytes 1 | tf_op jit(solution)/shard_map/forward/pallas_call | solution.py:84
  23.8 1.5 %collective-permute-start.6 = (bf16[512,512]{1,0:T(8,128)(2,1)S(1)}, bf16[512,512]{1,0:T(8,128)(2,1)}, u32[]{:S(2)}, u32[]{:S(2)}) collective-permute-start(bf16[512,512]{1,0:T(8,128)(2,1)S(1)} %forward.3.right), channel_id=1, source_target_pairs={{0,4},{4,0},{8,12},{12,8},{16,20},{20,16},{24,28},{28,24},{1,5},{5... | collective-permute-start | bytes 1572872 | tf_op jit(solution)/shard_map/ppermute | solution.py:25
  25.3 0.5 collective-permute-start.7
  25.7 0.1 stack.40.idx
  25.8 4.7 %own_gram.1 = (f32[1,128]{1,0:T(1,128)S(1)}, bf16[1024,1024]{1,0:T(8,128)(2,1)S(1)}) custom-call(s32[7]{0:T(128)S(1)} %stack.40.idx, bf16[512,4096]{1,0:T(8,128)(2,1)} %x.3, bf16[512,512]{1,0:T(8,128)(2,1)S(1)} %forward.2.left, bf16[512,512]{1,0:T(8,128)(2,1)S(1)} %forward.3.right), custom_call_target="tpu_custom_call" | custom-call | flops 1 | bytes 1 | tf_op jit(solution)/shard_map/own_gram/pallas_call | solution.py:192
  30.5 1.9 %collective-permute-done.2.y_left = bf16[512,512]{1,0:T(8,128)(2,1)} collective-permute-done((bf16[512,512]{1,0:T(8,128)(2,1)S(1)}, bf16[512,512]{1,0:T(8,128)(2,1)}, u32[]{:S(2)}, u32[]{:S(2)}) %collective-permute-start.2) | collective-permute-done | bytes 524320 | tf_op jit(solution)/shard_map/ppermute | solution.py:25
  32.4 0.6 collective-permute-done.3.z_left
  33.0 8.9 %input_grad_part.1 = (bf16[2,1024,512]{2,1,0:T(8,128)(2,1)}, bf16[2,1024,512]{2,1,0:T(8,128)(2,1)}) custom-call(s32[7]{0:T(128)S(1)} %stack.40.idx, bf16[4096,1024]{1,0:T(8,128)(2,1)} %w_keep.1, bf16[4096,1024]{1,0:T(8,128)(2,1)} %w_keep.1, bf16[512,512]{1,0:T(8,128)(2,1)S(1)} %forward.2.left, bf16[512,512]{1,0:T(8,128)(2,1)S(1)} %forward.3.right), custom_call_target="tpu_custom_call" | custom-call | flops 1 | bytes 1 | tf_op jit(solution)/shard_map/input_grad_part/pallas_call | solution.py:127
  42.0 0.5 collective-permute-start.10
  42.5 0.1 collective-permute-start.11
  42.6 1.2 collective-permute-start.9
  43.8 1.5 %collective-permute-start.12 = (bf16[512,512]{1,0:T(8,128)(2,1)}, bf16[512,512]{1,0:T(8,128)(2,1)S(1)}, u32[]{:S(2)}, u32[]{:S(2)}) collective-permute-start(bf16[512,512]{1,0:T(8,128)(2,1)} %collective-permute-done.3.z_left), channel_id=1, source_target_pairs={{0,4},{4,0},{8,12},{12,8},{16,20},{20,16},{24,28},{28,24},{1,5},{5... | collective-permute-start | bytes 1572872 | tf_op jit(solution)/shard_map/ppermute | solution.py:25
  45.2 1.3 collective-permute-done.8
  46.5 1.6 %collective-permute-start.13 = (bf16[512,512]{1,0:T(8,128)(2,1)}, bf16[512,512]{1,0:T(8,128)(2,1)S(1)}, u32[]{:S(2)}, u32[]{:S(2)}) collective-permute-start(bf16[512,512]{1,0:T(8,128)(2,1)} %collective-permute-done.6.y_right), channel_id=1, source_target_pairs={{0,8},{4,12},{8,0},{12,4},{16,24},{20,28},{24,16},{28,20},{1,9},{5... | collective-permute-start | bytes 1572872 | tf_op jit(solution)/shard_map/ppermute | solution.py:25
  48.1 2.8 %add_convert_fusion.1 = bf16[1,1024,512]{2,1,0:T(8,128)(2,1)} fusion(bf16[2,1024,512]{2,1,0:T(8,128)(2,1)} %collective-permute-done.8, s32[]{:T(128)S(6)} %select_n.50, bf16[2,1024,512]{2,1,0:T(8,128)(2,1)} %get-tuple-element.59), kind=kLoop, calls=%fused_computation.1 | loop fusion | flops 2097152 | bytes 3145732 | tf_op jit(solution)/shard_map/convert_element_type | solution.py:497
  50.9 7.2 %near_gram.1 = (f32[1,128]{1,0:T(1,128)S(1)}, bf16[2,1024,1024]{2,1,0:T(8,128)(2,1)S(1)}) custom-call(s32[7]{0:T(128)S(1)} %stack.40.idx, f32[1,128]{1,0:T(1,128)S(1)} %get-tuple-element.64.before, bf16[1024,1024]{1,0:T(8,128)(2,1)S(1)} %get-tuple-element.65.own, bf16[512,512]{1,0:T(8,128)(2,1)} %collective-permute-done.2.y_left, ...), custom_call_target="tpu_custom_call" | custom-call | flops 1 | bytes 1 | tf_op jit(solution)/shard_map/near_gram/pallas_call | solution.py:265
  58.1 0.5 collective-permute-start.15
  58.6 2.0 %collective-permute-done.13.right = bf16[512,512]{1,0:T(8,128)(2,1)S(1)} collective-permute-done((bf16[512,512]{1,0:T(8,128)(2,1)}, bf16[512,512]{1,0:T(8,128)(2,1)S(1)}, u32[]{:S(2)}, u32[]{:S(2)}) %collective-permute-start.13) | collective-permute-done | bytes 524320 | tf_op jit(solution)/shard_map/ppermute | solution.py:25
  60.7 4.8 %far_gram.1 = (f32[1,128]{1,0:T(1,128)S(1)}, bf16[1024,1024]{1,0:T(8,128)(2,1)S(1)}) custom-call(s32[7]{0:T(128)S(1)} %stack.40.idx, f32[1,128]{1,0:T(1,128)S(1)} %get-tuple-element.73.before, bf16[512,512]{1,0:T(8,128)(2,1)S(1)} %collective-permute-done.12.left, bf16[512,512]{1,0:T(8,128)(2,1)S(1)} %collective-permute-done.13.right, ...), custom_call_target="tpu_custom_call" | custom-call | flops 1 | bytes 1 | tf_op jit(solution)/shard_map/far_gram/pallas_call | solution.py:265
  65.5 1.1 collective-permute-done.16
  66.6 1.4 collective-permute-start.17
  68.0 2.1 %collective-permute-done.17 = f32[1,128]{1,0:T(1,128)S(1)} collective-permute-done((f32[1,128]{1,0:T(1,128)S(1)}, f32[1,128]{1,0:T(1,128)S(1)}, u32[]{:S(2)}, u32[]{:S(2)}) %collective-permute-start.17) | collective-permute-done | bytes 544 | tf_op jit(solution)/shard_map/ppermute | solution.py:25
  70.1 1.6 %collective-permute-start.18 = (f32[1,128]{1,0:T(1,128)S(1)}, f32[1,128]{1,0:T(1,128)S(1)}, u32[]{:S(2)}, u32[]{:S(2)}) collective-permute-start(f32[1,128]{1,0:T(1,128)S(1)} %add.104), channel_id=1, source_target_pairs={{0,8},{4,12},{8,0},{12,4},{16,24},{20,28},{24,16},{28,20},{1,9},{5... | collective-permute-start | bytes 1544 | tf_op jit(solution)/shard_map/ppermute | solution.py:25
  71.7 2.0 %collective-permute-done.18 = f32[1,128]{1,0:T(1,128)S(1)} collective-permute-done((f32[1,128]{1,0:T(1,128)S(1)}, f32[1,128]{1,0:T(1,128)S(1)}, u32[]{:S(2)}, u32[]{:S(2)}) %collective-permute-start.18) | collective-permute-done | bytes 544 | tf_op jit(solution)/shard_map/ppermute | solution.py:25
  73.7 1.2 collective-permute-start.19
  74.9 2.3 %collective-permute-done.19 = f32[1,128]{1,0:T(1,128)S(1)} collective-permute-done((f32[1,128]{1,0:T(1,128)S(1)}, f32[1,128]{1,0:T(1,128)S(1)}, u32[]{:S(2)}, u32[]{:S(2)}) %collective-permute-start.19) | collective-permute-done | bytes 544 | tf_op jit(solution)/shard_map/ppermute | solution.py:25
  77.2 2.1 %merge.4 = bf16[512,512]{1,0:T(8,128)(2,1)} custom-call(s32[7]{0:T(128)S(1)} %stack.40.idx, f32[1,128]{1,0:T(1,128)S(1)} %add.106.sums, bf16[1024,1024]{1,0:T(8,128)(2,1)S(1)} %get-tuple-element.65.own, bf16[2,1024,1024]{2,1,0:T(8,128)(2,1)S(1)} %get-tuple-element.74.grads, bf16[1024,1024]{1,0:T(8,128)(2,1)S(1)} %get-tuple-element.78.last), custom_call_target="tpu_custom_call" | custom-call | flops 1 | bytes 1 | tf_op jit(solution)/shard_map/merge/pallas_call | solution.py:265
  79.3 1.2 collective-permute-start.20
  80.5 2.6 %collective-permute-start.21 = (bf16[512,512]{1,0:T(8,128)(2,1)}, bf16[512,512]{1,0:T(8,128)(2,1)S(1)}, u32[]{:S(2)}, u32[]{:S(2)}) collective-permute-start(bf16[512,512]{1,0:T(8,128)(2,1)} %merge.4), channel_id=1, source_target_pairs={{0,16},{4,20},{8,24},{12,28},{16,0},{20,4},{24,8},{28,12},{1,17},{... | collective-permute-start | bytes 1572872 | tf_op jit(solution)/shard_map/ppermute | solution.py:25
  83.1 2.1 %merge.5 = bf16[512,512]{1,0:T(8,128)(2,1)} custom-call(s32[7]{0:T(128)S(1)} %stack.40.idx, f32[1,128]{1,0:T(1,128)S(1)} %add.106.sums, bf16[1024,1024]{1,0:T(8,128)(2,1)S(1)} %get-tuple-element.65.own, bf16[2,1024,1024]{2,1,0:T(8,128)(2,1)S(1)} %get-tuple-element.74.grads, bf16[1024,1024]{1,0:T(8,128)(2,1)S(1)} %get-tuple-element.78.last), custom_call_target="tpu_custom_call" | custom-call | flops 1 | bytes 1 | tf_op jit(solution)/shard_map/merge/pallas_call | solution.py:265
  85.2 0.3 collective-permute-start.22
  85.6 2.2 %copy-done.1 = bf16[2,1024,1024]{2,1,0:T(8,128)(2,1)S(1)} copy-done((bf16[2,1024,1024]{2,1,0:T(8,128)(2,1)S(1)}, bf16[2,1024,1024]{2,1,0:T(8,128)(2,1)}, u32[]{:S(2)}) %copy-start.1) | copy-done | bytes 4194328
  87.8 1.6 %copy-done.4 = bf16[1024,1024]{1,0:T(8,128)(2,1)S(1)} copy-done((bf16[1024,1024]{1,0:T(8,128)(2,1)S(1)}, bf16[1024,1024]{1,0:T(8,128)(2,1)}, u32[]{:S(2)}) %copy-start.4) | copy-done | bytes 2097176
  89.4 1.3 merge.7.kept.kept_1
  90.7 1.3 merge.6.kept.kept_0
  92.0 9.5 %collective-permute-done.20 = bf16[1,1024,512]{2,1,0:T(8,128)(2,1)} collective-permute-done((bf16[1,1024,512]{2,1,0:T(8,128)(2,1)}, bf16[1,1024,512]{2,1,0:T(8,128)(2,1)}, u32[]{:S(2)}, u32[]{:S(2)}) %collective-permute-start.20) | collective-permute-done | bytes 1048608 | tf_op jit(solution)/shard_map/ppermute | solution.py:25
  101.4 2.9 %fusion = bf16[1024,512]{1,0:T(8,128)(2,1)} fusion(bf16[1,1024,512]{2,1,0:T(8,128)(2,1)} %collective-permute-done.20, bf16[2,1024,512]{2,1,0:T(8,128)(2,1)} %collective-permute-done.8, s32[]{:T(128)S(6)} %select_n.49, bf16[2,1024,512]{2,1,0:T(8,128)(2,1)S(1)} %copy-done.7), kind=kLoop, calls=%fused_computation.2 | loop fusion | flops 3145728 | bytes 4194308 | tf_op jit(solution)/shard_map/squeeze | solution.py:527
  104.4 11.3 %collective-permute-done.21.received.received_0 = bf16[512,512]{1,0:T(8,128)(2,1)S(1)} collective-permute-done((bf16[512,512]{1,0:T(8,128)(2,1)}, bf16[512,512]{1,0:T(8,128)(2,1)S(1)}, u32[]{:S(2)}, u32[]{:S(2)}) %collective-permute-start.21) | collective-permute-done | bytes 524320 | tf_op jit(solution)/shard_map/ppermute | solution.py:25
  115.6 0.5 partial_sums.2.before
  116.1 9.5 %collective-permute-done.22.received.received_1 = bf16[512,512]{1,0:T(8,128)(2,1)S(1)} collective-permute-done((bf16[512,512]{1,0:T(8,128)(2,1)}, bf16[512,512]{1,0:T(8,128)(2,1)S(1)}, u32[]{:S(2)}, u32[]{:S(2)}) %collective-permute-start.22) | collective-permute-done | bytes 524320 | tf_op jit(solution)/shard_map/ppermute | solution.py:25
  125.7 0.5 partial_sums.3
  126.2 1.1 collective-permute-done.23
  127.3 1.5 %collective-permute-start.24 = (f32[1,128]{1,0:T(1,128)S(1)}, f32[1,128]{1,0:T(1,128)S(1)}, u32[]{:S(2)}, u32[]{:S(2)}) collective-permute-start(f32[1,128]{1,0:T(1,128)S(1)} %add.108), channel_id=1, source_target_pairs={{0,4},{4,0},{8,12},{12,8},{16,20},{20,16},{24,28},{28,24},{1,5},{5... | collective-permute-start | bytes 1544 | tf_op jit(solution)/shard_map/ppermute | solution.py:25
  128.7 2.1 %collective-permute-done.24 = f32[1,128]{1,0:T(1,128)S(1)} collective-permute-done((f32[1,128]{1,0:T(1,128)S(1)}, f32[1,128]{1,0:T(1,128)S(1)}, u32[]{:S(2)}, u32[]{:S(2)}) %collective-permute-start.24) | collective-permute-done | bytes 544 | tf_op jit(solution)/shard_map/ppermute | solution.py:25
  130.8 0.8 collective-permute-start.25
  131.6 2.8 %collective-permute-done.25 = f32[1,128]{1,0:T(1,128)S(1)} collective-permute-done((f32[1,128]{1,0:T(1,128)S(1)}, f32[1,128]{1,0:T(1,128)S(1)}, u32[]{:S(2)}, u32[]{:S(2)}) %collective-permute-start.25) | collective-permute-done | bytes 544 | tf_op jit(solution)/shard_map/ppermute | solution.py:25
  134.4 2.0 %collective-permute-start.26 = (f32[1,128]{1,0:T(1,128)S(1)}, f32[1,128]{1,0:T(1,128)S(1)}, u32[]{:S(2)}, u32[]{:S(2)}) collective-permute-start(f32[1,128]{1,0:T(1,128)S(1)} %add.110), channel_id=1, source_target_pairs={{0,16},{4,20},{8,24},{12,28},{16,0},{20,4},{24,8},{28,12},{1,17},{... | collective-permute-start | bytes 1544 | tf_op jit(solution)/shard_map/ppermute | solution.py:25
  136.4 2.4 %collective-permute-done.26 = f32[1,128]{1,0:T(1,128)S(1)} collective-permute-done((f32[1,128]{1,0:T(1,128)S(1)}, f32[1,128]{1,0:T(1,128)S(1)}, u32[]{:S(2)}, u32[]{:S(2)}) %collective-permute-start.26) | collective-permute-done | bytes 544 | tf_op jit(solution)/shard_map/ppermute | solution.py:25
  138.8 0.8 collective-permute-start.27
  139.6 2.8 %collective-permute-done.27 = f32[1,128]{1,0:T(1,128)S(1)} collective-permute-done((f32[1,128]{1,0:T(1,128)S(1)}, f32[1,128]{1,0:T(1,128)S(1)}, u32[]{:S(2)}, u32[]{:S(2)}) %collective-permute-start.27) | collective-permute-done | bytes 544 | tf_op jit(solution)/shard_map/ppermute | solution.py:25
  142.4 2.6 %update.1 = (f32[512,1024]{1,0:T(8,128)}, f32[2]{0:T(128)}) custom-call(s32[1]{0:T(128)} %bitcast.1.first_at.bit, f32[1,128]{1,0:T(1,128)S(1)} %add.112.sums, f32[512,1024]{1,0:T(8,128)S(1)} %copy-done.6, bf16[512,512]{1,0:T(8,128)(2,1)S(1)} %merge.6.kept.kept_0, bf16[512,512]{1,0:T(8,128)(2,1)S(1)} %merge.7.kept.kept_1, ...), custom_call_target="tpu_custom_call" | custom-call | flops 1 | bytes 1 | tf_op jit(solution)/shard_map/update/pallas_call | solution.py:424
  (39 shorter events, 0.3 us)
Async XLA Ops:
  0.6 6.8 %copy-start.5 = (bf16[512,1024]{1,0:T(8,128)(2,1)S(1)}, bf16[512,1024]{1,0:T(8,128)(2,1)}, u32[]{:S(2)}) copy-start(bf16[512,1024]{1,0:T(8,128)(2,1)} %targets.3) | copy-start | bytes 3145732
  2.8 11.0 %collective-permute-start = (bf16[256,512]{1,0:T(8,128)(2,1)S(1)}, bf16[256,512]{1,0:T(8,128)(2,1)S(1)}, u32[]{:S(2)}, u32[]{:S(2)}) collective-permute-start(bf16[256,512]{1,0:T(8,128)(2,1)S(1)} %bitcast.16), channel_id=1, source_target_pairs={{0,4},{4,0},{8,12},{12,8},{16,20},{20,16},{24,28},{28,24},{1,5},{5... | collective-permute-start | bytes 786440 | tf_op jit(solution)/shard_map/ppermute | solution.py:25
  5.8 9.2 %collective-permute-start.1 = (bf16[256,512]{1,0:T(8,128)(2,1)S(1)}, bf16[256,512]{1,0:T(8,128)(2,1)S(1)}, u32[]{:S(2)}, u32[]{:S(2)}) collective-permute-start(bf16[256,512]{1,0:T(8,128)(2,1)S(1)} %bitcast.15), channel_id=1, source_target_pairs={{0,8},{4,12},{8,0},{12,4},{16,24},{20,28},{24,16},{28,20},{1,9},{5... | collective-permute-start | bytes 786440 | tf_op jit(solution)/shard_map/ppermute | solution.py:25
  7.4 17.8 %collective-permute-start.5 = (bf16[256,512]{1,0:T(8,128)(2,1)S(1)}, bf16[256,512]{1,0:T(8,128)(2,1)S(1)}, u32[]{:S(2)}, u32[]{:S(2)}) collective-permute-start(bf16[256,512]{1,0:T(8,128)(2,1)S(1)} %bitcast.14), channel_id=1, source_target_pairs={{0,12},{4,8},{8,4},{12,0},{16,28},{20,24},{24,20},{28,16},{1,13},{... | collective-permute-start | bytes 786440 | tf_op jit(solution)/shard_map/ppermute | solution.py:25
  7.4 2.2 %copy-start.2 = (bf16[512,4096]{1,0:T(8,128)(2,1)S(1)}, bf16[512,4096]{1,0:T(8,128)(2,1)}, u32[]{:S(2)}) copy-start(bf16[512,4096]{1,0:T(8,128)(2,1)} %x.3) | copy-start | bytes 12582916
  15.9 14.5 %collective-permute-start.4 = (bf16[2,256,512]{2,1,0:T(8,128)(2,1)}, bf16[2,256,512]{2,1,0:T(8,128)(2,1)}, u32[]{:S(2)}, u32[]{:S(2)}) collective-permute-start(bf16[2,256,512]{2,1,0:T(8,128)(2,1)} %pad_maximum_fusion.refs_0_), channel_id=1, source_target_pairs={{0,2},{1,3},{2,0},{3,1},{4,6},{5,7},{6,4},{7,5},{8,10},{9,11},{10,... | collective-permute-start | bytes 1572872 | tf_op jit(solution)/shard_map/ppermute | solution.py:25
  17.4 15.0 %collective-permute-start.2 = (bf16[512,512]{1,0:T(8,128)(2,1)S(1)}, bf16[512,512]{1,0:T(8,128)(2,1)}, u32[]{:S(2)}, u32[]{:S(2)}) collective-permute-start(bf16[512,512]{1,0:T(8,128)(2,1)S(1)} %forward.2.left), channel_id=1, source_target_pairs={{0,4},{4,0},{8,12},{12,8},{16,20},{20,16},{24,28},{28,24},{1,5},{5... | collective-permute-start | bytes 1572872 | tf_op jit(solution)/shard_map/ppermute | solution.py:25
  18.0 15.0 %collective-permute-start.3 = (bf16[512,512]{1,0:T(8,128)(2,1)S(1)}, bf16[512,512]{1,0:T(8,128)(2,1)}, u32[]{:S(2)}, u32[]{:S(2)}) collective-permute-start(bf16[512,512]{1,0:T(8,128)(2,1)S(1)} %forward.2.left), channel_id=1, source_target_pairs={{0,8},{4,12},{8,0},{12,4},{16,24},{20,28},{24,16},{28,20},{1,9},{5... | collective-permute-start | bytes 1572872 | tf_op jit(solution)/shard_map/ppermute | solution.py:25
  23.8 18.2 %collective-permute-start.6 = (bf16[512,512]{1,0:T(8,128)(2,1)S(1)}, bf16[512,512]{1,0:T(8,128)(2,1)}, u32[]{:S(2)}, u32[]{:S(2)}) collective-permute-start(bf16[512,512]{1,0:T(8,128)(2,1)S(1)} %forward.3.right), channel_id=1, source_target_pairs={{0,4},{4,0},{8,12},{12,8},{16,20},{20,16},{24,28},{28,24},{1,5},{5... | collective-permute-start | bytes 1572872 | tf_op jit(solution)/shard_map/ppermute | solution.py:25
  25.3 16.7 %collective-permute-start.7 = (bf16[512,512]{1,0:T(8,128)(2,1)S(1)}, bf16[512,512]{1,0:T(8,128)(2,1)}, u32[]{:S(2)}, u32[]{:S(2)}) collective-permute-start(bf16[512,512]{1,0:T(8,128)(2,1)S(1)} %forward.3.right), channel_id=1, source_target_pairs={{0,8},{4,12},{8,0},{12,4},{16,24},{20,28},{24,16},{28,20},{1,9},{5... | collective-permute-start | bytes 1572872 | tf_op jit(solution)/shard_map/ppermute | solution.py:25
  41.9 4.6 %collective-permute-start.8 = (bf16[2,1024,512]{2,1,0:T(8,128)(2,1)}, bf16[2,1024,512]{2,1,0:T(8,128)(2,1)}, u32[]{:S(2)}, u32[]{:S(2)}) collective-permute-start(bf16[2,1024,512]{2,1,0:T(8,128)(2,1)} %get-tuple-element.60), channel_id=1, source_target_pairs={{0,1},{1,0},{2,3},{3,2},{4,5},{5,4},{6,7},{7,6},{8,9},{9,8},{10,11... | collective-permute-start | bytes 6291464 | tf_op jit(solution)/shard_map/ppermute | solution.py:25
  42.0 8.9 %collective-permute-start.10 = (bf16[2,256,512]{2,1,0:T(8,128)(2,1)}, bf16[2,256,512]{2,1,0:T(8,128)(2,1)}, u32[]{:S(2)}, u32[]{:S(2)}) collective-permute-start(bf16[2,256,512]{2,1,0:T(8,128)(2,1)} %pad_maximum_fusion.refs_0_), channel_id=1, source_target_pairs={{0,1},{1,0},{2,3},{3,2},{4,5},{5,4},{6,7},{7,6},{8,9},{9,8},{10,11... | collective-permute-start | bytes 1572872 | tf_op jit(solution)/shard_map/ppermute | solution.py:25
  42.5 8.4 %collective-permute-start.11 = (bf16[2,256,512]{2,1,0:T(8,128)(2,1)}, bf16[2,256,512]{2,1,0:T(8,128)(2,1)}, u32[]{:S(2)}, u32[]{:S(2)}) collective-permute-start(bf16[2,256,512]{2,1,0:T(8,128)(2,1)} %collective-permute-done.4.refs_1_), channel_id=1, source_target_pairs={{0,1},{1,0},{2,3},{3,2},{4,5},{5,4},{6,7},{7,6},{8,9},{9,8},{10,11... | collective-permute-start | bytes 1572872 | tf_op jit(solution)/shard_map/ppermute | solution.py:25
  42.6 15.5 %collective-permute-start.9 = (bf16[256,512]{1,0:T(8,128)(2,1)S(1)}, bf16[256,512]{1,0:T(8,128)(2,1)}, u32[]{:S(2)}, u32[]{:S(2)}) collective-permute-start(bf16[256,512]{1,0:T(8,128)(2,1)S(1)} %collective-permute-done.5.refs_0_), channel_id=1, source_target_pairs={{0,2},{1,3},{2,0},{3,1},{4,6},{5,7},{6,4},{7,5},{8,10},{9,11},{10,... | collective-permute-start | bytes 786440 | tf_op jit(solution)/shard_map/ppermute | solution.py:25
  43.8 14.9 %collective-permute-start.12 = (bf16[512,512]{1,0:T(8,128)(2,1)}, bf16[512,512]{1,0:T(8,128)(2,1)S(1)}, u32[]{:S(2)}, u32[]{:S(2)}) collective-permute-start(bf16[512,512]{1,0:T(8,128)(2,1)} %collective-permute-done.3.z_left), channel_id=1, source_target_pairs={{0,4},{4,0},{8,12},{12,8},{16,20},{20,16},{24,28},{28,24},{1,5},{5... | collective-permute-start | bytes 1572872 | tf_op jit(solution)/shard_map/ppermute | solution.py:25
  46.5 14.2 %collective-permute-start.13 = (bf16[512,512]{1,0:T(8,128)(2,1)}, bf16[512,512]{1,0:T(8,128)(2,1)S(1)}, u32[]{:S(2)}, u32[]{:S(2)}) collective-permute-start(bf16[512,512]{1,0:T(8,128)(2,1)} %collective-permute-done.6.y_right), channel_id=1, source_target_pairs={{0,8},{4,12},{8,0},{12,4},{16,24},{20,28},{24,16},{28,20},{1,9},{5... | collective-permute-start | bytes 1572872 | tf_op jit(solution)/shard_map/ppermute | solution.py:25
  58.0 25.1 %copy-start = (bf16[2,1024,1024]{2,1,0:T(8,128)(2,1)}, bf16[2,1024,1024]{2,1,0:T(8,128)(2,1)S(1)}, u32[]{:S(2)}) copy-start(bf16[2,1024,1024]{2,1,0:T(8,128)(2,1)S(1)} %get-tuple-element.74.grads) | copy-start | bytes 12582916
  58.1 2.6 %collective-permute-start.14 = (bf16[256,512]{1,0:T(8,128)(2,1)S(1)}, bf16[256,512]{1,0:T(8,128)(2,1)S(1)}, u32[]{:S(2)}, u32[]{:S(2)}) collective-permute-start(bf16[256,512]{1,0:T(8,128)(2,1)S(1)} %collective-permute-done.5.refs_0_), channel_id=1, source_target_pairs={{0,1},{1,0},{2,3},{3,2},{4,5},{5,4},{6,7},{7,6},{8,9},{9,8},{10,11... | collective-permute-start | bytes 786440 | tf_op jit(solution)/shard_map/ppermute | solution.py:25
  58.1 2.5 %collective-permute-start.15 = (bf16[256,512]{1,0:T(8,128)(2,1)}, bf16[256,512]{1,0:T(8,128)(2,1)S(1)}, u32[]{:S(2)}, u32[]{:S(2)}) collective-permute-start(bf16[256,512]{1,0:T(8,128)(2,1)} %collective-permute-done.9.refs_1_), channel_id=1, source_target_pairs={{0,1},{1,0},{2,3},{3,2},{4,5},{5,4},{6,7},{7,6},{8,9},{9,8},{10,11... | collective-permute-start | bytes 786440 | tf_op jit(solution)/shard_map/ppermute | solution.py:25
  65.4 17.7 %copy-start.3 = (bf16[1024,1024]{1,0:T(8,128)(2,1)}, bf16[1024,1024]{1,0:T(8,128)(2,1)S(1)}, u32[]{:S(2)}) copy-start(bf16[1024,1024]{1,0:T(8,128)(2,1)S(1)} %get-tuple-element.78.last) | copy-start | bytes 6291460
  65.4 1.1 collective-permute-start.16
  66.6 3.5 %collective-permute-start.17 = (f32[1,128]{1,0:T(1,128)S(1)}, f32[1,128]{1,0:T(1,128)S(1)}, u32[]{:S(2)}, u32[]{:S(2)}) collective-permute-start(f32[1,128]{1,0:T(1,128)S(1)} %add.103), channel_id=1, source_target_pairs={{0,4},{4,0},{8,12},{12,8},{16,20},{20,16},{24,28},{28,24},{1,5},{5... | collective-permute-start | bytes 1544 | tf_op jit(solution)/shard_map/ppermute | solution.py:25
  70.1 3.5 %collective-permute-start.18 = (f32[1,128]{1,0:T(1,128)S(1)}, f32[1,128]{1,0:T(1,128)S(1)}, u32[]{:S(2)}, u32[]{:S(2)}) collective-permute-start(f32[1,128]{1,0:T(1,128)S(1)} %add.104), channel_id=1, source_target_pairs={{0,8},{4,12},{8,0},{12,4},{16,24},{20,28},{24,16},{28,20},{1,9},{5... | collective-permute-start | bytes 1544 | tf_op jit(solution)/shard_map/ppermute | solution.py:25
  73.7 3.5 %collective-permute-start.19 = (f32[1,128]{1,0:T(1,128)S(1)}, f32[1,128]{1,0:T(1,128)S(1)}, u32[]{:S(2)}, u32[]{:S(2)}) collective-permute-start(f32[1,128]{1,0:T(1,128)S(1)} %add.105), channel_id=1, source_target_pairs={{0,2},{1,3},{2,0},{3,1},{4,6},{5,7},{6,4},{7,5},{8,10},{9,11},{10,... | collective-permute-start | bytes 1544 | tf_op jit(solution)/shard_map/ppermute | solution.py:25
  79.3 22.1 %collective-permute-start.20 = (bf16[1,1024,512]{2,1,0:T(8,128)(2,1)}, bf16[1,1024,512]{2,1,0:T(8,128)(2,1)}, u32[]{:S(2)}, u32[]{:S(2)}) collective-permute-start(bf16[1,1024,512]{2,1,0:T(8,128)(2,1)} %add_convert_fusion.1), channel_id=1, source_target_pairs={{0,2},{1,3},{2,0},{3,1},{4,6},{5,7},{6,4},{7,5},{8,10},{9,11},{10,... | collective-permute-start | bytes 3145736 | tf_op jit(solution)/shard_map/ppermute | solution.py:25
  80.5 35.1 %collective-permute-start.21 = (bf16[512,512]{1,0:T(8,128)(2,1)}, bf16[512,512]{1,0:T(8,128)(2,1)S(1)}, u32[]{:S(2)}, u32[]{:S(2)}) collective-permute-start(bf16[512,512]{1,0:T(8,128)(2,1)} %merge.4), channel_id=1, source_target_pairs={{0,16},{4,20},{8,24},{12,28},{16,0},{20,4},{24,8},{28,12},{1,17},{... | collective-permute-start | bytes 1572872 | tf_op jit(solution)/shard_map/ppermute | solution.py:25
  85.2 40.4 %collective-permute-start.22 = (bf16[512,512]{1,0:T(8,128)(2,1)}, bf16[512,512]{1,0:T(8,128)(2,1)S(1)}, u32[]{:S(2)}, u32[]{:S(2)}) collective-permute-start(bf16[512,512]{1,0:T(8,128)(2,1)} %merge.5), channel_id=1, source_target_pairs={{0,16},{4,20},{8,24},{12,28},{16,0},{20,4},{24,8},{28,12},{1,17},{... | collective-permute-start | bytes 1572872 | tf_op jit(solution)/shard_map/ppermute | solution.py:25
  85.6 2.2 %copy-start.1 = (bf16[2,1024,1024]{2,1,0:T(8,128)(2,1)S(1)}, bf16[2,1024,1024]{2,1,0:T(8,128)(2,1)}, u32[]{:S(2)}) copy-start(bf16[2,1024,1024]{2,1,0:T(8,128)(2,1)} %copy-done) | copy-start | bytes 12582916
  87.8 1.6 %copy-start.4 = (bf16[1024,1024]{1,0:T(8,128)(2,1)S(1)}, bf16[1024,1024]{1,0:T(8,128)(2,1)}, u32[]{:S(2)}) copy-start(bf16[1024,1024]{1,0:T(8,128)(2,1)} %copy-done.3) | copy-start | bytes 6291460
  90.7 10.8 %copy-start.7 = (bf16[2,1024,512]{2,1,0:T(8,128)(2,1)S(1)}, bf16[2,1024,512]{2,1,0:T(8,128)(2,1)}, u32[]{:S(2)}) copy-start(bf16[2,1024,512]{2,1,0:T(8,128)(2,1)} %get-tuple-element.59) | copy-start | bytes 6291460
  104.4 38.0 %copy-start.6 = (f32[512,1024]{1,0:T(8,128)S(1)}, f32[512,1024]{1,0:T(8,128)}, u32[]{:S(2)}) copy-start(f32[512,1024]{1,0:T(8,128)} %momentum.1) | copy-start | bytes 6291460
  126.2 1.1 collective-permute-start.23
  127.3 3.5 %collective-permute-start.24 = (f32[1,128]{1,0:T(1,128)S(1)}, f32[1,128]{1,0:T(1,128)S(1)}, u32[]{:S(2)}, u32[]{:S(2)}) collective-permute-start(f32[1,128]{1,0:T(1,128)S(1)} %add.108), channel_id=1, source_target_pairs={{0,4},{4,0},{8,12},{12,8},{16,20},{20,16},{24,28},{28,24},{1,5},{5... | collective-permute-start | bytes 1544 | tf_op jit(solution)/shard_map/ppermute | solution.py:25
  130.8 3.5 %collective-permute-start.25 = (f32[1,128]{1,0:T(1,128)S(1)}, f32[1,128]{1,0:T(1,128)S(1)}, u32[]{:S(2)}, u32[]{:S(2)}) collective-permute-start(f32[1,128]{1,0:T(1,128)S(1)} %add.109), channel_id=1, source_target_pairs={{0,8},{4,12},{8,0},{12,4},{16,24},{20,28},{24,16},{28,20},{1,9},{5... | collective-permute-start | bytes 1544 | tf_op jit(solution)/shard_map/ppermute | solution.py:25
  134.4 4.4 %collective-permute-start.26 = (f32[1,128]{1,0:T(1,128)S(1)}, f32[1,128]{1,0:T(1,128)S(1)}, u32[]{:S(2)}, u32[]{:S(2)}) collective-permute-start(f32[1,128]{1,0:T(1,128)S(1)} %add.110), channel_id=1, source_target_pairs={{0,16},{4,20},{8,24},{12,28},{16,0},{20,4},{24,8},{28,12},{1,17},{... | collective-permute-start | bytes 1544 | tf_op jit(solution)/shard_map/ppermute | solution.py:25
  138.8 3.5 %collective-permute-start.27 = (f32[1,128]{1,0:T(1,128)S(1)}, f32[1,128]{1,0:T(1,128)S(1)}, u32[]{:S(2)}, u32[]{:S(2)}) collective-permute-start(f32[1,128]{1,0:T(1,128)S(1)} %add.111), channel_id=1, source_target_pairs={{0,2},{1,3},{2,0},{3,1},{4,6},{5,7},{6,4},{7,5},{8,10},{9,11},{10,... | collective-permute-start | bytes 1544 | tf_op jit(solution)/shard_map/ppermute | solution.py:25

commit v6 on v5

--- a/solution.py
+++ b/solution.py
@@ -326,36 +326,48 @@
     return [factors[0] * first, factors[1] * first, factors[2] * second, factors[3] * second]
 
 
-def merge_kernel(scale, flip, per_block, width, at, idx, sums, own, grads, last, out):
+def merge_kernel(scale, flip, per_block, width, at, idx, sums, own, grads, last, out, tiles, sems):
     turn = idx[PLACE] * (QUAD + 1)
+    bit = 1 - idx[BIT] if flip else idx[BIT]
+    columns = out.shape[1]
+    steps = out.shape[0] // width
+    from_columns = pl.ds(at * columns, columns)
+    copies = []
+    for j in range(steps):
+        tile = (2 * (j // per_block) + bit) * per_block + j % per_block
+        there, here = pl.ds(pl.multiple_of(tile * width, width), width), pl.ds(j * width, width)
+        sources = (own, grads.at[0], grads.at[1], last)
+        for k, source in enumerate(sources):
+            copy = pltpu.make_async_copy(source.at[there, from_columns], tiles.at[k, here], sems.at[j, k])
+            copy.start()
+            copies.append(copy)
     factors = merge_factors(lambda a, b: sums[0, jnp.bitwise_xor(QUAD * a + b, turn)])
     factors = [factor * scale for factor in factors]
-    bit = 1 - idx[BIT] if flip else idx[BIT]
-    columns = out.shape[1]
-    for j in range(out.shape[0] // width):
-        tile = (2 * (j // per_block) + bit) * per_block + j % per_block
-
-        def strip(i, carry):
-            there, here = strip_at(tile * width + i * STRIP), strip_at(j * width + i * STRIP)
-            for lanes in lanes_of(columns):
-                from_lanes = slice(at * columns + lanes.start, at * columns + lanes.stop)
-                four = (own[there, from_lanes], grads[0, there, from_lanes])
-                four += (grads[1, there, from_lanes], last[there, from_lanes])
-                total = factors[0] * four[0].astype(jnp.float32)
-                for factor, value in zip(factors[1:], four[1:]):
-                    total = total + factor * value.astype(jnp.float32)
-                out[here, lanes] = total.astype(out.dtype)
-            return carry
-
-        lax.fori_loop(0, width // STRIP, strip, 0)
+    for copy in copies:
+        copy.wait()
+
+    def strip(i, carry):
+        rows = strip_at(i * STRIP)
+        for lanes in lanes_of(columns):
+            total = factors[0] * tiles[0, rows, lanes].astype(jnp.float32)
+            for k in range(1, QUAD):
+                total = total + factors[k] * tiles[k, rows, lanes].astype(jnp.float32)
+            out[rows, lanes] = total.astype(out.dtype)
+        return carry
+
+    lax.fori_loop(0, out.shape[0] // STRIP, strip, 0)
 
 
 def merge(idx, flip, sums, own, grads, last, scale, per_block, width, at, columns):
+    rows = own.shape[0] // 2
     return in_place(
         functools.partial(merge_kernel, scale, flip, per_block, width, at),
-        [(pltpu.SMEM, idx), (pltpu.SMEM, sums)] + [(pltpu.VMEM, v) for v in (own, grads, last)],
-        [jax.ShapeDtypeStruct((own.shape[0] // 2, columns), jnp.bfloat16)],
-        [],
+        [(pltpu.SMEM, idx), (pltpu.SMEM, sums)] + [(pltpu.HBM, in_hbm(v)) for v in (own, grads, last)],
+        [jax.ShapeDtypeStruct((rows, columns), jnp.bfloat16)],
+        [
+            pltpu.VMEM((QUAD, rows, columns), jnp.bfloat16),
+            pltpu.SemaphoreType.DMA((rows // width, QUAD)),
+        ],
         "merge",
     )[0]
 

time: 145 us -> 147 us (1.014)
  Pallas kernels: 44.1 us -> 48.4 us
  local copies, waits for them, and re-layouts: 8.16 us -> 5.7 us
    pallas_call x6, Pallas kernels: 18.7 us -> 22.9 us  [in_place(): pl.pallas_call(kernel, in_specs=[pl.BlockSpec(memory_space=m) for m, _ in...]
    unnamed x19 -> x17, local copies, waits for them, and re-layouts: 6.41 us -> 3.95 us
  transfers between devices with their start and end apart: 28 -> 28, of which waited for: 17 -> 17; matrix products, arithmetic and copies ran while one was open for 5% -> 4% of each run, Pallas kernels for 24% -> 26%
where the time goes in v6:
time: 147 us
  waiting for transfers between devices  56.3 us (38%)
  Pallas kernels  48.4 us (33%)
  starting transfers between devices  29.2 us (20%)
  other arithmetic  6.3 us (4%)
  local copies, waits for them, and re-layouts  5.7 us (4%)
    ppermute x28, waiting for transfers between devices, exchange(): return lax.ppermute(value, axis, pairs)  56.3 us
    ppermute x28, starting transfers between devices, exchange(): return lax.ppermute(value, axis, pairs)  29.2 us
    pallas_call x6, Pallas kernels, in_place(): pl.pallas_call(kernel, in_specs=[pl.BlockSpec(memory_space=m) for m, _ in...  22.9 us
    pallas_call x1, Pallas kernels, input_grad_part(): pl.pallas_call(input_grad_kernel, grid_spec=pltpu.PrefetchScalarGridSpec(...  8.9 us
    pallas_call x2, Pallas kernels, forward(): pl.pallas_call(forward_kernel, grid=(columns // tile,), in_specs=[pl.Bloc...  8.29 us
    pallas_call x1, Pallas kernels, own_gram(): pl.pallas_call(own_kernel, grid_spec=pltpu.PrefetchScalarGridSpec(num_sca...  4.67 us
    unnamed x17, local copies, waits for them, and re-layouts  3.95 us
  transfers between devices with their start and end apart: 28, of which 17 were waited for; matrix products, arithmetic and copies ran while one was open for 4% of the time, Pallas kernels for 26%

profile of v6, /device:TPU:0, one launch (start us, length us, event | category | flops | bytes accessed | tf_op | source)
XLA Modules:
  0.0 146.8 jit_solution(3654047090256642462)
XLA Ops:
  0.7 1.7 %constant_dynamic-slice_fusion = (bf16[512,256]{1,0:T(8,128)(2,1)S(1)}, bf16[512,256]{1,0:T(8,128)(2,1)S(1)}, bf16[512,256]{1,0:T(8,128)(2,1)S(1)}) fusion(bf16[512,4096]{1,0:T(8,128)(2,1)} %x.3, s32[]{:T(128)S(6)} %select_n.47, s32[]{:T(128)S(6)} %select_n.46, s32[]{:T(128)S(6)} %select_n.45), kind=kLoop, calls=%fused_computation.4 | loop fusion | bytes 1572876 | tf_op jit(solution)/shard_map/dynamic_slice | solution.py:465
  2.4 0.1 copy.10
  2.5 0.1 copy.11
  2.6 0.1 copy.12
  2.8 3.0 %collective-permute-start = (bf16[256,512]{1,0:T(8,128)(2,1)S(1)}, bf16[256,512]{1,0:T(8,128)(2,1)S(1)}, u32[]{:S(2)}, u32[]{:S(2)}) collective-permute-start(bf16[256,512]{1,0:T(8,128)(2,1)S(1)} %bitcast.16), channel_id=1, source_target_pairs={{0,4},{4,0},{8,12},{12,8},{16,20},{20,16},{24,28},{28,24},{1,5},{5... | collective-permute-start | bytes 786440 | tf_op jit(solution)/shard_map/ppermute | solution.py:25
  5.8 1.6 %collective-permute-start.1 = (bf16[256,512]{1,0:T(8,128)(2,1)S(1)}, bf16[256,512]{1,0:T(8,128)(2,1)S(1)}, u32[]{:S(2)}, u32[]{:S(2)}) collective-permute-start(bf16[256,512]{1,0:T(8,128)(2,1)S(1)} %bitcast.15), channel_id=1, source_target_pairs={{0,8},{4,12},{8,0},{12,4},{16,24},{20,28},{24,16},{28,20},{1,9},{5... | collective-permute-start | bytes 786440 | tf_op jit(solution)/shard_map/ppermute | solution.py:25
  7.4 2.2 %copy-done.2 = bf16[512,4096]{1,0:T(8,128)(2,1)S(1)} copy-done((bf16[512,4096]{1,0:T(8,128)(2,1)S(1)}, bf16[512,4096]{1,0:T(8,128)(2,1)}, u32[]{:S(2)}) %copy-start.2) | copy-done | bytes 4194328
  9.6 4.1 %forward.2.left = bf16[512,512]{1,0:T(8,128)(2,1)S(1)} custom-call(bf16[512,4096]{1,0:T(8,128)(2,1)S(1)} %copy-done.2, bf16[4096,1024]{1,0:T(8,128)(2,1)} %w_keep.1, bf16[512,1024]{1,0:T(8,128)(2,1)S(1)} %copy-done.4), custom_call_target="tpu_custom_call" | custom-call | flops 1 | bytes 1 | tf_op jit(solution)/shard_map/forward/pallas_call | solution.py:84
  13.8 1.3 collective-permute-done.1
  15.1 0.9 pad_maximum_fusion.refs_0_
  15.9 1.5 %collective-permute-start.4 = (bf16[2,256,512]{2,1,0:T(8,128)(2,1)}, bf16[2,256,512]{2,1,0:T(8,128)(2,1)}, u32[]{:S(2)}, u32[]{:S(2)}) collective-permute-start(bf16[2,256,512]{2,1,0:T(8,128)(2,1)} %pad_maximum_fusion.refs_0_), channel_id=1, source_target_pairs={{0,2},{1,3},{2,0},{3,1},{4,6},{5,7},{6,4},{7,5},{8,10},{9,11},{10,... | collective-permute-start | bytes 1572872 | tf_op jit(solution)/shard_map/ppermute | solution.py:25
  17.4 0.6 collective-permute-start.2
  18.0 1.6 %collective-permute-start.3 = (bf16[512,512]{1,0:T(8,128)(2,1)S(1)}, bf16[512,512]{1,0:T(8,128)(2,1)}, u32[]{:S(2)}, u32[]{:S(2)}) collective-permute-start(bf16[512,512]{1,0:T(8,128)(2,1)S(1)} %forward.2.left), channel_id=1, source_target_pairs={{0,8},{4,12},{8,0},{12,4},{16,24},{20,28},{24,16},{28,20},{1,9},{5... | collective-permute-start | bytes 1572872 | tf_op jit(solution)/shard_map/ppermute | solution.py:25
  19.6 4.1 %forward.3.right = bf16[512,512]{1,0:T(8,128)(2,1)S(1)} custom-call(bf16[512,4096]{1,0:T(8,128)(2,1)S(1)} %copy-done.2, bf16[4096,1024]{1,0:T(8,128)(2,1)} %w_keep.1, bf16[512,1024]{1,0:T(8,128)(2,1)S(1)} %copy-done.4), custom_call_target="tpu_custom_call" | custom-call | flops 1 | bytes 1 | tf_op jit(solution)/shard_map/forward/pallas_call | solution.py:84
  23.8 1.5 %collective-permute-start.6 = (bf16[512,512]{1,0:T(8,128)(2,1)S(1)}, bf16[512,512]{1,0:T(8,128)(2,1)}, u32[]{:S(2)}, u32[]{:S(2)}) collective-permute-start(bf16[512,512]{1,0:T(8,128)(2,1)S(1)} %forward.3.right), channel_id=1, source_target_pairs={{0,4},{4,0},{8,12},{12,8},{16,20},{20,16},{24,28},{28,24},{1,5},{5... | collective-permute-start | bytes 1572872 | tf_op jit(solution)/shard_map/ppermute | solution.py:25
  25.2 0.5 collective-permute-start.7
  25.7 0.1 stack.40.idx
  25.8 4.7 %own_gram.1 = (f32[1,128]{1,0:T(1,128)S(1)}, bf16[1024,1024]{1,0:T(8,128)(2,1)S(1)}) custom-call(s32[7]{0:T(128)S(1)} %stack.40.idx, bf16[512,4096]{1,0:T(8,128)(2,1)} %x.3, bf16[512,512]{1,0:T(8,128)(2,1)S(1)} %forward.2.left, bf16[512,512]{1,0:T(8,128)(2,1)S(1)} %forward.3.right), custom_call_target="tpu_custom_call" | custom-call | flops 1 | bytes 1 | tf_op jit(solution)/shard_map/own_gram/pallas_call | solution.py:192
  30.5 1.9 %collective-permute-done.2.y_left = bf16[512,512]{1,0:T(8,128)(2,1)} collective-permute-done((bf16[512,512]{1,0:T(8,128)(2,1)S(1)}, bf16[512,512]{1,0:T(8,128)(2,1)}, u32[]{:S(2)}, u32[]{:S(2)}) %collective-permute-start.2) | collective-permute-done | bytes 524320 | tf_op jit(solution)/shard_map/ppermute | solution.py:25
  32.4 0.6 collective-permute-done.3.z_left
  33.0 8.9 %input_grad_part.1 = (bf16[2,1024,512]{2,1,0:T(8,128)(2,1)}, bf16[2,1024,512]{2,1,0:T(8,128)(2,1)}) custom-call(s32[7]{0:T(128)S(1)} %stack.40.idx, bf16[4096,1024]{1,0:T(8,128)(2,1)} %w_keep.1, bf16[4096,1024]{1,0:T(8,128)(2,1)} %w_keep.1, bf16[512,512]{1,0:T(8,128)(2,1)S(1)} %forward.2.left, bf16[512,512]{1,0:T(8,128)(2,1)S(1)} %forward.3.right), custom_call_target="tpu_custom_call" | custom-call | flops 1 | bytes 1 | tf_op jit(solution)/shard_map/input_grad_part/pallas_call | solution.py:127
  41.9 0.1 collective-permute-start.8
  42.0 0.5 collective-permute-start.10
  42.5 0.1 collective-permute-start.11
  42.6 1.2 collective-permute-start.9
  43.8 1.5 collective-permute-start.12
  45.2 1.2 collective-permute-done.8
  46.5 1.6 %collective-permute-start.13 = (bf16[512,512]{1,0:T(8,128)(2,1)}, bf16[512,512]{1,0:T(8,128)(2,1)S(1)}, u32[]{:S(2)}, u32[]{:S(2)}) collective-permute-start(bf16[512,512]{1,0:T(8,128)(2,1)} %collective-permute-done.6.y_right), channel_id=1, source_target_pairs={{0,8},{4,12},{8,0},{12,4},{16,24},{20,28},{24,16},{28,20},{1,9},{5... | collective-permute-start | bytes 1572872 | tf_op jit(solution)/shard_map/ppermute | solution.py:25
  48.1 2.8 %add_convert_fusion.1 = bf16[1,1024,512]{2,1,0:T(8,128)(2,1)} fusion(bf16[2,1024,512]{2,1,0:T(8,128)(2,1)} %collective-permute-done.8, s32[]{:T(128)S(6)} %select_n.50, bf16[2,1024,512]{2,1,0:T(8,128)(2,1)} %get-tuple-element.59), kind=kLoop, calls=%fused_computation.1 | loop fusion | flops 2097152 | bytes 3145732 | tf_op jit(solution)/shard_map/convert_element_type | solution.py:509
  50.9 7.2 %near_gram.1 = (f32[1,128]{1,0:T(1,128)S(1)}, bf16[2,1024,1024]{2,1,0:T(8,128)(2,1)S(1)}) custom-call(s32[7]{0:T(128)S(1)} %stack.40.idx, f32[1,128]{1,0:T(1,128)S(1)} %get-tuple-element.64.before, bf16[1024,1024]{1,0:T(8,128)(2,1)S(1)} %get-tuple-element.65.own, bf16[512,512]{1,0:T(8,128)(2,1)} %collective-permute-done.2.y_left, ...), custom_call_target="tpu_custom_call" | custom-call | flops 1 | bytes 1 | tf_op jit(solution)/shard_map/near_gram/pallas_call | solution.py:265
  58.1 0.5 collective-permute-start.15
  58.6 2.0 %collective-permute-done.13.right = bf16[512,512]{1,0:T(8,128)(2,1)S(1)} collective-permute-done((bf16[512,512]{1,0:T(8,128)(2,1)}, bf16[512,512]{1,0:T(8,128)(2,1)S(1)}, u32[]{:S(2)}, u32[]{:S(2)}) %collective-permute-start.13) | collective-permute-done | bytes 524320 | tf_op jit(solution)/shard_map/ppermute | solution.py:25
  60.7 4.7 %far_gram.1 = (f32[1,128]{1,0:T(1,128)S(1)}, bf16[1024,1024]{1,0:T(8,128)(2,1)S(1)}) custom-call(s32[7]{0:T(128)S(1)} %stack.40.idx, f32[1,128]{1,0:T(1,128)S(1)} %get-tuple-element.73.before, bf16[512,512]{1,0:T(8,128)(2,1)S(1)} %collective-permute-done.12.left, bf16[512,512]{1,0:T(8,128)(2,1)S(1)} %collective-permute-done.13.right, ...), custom_call_target="tpu_custom_call" | custom-call | flops 1 | bytes 1 | tf_op jit(solution)/shard_map/far_gram/pallas_call | solution.py:265
  65.4 1.3 copy-done.3
  66.7 1.1 collective-permute-done.16
  67.9 1.4 collective-permute-start.17
  69.3 2.1 %collective-permute-done.17 = f32[1,128]{1,0:T(1,128)S(1)} collective-permute-done((f32[1,128]{1,0:T(1,128)S(1)}, f32[1,128]{1,0:T(1,128)S(1)}, u32[]{:S(2)}, u32[]{:S(2)}) %collective-permute-start.17) | collective-permute-done | bytes 544 | tf_op jit(solution)/shard_map/ppermute | solution.py:25
  71.4 1.6 %collective-permute-start.18 = (f32[1,128]{1,0:T(1,128)S(1)}, f32[1,128]{1,0:T(1,128)S(1)}, u32[]{:S(2)}, u32[]{:S(2)}) collective-permute-start(f32[1,128]{1,0:T(1,128)S(1)} %add.104), channel_id=1, source_target_pairs={{0,8},{4,12},{8,0},{12,4},{16,24},{20,28},{24,16},{28,20},{1,9},{5... | collective-permute-start | bytes 1544 | tf_op jit(solution)/shard_map/ppermute | solution.py:25
  73.0 2.0 %collective-permute-done.18 = f32[1,128]{1,0:T(1,128)S(1)} collective-permute-done((f32[1,128]{1,0:T(1,128)S(1)}, f32[1,128]{1,0:T(1,128)S(1)}, u32[]{:S(2)}, u32[]{:S(2)}) %collective-permute-start.18) | collective-permute-done | bytes 544 | tf_op jit(solution)/shard_map/ppermute | solution.py:25
  75.0 1.3 collective-permute-start.19
  76.2 2.3 %collective-permute-done.19 = f32[1,128]{1,0:T(1,128)S(1)} collective-permute-done((f32[1,128]{1,0:T(1,128)S(1)}, f32[1,128]{1,0:T(1,128)S(1)}, u32[]{:S(2)}, u32[]{:S(2)}) %collective-permute-start.19) | collective-permute-done | bytes 544 | tf_op jit(solution)/shard_map/ppermute | solution.py:25
  78.5 2.7 %merge.4 = bf16[512,512]{1,0:T(8,128)(2,1)S(1)} custom-call(s32[7]{0:T(128)S(1)} %stack.40.idx, f32[1,128]{1,0:T(1,128)S(1)} %add.106.sums, bf16[1024,1024]{1,0:T(8,128)(2,1)} %copy-done.1, bf16[2,1024,1024]{2,1,0:T(8,128)(2,1)} %copy-done, bf16[1024,1024]{1,0:T(8,128)(2,1)} %copy-done.3), custom_call_target="tpu_custom_call" | custom-call | flops 1 | bytes 1 | tf_op jit(solution)/shard_map/merge/pallas_call | solution.py:265
  81.2 1.3 collective-permute-start.20
  82.6 2.6 %collective-permute-start.21 = (bf16[512,512]{1,0:T(8,128)(2,1)S(1)}, bf16[512,512]{1,0:T(8,128)(2,1)S(1)}, u32[]{:S(2)}, u32[]{:S(2)}) collective-permute-start(bf16[512,512]{1,0:T(8,128)(2,1)S(1)} %merge.4), channel_id=1, source_target_pairs={{0,16},{4,20},{8,24},{12,28},{16,0},{20,4},{24,8},{28,12},{1,17},{... | collective-permute-start | bytes 1572872 | tf_op jit(solution)/shard_map/ppermute | solution.py:25
  85.2 2.7 %merge.5 = bf16[512,512]{1,0:T(8,128)(2,1)S(1)} custom-call(s32[7]{0:T(128)S(1)} %stack.40.idx, f32[1,128]{1,0:T(1,128)S(1)} %add.106.sums, bf16[1024,1024]{1,0:T(8,128)(2,1)} %copy-done.1, bf16[2,1024,1024]{2,1,0:T(8,128)(2,1)} %copy-done, bf16[1024,1024]{1,0:T(8,128)(2,1)} %copy-done.3), custom_call_target="tpu_custom_call" | custom-call | flops 1 | bytes 1 | tf_op jit(solution)/shard_map/merge/pallas_call | solution.py:265
  87.9 0.4 collective-permute-start.22
  88.3 2.7 %merge.7.kept.kept_1 = bf16[512,512]{1,0:T(8,128)(2,1)S(1)} custom-call(s32[7]{0:T(128)S(1)} %stack.40.idx, f32[1,128]{1,0:T(1,128)S(1)} %add.106.sums, bf16[1024,1024]{1,0:T(8,128)(2,1)} %copy-done.1, bf16[2,1024,1024]{2,1,0:T(8,128)(2,1)} %copy-done, bf16[1024,1024]{1,0:T(8,128)(2,1)} %copy-done.3), custom_call_target="tpu_custom_call" | custom-call | flops 1 | bytes 1 | tf_op jit(solution)/shard_map/merge/pallas_call | solution.py:265
  91.1 2.8 %merge.6.kept.kept_0 = bf16[512,512]{1,0:T(8,128)(2,1)S(1)} custom-call(s32[7]{0:T(128)S(1)} %stack.40.idx, f32[1,128]{1,0:T(1,128)S(1)} %add.106.sums, bf16[1024,1024]{1,0:T(8,128)(2,1)} %copy-done.1, bf16[2,1024,1024]{2,1,0:T(8,128)(2,1)} %copy-done, bf16[1024,1024]{1,0:T(8,128)(2,1)} %copy-done.3), custom_call_target="tpu_custom_call" | custom-call | flops 1 | bytes 1 | tf_op jit(solution)/shard_map/merge/pallas_call | solution.py:265
  93.9 9.4 %collective-permute-done.20 = bf16[1,1024,512]{2,1,0:T(8,128)(2,1)S(1)} collective-permute-done((bf16[1,1024,512]{2,1,0:T(8,128)(2,1)}, bf16[1,1024,512]{2,1,0:T(8,128)(2,1)S(1)}, u32[]{:S(2)}, u32[]{:S(2)}) %collective-permute-start.20) | collective-permute-done | bytes 1048608 | tf_op jit(solution)/shard_map/ppermute | solution.py:25
  103.3 2.6 %fusion = bf16[1024,512]{1,0:T(8,128)(2,1)} fusion(bf16[1,1024,512]{2,1,0:T(8,128)(2,1)S(1)} %collective-permute-done.20, bf16[2,1024,512]{2,1,0:T(8,128)(2,1)} %collective-permute-done.8, s32[]{:T(128)S(6)} %select_n.49, bf16[2,1024,512]{2,1,0:T(8,128)(2,1)S(1)} %copy-done.6), kind=kLoop, calls=%fused_computation.2 | loop fusion | flops 3145728 | bytes 4194308 | tf_op jit(solution)/shard_map/squeeze | solution.py:539
  106.0 11.5 %collective-permute-done.21.received.received_0 = bf16[512,512]{1,0:T(8,128)(2,1)S(1)} collective-permute-done((bf16[512,512]{1,0:T(8,128)(2,1)S(1)}, bf16[512,512]{1,0:T(8,128)(2,1)S(1)}, u32[]{:S(2)}, u32[]{:S(2)}) %collective-permute-start.21) | collective-permute-done | bytes 524320 | tf_op jit(solution)/shard_map/ppermute | solution.py:25
  117.5 0.5 partial_sums.2.before
  118.0 9.5 %collective-permute-done.22.received.received_1 = bf16[512,512]{1,0:T(8,128)(2,1)S(1)} collective-permute-done((bf16[512,512]{1,0:T(8,128)(2,1)S(1)}, bf16[512,512]{1,0:T(8,128)(2,1)S(1)}, u32[]{:S(2)}, u32[]{:S(2)}) %collective-permute-start.22) | collective-permute-done | bytes 524320 | tf_op jit(solution)/shard_map/ppermute | solution.py:25
  127.5 0.5 partial_sums.3
  128.0 1.1 collective-permute-done.23
  129.1 1.5 collective-permute-start.24
  130.6 2.1 %collective-permute-done.24 = f32[1,128]{1,0:T(1,128)S(1)} collective-permute-done((f32[1,128]{1,0:T(1,128)S(1)}, f32[1,128]{1,0:T(1,128)S(1)}, u32[]{:S(2)}, u32[]{:S(2)}) %collective-permute-start.24) | collective-permute-done | bytes 544 | tf_op jit(solution)/shard_map/ppermute | solution.py:25
  132.7 0.7 collective-permute-start.25
  133.3 2.9 %collective-permute-done.25 = f32[1,128]{1,0:T(1,128)S(1)} collective-permute-done((f32[1,128]{1,0:T(1,128)S(1)}, f32[1,128]{1,0:T(1,128)S(1)}, u32[]{:S(2)}, u32[]{:S(2)}) %collective-permute-start.25) | collective-permute-done | bytes 544 | tf_op jit(solution)/shard_map/ppermute | solution.py:25
  136.2 2.0 %collective-permute-start.26 = (f32[1,128]{1,0:T(1,128)S(1)}, f32[1,128]{1,0:T(1,128)S(1)}, u32[]{:S(2)}, u32[]{:S(2)}) collective-permute-start(f32[1,128]{1,0:T(1,128)S(1)} %add.110), channel_id=1, source_target_pairs={{0,16},{4,20},{8,24},{12,28},{16,0},{20,4},{24,8},{28,12},{1,17},{... | collective-permute-start | bytes 1544 | tf_op jit(solution)/shard_map/ppermute | solution.py:25
  138.2 2.4 %collective-permute-done.26 = f32[1,128]{1,0:T(1,128)S(1)} collective-permute-done((f32[1,128]{1,0:T(1,128)S(1)}, f32[1,128]{1,0:T(1,128)S(1)}, u32[]{:S(2)}, u32[]{:S(2)}) %collective-permute-start.26) | collective-permute-done | bytes 544 | tf_op jit(solution)/shard_map/ppermute | solution.py:25
  140.6 0.8 collective-permute-start.27
  141.4 2.8 %collective-permute-done.27 = f32[1,128]{1,0:T(1,128)S(1)} collective-permute-done((f32[1,128]{1,0:T(1,128)S(1)}, f32[1,128]{1,0:T(1,128)S(1)}, u32[]{:S(2)}, u32[]{:S(2)}) %collective-permute-start.27) | collective-permute-done | bytes 544 | tf_op jit(solution)/shard_map/ppermute | solution.py:25
  144.2 2.6 %update.1 = (f32[512,1024]{1,0:T(8,128)}, f32[2]{0:T(128)}) custom-call(s32[1]{0:T(128)} %bitcast.1.first_at.bit, f32[1,128]{1,0:T(1,128)S(1)} %add.112.sums, f32[512,1024]{1,0:T(8,128)S(1)} %copy-done.5, bf16[512,512]{1,0:T(8,128)(2,1)S(1)} %merge.6.kept.kept_0, bf16[512,512]{1,0:T(8,128)(2,1)S(1)} %merge.7.kept.kept_1, ...), custom_call_target="tpu_custom_call" | custom-call | flops 1 | bytes 1 | tf_op jit(solution)/shard_map/update/pallas_call | solution.py:436
  (37 shorter events, 0.2 us)
Async XLA Ops:
  0.6 6.8 %copy-start.4 = (bf16[512,1024]{1,0:T(8,128)(2,1)S(1)}, bf16[512,1024]{1,0:T(8,128)(2,1)}, u32[]{:S(2)}) copy-start(bf16[512,1024]{1,0:T(8,128)(2,1)} %targets.3) | copy-start | bytes 3145732
  2.8 11.0 %collective-permute-start = (bf16[256,512]{1,0:T(8,128)(2,1)S(1)}, bf16[256,512]{1,0:T(8,128)(2,1)S(1)}, u32[]{:S(2)}, u32[]{:S(2)}) collective-permute-start(bf16[256,512]{1,0:T(8,128)(2,1)S(1)} %bitcast.16), channel_id=1, source_target_pairs={{0,4},{4,0},{8,12},{12,8},{16,20},{20,16},{24,28},{28,24},{1,5},{5... | collective-permute-start | bytes 786440 | tf_op jit(solution)/shard_map/ppermute | solution.py:25
  5.8 9.2 %collective-permute-start.1 = (bf16[256,512]{1,0:T(8,128)(2,1)S(1)}, bf16[256,512]{1,0:T(8,128)(2,1)S(1)}, u32[]{:S(2)}, u32[]{:S(2)}) collective-permute-start(bf16[256,512]{1,0:T(8,128)(2,1)S(1)} %bitcast.15), channel_id=1, source_target_pairs={{0,8},{4,12},{8,0},{12,4},{16,24},{20,28},{24,16},{28,20},{1,9},{5... | collective-permute-start | bytes 786440 | tf_op jit(solution)/shard_map/ppermute | solution.py:25
  7.4 17.8 %collective-permute-start.5 = (bf16[256,512]{1,0:T(8,128)(2,1)S(1)}, bf16[256,512]{1,0:T(8,128)(2,1)S(1)}, u32[]{:S(2)}, u32[]{:S(2)}) collective-permute-start(bf16[256,512]{1,0:T(8,128)(2,1)S(1)} %bitcast.14), channel_id=1, source_target_pairs={{0,12},{4,8},{8,4},{12,0},{16,28},{20,24},{24,20},{28,16},{1,13},{... | collective-permute-start | bytes 786440 | tf_op jit(solution)/shard_map/ppermute | solution.py:25
  7.4 2.2 %copy-start.2 = (bf16[512,4096]{1,0:T(8,128)(2,1)S(1)}, bf16[512,4096]{1,0:T(8,128)(2,1)}, u32[]{:S(2)}) copy-start(bf16[512,4096]{1,0:T(8,128)(2,1)} %x.3) | copy-start | bytes 12582916
  15.9 14.5 %collective-permute-start.4 = (bf16[2,256,512]{2,1,0:T(8,128)(2,1)}, bf16[2,256,512]{2,1,0:T(8,128)(2,1)}, u32[]{:S(2)}, u32[]{:S(2)}) collective-permute-start(bf16[2,256,512]{2,1,0:T(8,128)(2,1)} %pad_maximum_fusion.refs_0_), channel_id=1, source_target_pairs={{0,2},{1,3},{2,0},{3,1},{4,6},{5,7},{6,4},{7,5},{8,10},{9,11},{10,... | collective-permute-start | bytes 1572872 | tf_op jit(solution)/shard_map/ppermute | solution.py:25
  17.4 15.0 %collective-permute-start.2 = (bf16[512,512]{1,0:T(8,128)(2,1)S(1)}, bf16[512,512]{1,0:T(8,128)(2,1)}, u32[]{:S(2)}, u32[]{:S(2)}) collective-permute-start(bf16[512,512]{1,0:T(8,128)(2,1)S(1)} %forward.2.left), channel_id=1, source_target_pairs={{0,4},{4,0},{8,12},{12,8},{16,20},{20,16},{24,28},{28,24},{1,5},{5... | collective-permute-start | bytes 1572872 | tf_op jit(solution)/shard_map/ppermute | solution.py:25
  18.0 15.0 %collective-permute-start.3 = (bf16[512,512]{1,0:T(8,128)(2,1)S(1)}, bf16[512,512]{1,0:T(8,128)(2,1)}, u32[]{:S(2)}, u32[]{:S(2)}) collective-permute-start(bf16[512,512]{1,0:T(8,128)(2,1)S(1)} %forward.2.left), channel_id=1, source_target_pairs={{0,8},{4,12},{8,0},{12,4},{16,24},{20,28},{24,16},{28,20},{1,9},{5... | collective-permute-start | bytes 1572872 | tf_op jit(solution)/shard_map/ppermute | solution.py:25
  23.8 18.1 %collective-permute-start.6 = (bf16[512,512]{1,0:T(8,128)(2,1)S(1)}, bf16[512,512]{1,0:T(8,128)(2,1)}, u32[]{:S(2)}, u32[]{:S(2)}) collective-permute-start(bf16[512,512]{1,0:T(8,128)(2,1)S(1)} %forward.3.right), channel_id=1, source_target_pairs={{0,4},{4,0},{8,12},{12,8},{16,20},{20,16},{24,28},{28,24},{1,5},{5... | collective-permute-start | bytes 1572872 | tf_op jit(solution)/shard_map/ppermute | solution.py:25
  25.2 16.7 %collective-permute-start.7 = (bf16[512,512]{1,0:T(8,128)(2,1)S(1)}, bf16[512,512]{1,0:T(8,128)(2,1)}, u32[]{:S(2)}, u32[]{:S(2)}) collective-permute-start(bf16[512,512]{1,0:T(8,128)(2,1)S(1)} %forward.3.right), channel_id=1, source_target_pairs={{0,8},{4,12},{8,0},{12,4},{16,24},{20,28},{24,16},{28,20},{1,9},{5... | collective-permute-start | bytes 1572872 | tf_op jit(solution)/shard_map/ppermute | solution.py:25
  30.5 30.2 %copy-start.1 = (bf16[1024,1024]{1,0:T(8,128)(2,1)}, bf16[1024,1024]{1,0:T(8,128)(2,1)S(1)}, u32[]{:S(2)}) copy-start(bf16[1024,1024]{1,0:T(8,128)(2,1)S(1)} %get-tuple-element.65.own) | copy-start | bytes 6291460
  41.9 4.6 %collective-permute-start.8 = (bf16[2,1024,512]{2,1,0:T(8,128)(2,1)}, bf16[2,1024,512]{2,1,0:T(8,128)(2,1)}, u32[]{:S(2)}, u32[]{:S(2)}) collective-permute-start(bf16[2,1024,512]{2,1,0:T(8,128)(2,1)} %get-tuple-element.60), channel_id=1, source_target_pairs={{0,1},{1,0},{2,3},{3,2},{4,5},{5,4},{6,7},{7,6},{8,9},{9,8},{10,11... | collective-permute-start | bytes 6291464 | tf_op jit(solution)/shard_map/ppermute | solution.py:25
  42.0 8.9 %collective-permute-start.10 = (bf16[2,256,512]{2,1,0:T(8,128)(2,1)}, bf16[2,256,512]{2,1,0:T(8,128)(2,1)}, u32[]{:S(2)}, u32[]{:S(2)}) collective-permute-start(bf16[2,256,512]{2,1,0:T(8,128)(2,1)} %pad_maximum_fusion.refs_0_), channel_id=1, source_target_pairs={{0,1},{1,0},{2,3},{3,2},{4,5},{5,4},{6,7},{7,6},{8,9},{9,8},{10,11... | collective-permute-start | bytes 1572872 | tf_op jit(solution)/shard_map/ppermute | solution.py:25
  42.5 8.4 %collective-permute-start.11 = (bf16[2,256,512]{2,1,0:T(8,128)(2,1)}, bf16[2,256,512]{2,1,0:T(8,128)(2,1)}, u32[]{:S(2)}, u32[]{:S(2)}) collective-permute-start(bf16[2,256,512]{2,1,0:T(8,128)(2,1)} %collective-permute-done.4.refs_1_), channel_id=1, source_target_pairs={{0,1},{1,0},{2,3},{3,2},{4,5},{5,4},{6,7},{7,6},{8,9},{9,8},{10,11... | collective-permute-start | bytes 1572872 | tf_op jit(solution)/shard_map/ppermute | solution.py:25
  42.6 15.5 %collective-permute-start.9 = (bf16[256,512]{1,0:T(8,128)(2,1)S(1)}, bf16[256,512]{1,0:T(8,128)(2,1)}, u32[]{:S(2)}, u32[]{:S(2)}) collective-permute-start(bf16[256,512]{1,0:T(8,128)(2,1)S(1)} %collective-permute-done.5.refs_0_), channel_id=1, source_target_pairs={{0,2},{1,3},{2,0},{3,1},{4,6},{5,7},{6,4},{7,5},{8,10},{9,11},{10,... | collective-permute-start | bytes 786440 | tf_op jit(solution)/shard_map/ppermute | solution.py:25
  43.8 14.9 %collective-permute-start.12 = (bf16[512,512]{1,0:T(8,128)(2,1)}, bf16[512,512]{1,0:T(8,128)(2,1)S(1)}, u32[]{:S(2)}, u32[]{:S(2)}) collective-permute-start(bf16[512,512]{1,0:T(8,128)(2,1)} %collective-permute-done.3.z_left), channel_id=1, source_target_pairs={{0,4},{4,0},{8,12},{12,8},{16,20},{20,16},{24,28},{28,24},{1,5},{5... | collective-permute-start | bytes 1572872 | tf_op jit(solution)/shard_map/ppermute | solution.py:25
  46.5 14.2 %collective-permute-start.13 = (bf16[512,512]{1,0:T(8,128)(2,1)}, bf16[512,512]{1,0:T(8,128)(2,1)S(1)}, u32[]{:S(2)}, u32[]{:S(2)}) collective-permute-start(bf16[512,512]{1,0:T(8,128)(2,1)} %collective-permute-done.6.y_right), channel_id=1, source_target_pairs={{0,8},{4,12},{8,0},{12,4},{16,24},{20,28},{24,16},{28,20},{1,9},{5... | collective-permute-start | bytes 1572872 | tf_op jit(solution)/shard_map/ppermute | solution.py:25
  58.0 7.4 %copy-start = (bf16[2,1024,1024]{2,1,0:T(8,128)(2,1)}, bf16[2,1024,1024]{2,1,0:T(8,128)(2,1)S(1)}, u32[]{:S(2)}) copy-start(bf16[2,1024,1024]{2,1,0:T(8,128)(2,1)S(1)} %get-tuple-element.74.grads) | copy-start | bytes 12582916
  58.0 2.6 %collective-permute-start.14 = (bf16[256,512]{1,0:T(8,128)(2,1)S(1)}, bf16[256,512]{1,0:T(8,128)(2,1)S(1)}, u32[]{:S(2)}, u32[]{:S(2)}) collective-permute-start(bf16[256,512]{1,0:T(8,128)(2,1)S(1)} %collective-permute-done.5.refs_0_), channel_id=1, source_target_pairs={{0,1},{1,0},{2,3},{3,2},{4,5},{5,4},{6,7},{7,6},{8,9},{9,8},{10,11... | collective-permute-start | bytes 786440 | tf_op jit(solution)/shard_map/ppermute | solution.py:25
  58.1 2.5 %collective-permute-start.15 = (bf16[256,512]{1,0:T(8,128)(2,1)}, bf16[256,512]{1,0:T(8,128)(2,1)S(1)}, u32[]{:S(2)}, u32[]{:S(2)}) collective-permute-start(bf16[256,512]{1,0:T(8,128)(2,1)} %collective-permute-done.9.refs_1_), channel_id=1, source_target_pairs={{0,1},{1,0},{2,3},{3,2},{4,5},{5,4},{6,7},{7,6},{8,9},{9,8},{10,11... | collective-permute-start | bytes 786440 | tf_op jit(solution)/shard_map/ppermute | solution.py:25
  65.4 1.3 copy-start.3
  66.7 1.1 collective-permute-start.16
  67.9 3.5 %collective-permute-start.17 = (f32[1,128]{1,0:T(1,128)S(1)}, f32[1,128]{1,0:T(1,128)S(1)}, u32[]{:S(2)}, u32[]{:S(2)}) collective-permute-start(f32[1,128]{1,0:T(1,128)S(1)} %add.103), channel_id=1, source_target_pairs={{0,4},{4,0},{8,12},{12,8},{16,20},{20,16},{24,28},{28,24},{1,5},{5... | collective-permute-start | bytes 1544 | tf_op jit(solution)/shard_map/ppermute | solution.py:25
  71.4 3.5 %collective-permute-start.18 = (f32[1,128]{1,0:T(1,128)S(1)}, f32[1,128]{1,0:T(1,128)S(1)}, u32[]{:S(2)}, u32[]{:S(2)}) collective-permute-start(f32[1,128]{1,0:T(1,128)S(1)} %add.104), channel_id=1, source_target_pairs={{0,8},{4,12},{8,0},{12,4},{16,24},{20,28},{24,16},{28,20},{1,9},{5... | collective-permute-start | bytes 1544 | tf_op jit(solution)/shard_map/ppermute | solution.py:25
  75.0 3.5 %collective-permute-start.19 = (f32[1,128]{1,0:T(1,128)S(1)}, f32[1,128]{1,0:T(1,128)S(1)}, u32[]{:S(2)}, u32[]{:S(2)}) collective-permute-start(f32[1,128]{1,0:T(1,128)S(1)} %add.105), channel_id=1, source_target_pairs={{0,2},{1,3},{2,0},{3,1},{4,6},{5,7},{6,4},{7,5},{8,10},{9,11},{10,... | collective-permute-start | bytes 1544 | tf_op jit(solution)/shard_map/ppermute | solution.py:25
  81.2 22.1 %collective-permute-start.20 = (bf16[1,1024,512]{2,1,0:T(8,128)(2,1)}, bf16[1,1024,512]{2,1,0:T(8,128)(2,1)S(1)}, u32[]{:S(2)}, u32[]{:S(2)}) collective-permute-start(bf16[1,1024,512]{2,1,0:T(8,128)(2,1)} %add_convert_fusion.1), channel_id=1, source_target_pairs={{0,2},{1,3},{2,0},{3,1},{4,6},{5,7},{6,4},{7,5},{8,10},{9,11},{10,... | collective-permute-start | bytes 3145736 | tf_op jit(solution)/shard_map/ppermute | solution.py:25
  82.6 34.9 %collective-permute-start.21 = (bf16[512,512]{1,0:T(8,128)(2,1)S(1)}, bf16[512,512]{1,0:T(8,128)(2,1)S(1)}, u32[]{:S(2)}, u32[]{:S(2)}) collective-permute-start(bf16[512,512]{1,0:T(8,128)(2,1)S(1)} %merge.4), channel_id=1, source_target_pairs={{0,16},{4,20},{8,24},{12,28},{16,0},{20,4},{24,8},{28,12},{1,17},{... | collective-permute-start | bytes 1572872 | tf_op jit(solution)/shard_map/ppermute | solution.py:25
  87.9 39.6 %collective-permute-start.22 = (bf16[512,512]{1,0:T(8,128)(2,1)S(1)}, bf16[512,512]{1,0:T(8,128)(2,1)S(1)}, u32[]{:S(2)}, u32[]{:S(2)}) collective-permute-start(bf16[512,512]{1,0:T(8,128)(2,1)S(1)} %merge.5), channel_id=1, source_target_pairs={{0,16},{4,20},{8,24},{12,28},{16,0},{20,4},{24,8},{28,12},{1,17},{... | collective-permute-start | bytes 1572872 | tf_op jit(solution)/shard_map/ppermute | solution.py:25
  91.1 12.3 %copy-start.6 = (bf16[2,1024,512]{2,1,0:T(8,128)(2,1)S(1)}, bf16[2,1024,512]{2,1,0:T(8,128)(2,1)}, u32[]{:S(2)}) copy-start(bf16[2,1024,512]{2,1,0:T(8,128)(2,1)} %get-tuple-element.59) | copy-start | bytes 6291460
  106.0 38.2 %copy-start.5 = (f32[512,1024]{1,0:T(8,128)S(1)}, f32[512,1024]{1,0:T(8,128)}, u32[]{:S(2)}) copy-start(f32[512,1024]{1,0:T(8,128)} %momentum.1) | copy-start | bytes 6291460
  128.0 1.1 collective-permute-start.23
  129.1 3.5 %collective-permute-start.24 = (f32[1,128]{1,0:T(1,128)S(1)}, f32[1,128]{1,0:T(1,128)S(1)}, u32[]{:S(2)}, u32[]{:S(2)}) collective-permute-start(f32[1,128]{1,0:T(1,128)S(1)} %add.108), channel_id=1, source_target_pairs={{0,4},{4,0},{8,12},{12,8},{16,20},{20,16},{24,28},{28,24},{1,5},{5... | collective-permute-start | bytes 1544 | tf_op jit(solution)/shard_map/ppermute | solution.py:25
  132.7 3.5 %collective-permute-start.25 = (f32[1,128]{1,0:T(1,128)S(1)}, f32[1,128]{1,0:T(1,128)S(1)}, u32[]{:S(2)}, u32[]{:S(2)}) collective-permute-start(f32[1,128]{1,0:T(1,128)S(1)} %add.109), channel_id=1, source_target_pairs={{0,8},{4,12},{8,0},{12,4},{16,24},{20,28},{24,16},{28,20},{1,9},{5... | collective-permute-start | bytes 1544 | tf_op jit(solution)/shard_map/ppermute | solution.py:25
  136.2 4.4 %collective-permute-start.26 = (f32[1,128]{1,0:T(1,128)S(1)}, f32[1,128]{1,0:T(1,128)S(1)}, u32[]{:S(2)}, u32[]{:S(2)}) collective-permute-start(f32[1,128]{1,0:T(1,128)S(1)} %add.110), channel_id=1, source_target_pairs={{0,16},{4,20},{8,24},{12,28},{16,0},{20,4},{24,8},{28,12},{1,17},{... | collective-permute-start | bytes 1544 | tf_op jit(solution)/shard_map/ppermute | solution.py:25
  140.6 3.5 %collective-permute-start.27 = (f32[1,128]{1,0:T(1,128)S(1)}, f32[1,128]{1,0:T(1,128)S(1)}, u32[]{:S(2)}, u32[]{:S(2)}) collective-permute-start(f32[1,128]{1,0:T(1,128)S(1)} %add.111), channel_id=1, source_target_pairs={{0,2},{1,3},{2,0},{3,1},{4,6},{5,7},{6,4},{7,5},{8,10},{9,11},{10,... | collective-permute-start | bytes 1544 | tf_op jit(solution)/shard_map/ppermute | solution.py:25
